TPU v7x, 128 devices: a whole 4x4x4 slice. The times are simulated.
128 devices in a mesh: lon: 8 (over y, x_hi), lat: 16 (over x_lo, z, core).
Axes of the slice: x: 4 (x_hi: 2, x_lo: 2; x = x_hi * 2 + x_lo), y: 4, z: 4, core: 2. Of those that a mesh axis runs over, the one named last changes fastest.
Arguments:
- field: float32 [80, 4096, 2048], P(None, 'lon', 'lat'), may hold values from -6 to 6
- lon_test: float32 [4096, 200], P('lon'), may hold values from -0.09375 to 0.09375
- lat_test: float32 [2048, 200], P('lat'), may hold values from -0.125 to 0.125
- time_test: float32 [80, 200], replicated, may hold values from -0.625 to 0.625
- lon_core: float32 [96, 4096], P(None, 'lon'), may hold values from -0.09375 to 0.09375
- lat_core: float32 [96, 2048], P(None, 'lat'), may hold values from -0.125 to 0.125
- time_core: float32 [96, 80], replicated, may hold values from -0.625 to 0.625
Outputs:
- sketch_lon: float32 [4096, 200], P(('lon', 'lat'))
- sketch_lat: float32 [2048, 200], P('lat')
- sketch_time: float32 [80, 200], replicated
- core_sketch: float32 [96, 96, 96], P(None, 'lon', 'lat')
All inputs are finite; a program needn't handle non-finite values.
Results may differ from a plain program's by a relative error of at most 0.000096.
Values sent between devices are 32-bit elements; how exact they have to be, the bound alone decides.
No kernel may reach another device: no remote copies, remote signals or barrier semaphores. Data moves between devices by JAX's collectives and lax.ppermute only.
A program may use at most 128 MiB of HBM per device.

v0:
```python
import jax
import jax.numpy as jnp
from jax import lax
from jax.sharding import PartitionSpec as P


def sum_core(partial_value):
    first = lax.psum_scatter(partial_value, "lon", scatter_dimension=1, tiled=True)
    return lax.psum_scatter(first, "lat", scatter_dimension=2, tiled=True)


def on_device(field, lon_test, lat_test, time_test, lon_core, lat_core, time_core):
    highest = lax.Precision.HIGHEST
    mixed = jnp.einsum("tij,jk->tik", field, lat_test, precision=highest)
    lon_part = jnp.einsum("tik,tk->ik", mixed, time_test, precision=highest)
    sketch_lon = lax.psum_scatter(lon_part, "lat", scatter_dimension=0, tiled=True)
    hour_part = jnp.einsum("tik,ik->tk", mixed, lon_test, precision=highest)
    sketch_time = lax.psum(hour_part, ("lon", "lat"))
    across = jnp.einsum("tij,ik->tkj", field, lon_test, precision=highest)
    lat_part = jnp.einsum("tkj,tk->jk", across, time_test, precision=highest)
    sketch_lat = lax.psum(lat_part, "lon")
    narrowed = jnp.einsum("tij,bj->tib", field, lat_core, precision=highest)
    crossed = jnp.einsum("tib,ai->tab", narrowed, lon_core, precision=highest)
    core_part = jnp.einsum("tab,ct->cab", crossed, time_core, precision=highest)
    core_sketch = sum_core(core_part)
    return (sketch_lon, sketch_lat, sketch_time, core_sketch)


def solution(mesh):
    return jax.shard_map(
        on_device,
        mesh=mesh,
        in_specs=(
            P(None, "lon", "lat"),
            P("lon", None),
            P("lat", None),
            P(),
            P(None, "lon"),
            P(None, "lat"),
            P(),
        ),
        out_specs=(P(("lon", "lat"), None), P("lat", None), P(), P(None, "lon", "lat")),
        check_vma=False,
    )
```

profile of v0, /device:TPU:0, one launch (start us, length us, event | category | flops | bytes accessed | tf_op | source)
XLA Modules:
  0.0 445.6 jit_solution(2891032700498763860)
XLA Ops:
  7.2 0.0 reduce-scatter.6.cloned.1.call-start
  7.2 27.4 %fusion.8 = f32[80,512,96]{1,2,0:T(8,128)} fusion(f32[80,512,128]{2,1,0:T(8,128)} %param.7, f32[96,128]{1,0:T(8,128)} %param.12), kind=kOutput, calls=%fused_computation.12 | convolution fusion | flops 6039797760 | bytes 36749312 | tf_op jit(solution)/shard_map/tij,bj->tib/dot_general | solution.py:22
  34.6 16.5 %convolution_bitcast_fusion.2 = f32[80,96,96]{1,2,0:T(8,128)} fusion(f32[80,512,96]{1,2,0:T(8,128)} %fusion.8, f32[96,512]{1,0:T(8,128)S(1)} %copy-done.2), kind=kOutput, calls=%fused_computation.7 | convolution fusion | flops 4529848320 | bytes 18874368 | tf_op jit(solution)/shard_map/tib,ai->tab/dot_general | solution.py:23
  51.2 6.3 %copy.11 = f32[80,96,96]{2,0,1:T(8,128)} copy(f32[80,96,96]{1,2,0:T(8,128)} %convolution_bitcast_fusion.2) | data formatting | bytes 5898240 | tf_op jit(solution)/shard_map/tib,ai->tab/transpose | solution.py:23
  57.5 22.5 %convolution_bitcast_fusion.1 = f32[96,96,96]{0,2,1:T(8,128)} fusion(f32[80,96,96]{2,0,1:T(8,128)} %copy.11, f32[96,80]{0,1:T(8,128)S(1)} %copy-done.4), kind=kOutput, calls=%fused_computation.6 | convolution fusion | flops 849346560 | bytes 6518784 | tf_op jit(solution)/shard_map/tab,ct->cab/dot_general | solution.py:24
  80.0 0.0 reduce-scatter.6.cloned.1.call-update
  80.1 0.0 all-reduce.6.cloned.1.call-start
  80.1 90.0 %reduce-scatter.6.cloned.1.call-done = f32[96,12,96]{0,2,1:T(8,128)} async-done(((f32[96,96,96]{0,2,1:T(8,128)}), f32[96,12,96]{0,2,1:T(8,128)}) %reduce-scatter.6.cloned.1.call-update) | async-done | bytes 442384 | tf_op jit(solution)/shard_map/reduce_scatter | solution.py:8
  170.2 0.0 all-reduce.4.cloned.1.call-start
  170.2 21.2 %convolution_bitcast_fusion = f32[80,200,128]{2,1,0:T(8,128)} fusion(f32[80,512,128]{2,1,0:T(8,128)} %param.7, f32[512,200]{0,1:T(8,128)S(1)} %copy-done), kind=kOutput, calls=%fused_computation.5 | convolution fusion | flops 12582912000 | bytes 29573120 | tf_op jit(solution)/shard_map/tij,ik->tkj/dot_general | solution.py:19
  191.4 0.1 copy.20
  191.5 13.5 %fusion.2 = f32[200,1,128]{2,1,0:T(1,128)} fusion(f32[80,200,1]{0,2,1:T(1,128)S(1)} %copy.20, f32[80,200,128]{2,1,0:T(8,128)} %convolution_bitcast_fusion), kind=kOutput, calls=%fused_computation.3 | convolution fusion | flops 24576000 | bytes 8358400 | tf_op jit(solution)/shard_map/tkj,tk->jk/dot_general | solution.py:20
  205.0 0.0 reduce-scatter.4.cloned.1.call-start
  205.0 36.4 %multiply_reduce_fusion = (f32[200,512]{1,0:T(8,128)S(1)}, f32[80,512,200]{1,2,0:T(8,128)}) fusion(f32[200,80]{0,1:T(8,128)S(1)} %bitcast.49, f32[80,512,128]{2,1,0:T(8,128)} %param.7, f32[128,200]{0,1:T(8,128)S(1)} %copy-done.3), kind=kOutput, calls=%fused_computation.2 | convolution fusion | flops 12599193600 | bytes 54315520 | tf_op jit(solution)/shard_map/tij,jk->tik/dot_general | solution.py:14
  241.5 1.0 copy.18
  242.5 0.0 reduce-scatter.4.cloned.1.call-update
  242.5 53.1 %fusion = f32[200,1,80]{2,1,0:T(1,128)S(1)} fusion(f32[80,512,200]{1,2,0:T(8,128)} %get-tuple-element.5, f32[512,200,1]{0,1,2:T(8,128)S(1)} %bitcast.46), kind=kOutput, calls=%fused_computation | convolution fusion | flops 98304000 | bytes 33241600 | tf_op jit(solution)/shard_map/tik,ik->tk/dot_general | solution.py:17
  295.6 0.1 copy.24
  295.8 0.6 dynamic-slice
  297.0 66.3 %psum.15 = f32[80,200]{1,0:T(8,128)} all-reduce(f32[80,200]{1,0:T(8,128)S(1)} %bitcast.51), channel_id=1, replica_groups=mesh['lon'=8,'lat'=16] {'lon','lat'}, use_global_device_ids=true, to_apply=%region_2.0 | all-reduce | flops 16000 | bytes 128000 | tf_op jit(solution)/shard_map/psum | solution.py:18
  363.3 1.5 constant_dynamic-slice_fusion
  364.8 11.8 %all-reduce.4.cloned.1.call-done = f32[128,200]{0,1:T(8,128)} async-done(((f32[128,200]{0,1:T(8,128)}), f32[128,200]{0,1:T(8,128)}) %all-reduce.4.cloned.1.call-update) | async-done | bytes 102416 | tf_op jit(solution)/shard_map/psum | solution.py:21
  376.6 60.7 %reduce-scatter.4.cloned.1.call-done = f32[32,200]{1,0:T(8,128)} async-done(((f32[512,200]{1,0:T(8,128)}), f32[32,200]{1,0:T(8,128)}) %reduce-scatter.4.cloned.1.call-update) | async-done | bytes 25616 | tf_op jit(solution)/shard_map/reduce_scatter | solution.py:16
  437.3 1.5 copy.35
  (15 shorter events, 0.1 us)
Async XLA Ops:
  7.2 163.1 %copy-start = (f32[512,200]{0,1:T(8,128)S(1)}, f32[512,200]{0,1:T(8,128)}, u32[]{:S(2)}) copy-start(f32[512,200]{0,1:T(8,128)} %param.8) | copy-start | bytes 1228804
  7.2 27.5 %copy-start.2 = (f32[96,512]{1,0:T(8,128)S(1)}, f32[96,512]{1,0:T(8,128)}, u32[]{:S(2)}) copy-start(f32[96,512]{1,0:T(8,128)} %param.11) | copy-start | bytes 589828
  7.2 162.9 %reduce-scatter.6.cloned.1.call-start = ((), (), s32[]{:S(2)}) async-start(), calls=%async_computation.4 | async-start | bytes 5308416 | tf_op jit(solution)/shard_map/reduce_scatter | solution.py:8
  34.6 22.9 %copy-start.4 = (f32[96,80]{0,1:T(8,128)S(1)}, f32[96,80]{0,1:T(8,128)}, u32[]{:S(2)}) copy-start(f32[96,80]{0,1:T(8,128)} %param.13) | copy-start | bytes 92164
  80.1 283.2 %all-reduce.6.cloned.1.call-start = ((), (), s32[]{:S(2)}) async-start(), calls=%async_computation.5 | async-start | bytes 1179648
  170.1 21.3 %copy-start.1 = (f32[80,200]{1,0:T(8,128)S(1)}, f32[80,200]{1,0:T(8,128)}, u32[]{:S(2)}) copy-start(f32[80,200]{1,0:T(8,128)} %param.10) | copy-start | bytes 192004
  170.2 34.9 %copy-start.3 = (f32[128,200]{0,1:T(8,128)S(1)}, f32[128,200]{0,1:T(8,128)}, u32[]{:S(2)}) copy-start(f32[128,200]{0,1:T(8,128)} %param.9) | copy-start | bytes 307204
  170.2 206.4 %all-reduce.4.cloned.1.call-start = ((), (), s32[]{:S(2)}) async-start(), calls=%async_computation.3 | async-start | bytes 204800 | tf_op jit(solution)/shard_map/psum | solution.py:21
  205.0 232.3 %reduce-scatter.4.cloned.1.call-start = ((), (), s32[]{:S(2)}) async-start(), calls=%async_computation.2 | async-start | bytes 557056 | tf_op jit(solution)/shard_map/reduce_scatter | solution.py:16
  242.5 53.3 %copy-start.5 = (u32[128]{0:T(128)S(1)}, u32[128]{0:T(128)}, u32[]{:S(2)}) copy-start(u32[128]{0:T(128)} %constant.3) | copy-start | bytes 1540
Sparse Core Ops, SparseCore 0:
  80.2 89.8 reduce-scatter.5
  172.6 116.7 all-reduce.5
  292.6 83.8 all-reduce.3
  379.3 57.9 reduce-scatter.3
where the time goes:
time: 448 us; the launch traced here: 446 us
  matrix products  191 us (43%)
  waiting for transfers between devices  163 us (36%)
  blocking collectives  66.3 us (15%)
  between operations  14.7 us (3%)
  local copies, waits for them, and re-layouts  11.2 us (2%)
    reduce_scatter x1, waiting for transfers between devices, sum_core(): lax.psum_scatter(partial_value, 'lon', scatter_dimension=1, tiled=True)  90 us
    psum x1, blocking collectives, on_device(): sketch_time = lax.psum(hour_part, ('lon', 'lat'))  66.3 us
    reduce_scatter x1, waiting for transfers between devices, on_device(): lax.psum_scatter(lon_part, 'lat', scatter_dimension=0, tiled=True)  60.7 us
    dot_general x1, matrix products, on_device(): hour_part = jnp.einsum('tik,ik->tk', mixed, lon_test, precision=highest)  53.1 us
    dot_general x1, matrix products, on_device(): mixed = jnp.einsum('tij,jk->tik', field, lat_test, precision=highest)  36.4 us
    dot_general x1, matrix products, on_device(): narrowed = jnp.einsum('tij,bj->tib', field, lat_core, precision=highest)  27.4 us
    dot_general x1, matrix products, on_device(): core_part = jnp.einsum('tab,ct->cab', crossed, time_core, precision=highest)  22.5 us
    dot_general x1, matrix products, on_device(): across = jnp.einsum('tij,ik->tkj', field, lon_test, precision=highest)  21.2 us
  transfers between devices with their start and end apart: 4, of which 3 were waited for; matrix products, arithmetic and copies ran while one was open for 29% of the time, Pallas kernels for 0%

commit v1 on v0

v1 whole, which is shorter than its diff:
```python
import jax
import jax.numpy as jnp
from jax import lax
from jax.experimental import pallas as pl
from jax.experimental.pallas import tpu as pltpu
from jax.sharding import PartitionSpec as P

F32 = jnp.float32
BF16 = jnp.bfloat16
BOTH = ("lon", "lat")
HOURS = 8
VMEM = 56 * 1024 * 1024


def halves(value):
    top = value.astype(BF16)
    return top, (value - top.astype(F32)).astype(BF16)


def dot(left, right, dims=((1,), (0,))):
    return lax.dot_general(left, right, (dims, ((), ())), preferred_element_type=F32)


def stacked_dot(weights, rows, right_top, right_low):
    upper = dot(weights[...], right_top)
    return upper[:rows] + upper[rows:] + dot(weights[:rows], right_low)


def pair_of_hours(field_ref, at):
    return jnp.concatenate([field_ref[at], field_ref[at + 1]], axis=1)


def core_kernel(field_ref, lon_ref, lat_ref, keep_ref, send_ref, weights, crossed):
    step = pl.program_id(0)
    modes = lon_ref.shape[0]

    @pl.when(step == 0)
    def _():
        top, low = halves(lon_ref[...])
        weights[:modes] = top
        weights[modes:] = low

    for at in range(0, HOURS, 2):
        top, low = halves(pair_of_hours(field_ref, at))
        both = stacked_dot(weights, modes, top, low)
        crossed[:, step, at, :] = both[:, :128]
        crossed[:, step, at + 1, :] = both[:, 128:]

    @pl.when(step == pl.num_programs(0) - 1)
    def _():
        lat_top, lat_low = halves(lat_ref[...])
        lats = jnp.concatenate([lat_top, lat_low], axis=0)
        for owner in range(8):
            block = crossed[owner * 12 : owner * 12 + 12].reshape(960, 128)
            block = jnp.concatenate([block, jnp.zeros((64, 128), F32)], axis=0)
            top, low = halves(block)
            upper = dot(lats, top, ((1,), (1,)))
            result = upper[:96] + upper[96:] + dot(lat_top, low, ((1,), (1,)))
            for part, out in enumerate((keep_ref, send_ref)):
                for b in range(6):
                    row = part * 48 + b * 8
                    for q in range(8):
                        out[owner, :, q * 6 + b, :] = result[row : row + 8, q * 128 : q * 128 + 128]


def core_partial(field, lon_core, lat_rows):
    hours, lons, lats = field.shape
    modes = lon_core.shape[0]
    shape = jax.ShapeDtypeStruct((8, 8, 48, 128), F32)
    whole = pl.BlockSpec((8, 8, 48, 128), lambda s: (0, 0, 0, 0))
    return pl.pallas_call(
        core_kernel,
        grid=(hours // HOURS,),
        in_specs=[
            pl.BlockSpec((HOURS, lons, lats), lambda s: (s, 0, 0)),
            pl.BlockSpec((modes, lons), lambda s: (0, 0)),
            pl.BlockSpec((96, lats), lambda s: (0, 0)),
        ],
        out_specs=[whole, whole],
        out_shape=[shape, shape],
        scratch_shapes=[
            pltpu.VMEM((2 * modes, lons), BF16),
            pltpu.VMEM((modes, hours // HOURS, HOURS, lats), F32),
        ],
        compiler_params=pltpu.CompilerParams(vmem_limit_bytes=VMEM),
        cost_estimate=pl.CostEstimate(flops=6 * hours * lons * lats * modes, bytes_accessed=24 << 20, transcendentals=0),
        name="core_partial",
    )(field, lon_core, lat_rows)


def across_kernel(field_ref, lon_ref, lat_ref, time_ref, out_ref, weights, lat_t):
    step = pl.program_id(0)
    rank = lat_t.shape[0]

    @pl.when(step == 0)
    def _():
        top, low = halves(lon_ref[...].T)
        weights[:rank] = top
        weights[rank:] = low
        lat_t[...] = lat_ref[...].T
        out_ref[...] = jnp.zeros_like(out_ref)

    times = time_ref[...].T
    lane = lax.broadcasted_iota(jnp.int32, (rank, 128), 1)
    lat_sum = out_ref[0]
    hour_sum = out_ref[1]
    for at in range(0, HOURS, 2):
        top, low = halves(pair_of_hours(field_ref, at))
        both = stacked_dot(weights, rank, top, low)
        for part in range(2):
            across = both[:, part * 128 : part * 128 + 128]
            hour = at + part
            lat_sum = lat_sum + across * times[:, hour : hour + 1]
            total = jnp.sum(across * lat_t[...], axis=1, keepdims=True)
            hour_sum = jnp.where(lane == step * HOURS + hour, total, hour_sum)
    out_ref[0] = lat_sum
    out_ref[1] = hour_sum


def across_partial(field, lon_test, lat_test, time_test):
    hours, lons, lats = field.shape
    rank = lon_test.shape[1]
    return pl.pallas_call(
        across_kernel,
        grid=(hours // HOURS,),
        in_specs=[
            pl.BlockSpec((HOURS, lons, lats), lambda s: (s, 0, 0)),
            pl.BlockSpec((lons, rank), lambda s: (0, 0)),
            pl.BlockSpec((lats, rank), lambda s: (0, 0)),
            pl.BlockSpec((HOURS, rank), lambda s: (s, 0)),
        ],
        out_specs=pl.BlockSpec((2, rank, 128), lambda s: (0, 0, 0)),
        out_shape=jax.ShapeDtypeStruct((2, rank, 128), F32),
        scratch_shapes=[pltpu.VMEM((2 * rank, lons), BF16), pltpu.VMEM((rank, lats), F32)],
        compiler_params=pltpu.CompilerParams(vmem_limit_bytes=VMEM),
        cost_estimate=pl.CostEstimate(flops=6 * hours * lons * lats * rank, bytes_accessed=22 << 20, transcendentals=0),
        name="across_partial",
    )(field, lon_test, lat_test, time_test)


def lon_kernel(field_ref, lat_ref, time_ref, out_ref):
    @pl.when(pl.program_id(0) == 0)
    def _():
        out_ref[...] = jnp.zeros_like(out_ref)

    total = out_ref[...]
    for at in range(0, HOURS, 2):
        top, low = halves(pair_of_hours(field_ref, at))
        tests = [lat_ref[...] * time_ref[hour : hour + 1, :] for hour in (at, at + 1)]
        test_top, test_low = halves(jnp.concatenate(tests, axis=0))
        total = total + dot(top, test_top) + dot(low, test_top) + dot(top, test_low)
    out_ref[...] = total


def lon_partial(field, lat_test, time_test):
    hours, lons, lats = field.shape
    rank = lat_test.shape[1]
    return pl.pallas_call(
        lon_kernel,
        grid=(hours // HOURS,),
        in_specs=[
            pl.BlockSpec((HOURS, lons, lats), lambda s: (s, 0, 0)),
            pl.BlockSpec((lats, rank), lambda s: (0, 0)),
            pl.BlockSpec((HOURS, rank), lambda s: (s, 0)),
        ],
        out_specs=pl.BlockSpec((lons, rank), lambda s: (0, 0)),
        out_shape=jax.ShapeDtypeStruct((lons, rank), F32),
        compiler_params=pltpu.CompilerParams(vmem_limit_bytes=VMEM),
        cost_estimate=pl.CostEstimate(flops=6 * hours * lons * lats * rank, bytes_accessed=22 << 20, transcendentals=0),
        name="lon_partial",
    )(field, lat_test, time_test)


def finish_kernel(parts_ref, time_ref, out_ref):
    total = parts_ref[0]
    for source in range(1, parts_ref.shape[0]):
        total = total + parts_ref[source]
    flipped = total.T
    column = jnp.concatenate([flipped[:, q * 6 : q * 6 + 6] for q in range(8)], axis=0)
    for a in range(12):
        out_ref[:, a, :] = lax.dot_general(
            time_ref[...],
            column[a * 80 : a * 80 + 80],
            (((1,), (0,)), ((), ())),
            precision=lax.Precision.HIGHEST,
            preferred_element_type=F32,
        )


def finish_core(parts, time_core):
    return pl.pallas_call(
        finish_kernel,
        out_shape=jax.ShapeDtypeStruct((96, 12, 6), F32),
        compiler_params=pltpu.CompilerParams(vmem_limit_bytes=VMEM),
        name="finish_core",
    )(parts, time_core)


def places(move):
    pairs = []
    for source in range(128):
        lon, lat = divmod(source, 16)
        x, y, z, core = (lon % 2) * 2 + lat // 8, lon // 2, lat // 2 % 4, lat % 2
        x, y, z, core = move(x, y, z, core)
        pairs.append((source, (y * 2 + x // 2) * 16 + x % 2 * 8 + z * 2 + core))
    return pairs


OTHER_CORE = places(lambda x, y, z, core: (x, y, z, 1 - core))
Y_FLIP = places(lambda x, y, z, core: (x, y ^ 1, z, core))
Y_FOLD = places(lambda x, y, z, core: (x, 3 - y, z, core))
Z_FLIP = places(lambda x, y, z, core: (x, y, z ^ 1, core))
Z_FOLD = places(lambda x, y, z, core: (x, y, 3 - z, core))
X_FLIP = places(lambda x, y, z, core: (x ^ 1, y, z, core))
X_HALF = places(lambda x, y, z, core: (x ^ 2, y, z, core))
SAME_CORE = [[lon * 16 + 2 * at + core for lon in range(8) for at in range(8)] for core in (0, 1)]


def add_from(value, pairs):
    return value + lax.ppermute(value, BOTH, pairs)


def on_device(field, lon_test, lat_test, time_test, lon_core, lat_core, time_core):
    core = lax.axis_index("lat") % 2

    rows = lat_core.reshape(8, 2, 6, -1)
    rows = jnp.where(core == 0, rows, rows[:, ::-1])
    rows = rows.transpose(1, 2, 0, 3).reshape(96, -1)
    keep, send = core_partial(field, lon_core, rows)
    arrived = lax.ppermute(send, BOTH, OTHER_CORE)
    chip = (keep + arrived).reshape(64, 48, 128)
    parts = lax.all_to_all(chip, BOTH, 0, 0, axis_index_groups=SAME_CORE)

    sums = across_partial(field, lon_test, lat_test, time_test)
    other = lax.ppermute(lax.dynamic_slice(sums[1], ((1 - core) * 96, 0), (104, 128)), BOTH, OTHER_CORE)
    hour = lax.dynamic_slice(sums[1], (core * 96, 0), (104, 128)) + other
    joined = jnp.concatenate([sums[0], hour], axis=0)
    for pairs in (Y_FLIP, Y_FOLD, X_HALF):
        joined = add_from(joined, pairs)
    sketch_lat = joined[:200].T
    hour = joined[200:]
    for pairs in (Z_FLIP, Z_FOLD, X_FLIP):
        hour = add_from(hour, pairs)
    other = lax.ppermute(hour, BOTH, OTHER_CORE)
    first, second = jnp.where(core == 0, hour, other), jnp.where(core == 0, other, hour)
    sketch_time = jnp.concatenate([first[:96], second], axis=0).T[:80]

    lon_part = lon_partial(field, lat_test, time_test)
    shares = lax.all_to_all(lon_part.reshape(16, 32, 200), "lat", 0, 0)
    sketch_lon = jnp.sum(shares, axis=0)

    core_sketch = finish_core(parts, time_core)
    return (sketch_lon, sketch_lat, sketch_time, core_sketch)


def solution(mesh):
    return jax.shard_map(
        on_device,
        mesh=mesh,
        in_specs=(
            P(None, "lon", "lat"),
            P("lon", None),
            P("lat", None),
            P(),
            P(None, "lon"),
            P(None, "lat"),
            P(),
        ),
        out_specs=(P(("lon", "lat"), None), P("lat", None), P(), P(None, "lon", "lat")),
        check_vma=False,
    )
```

time: 448 us -> 135 us (0.30)
  matrix products: 191 us -> 0 us
  waiting for transfers between devices: 163 us -> 39.3 us
  blocking collectives: 66.3 us -> 0 us
  Pallas kernels: 0 us -> 52.2 us
  starting transfers between devices: 0.16 us -> 28.2 us
  between operations: 14.7 us -> 0.79 us
    dot_general x7 -> x0, matrix products: 191 us -> none  [the longest x1 53.1 us: on_device(): hour_part = jnp.einsum('tik,ik->tk', mixed, lon_test, precision=highest)]
    reduce_scatter x2 -> x0, waiting for transfers between devices: 151 us -> none  [the longest x1 90 us: sum_core(): lax.psum_scatter(partial_value, 'lon', scatter_dimension=1, tiled=True)]
    psum x1 -> x0, blocking collectives: 66.3 us -> none  [on_device(): sketch_time = lax.psum(hour_part, ('lon', 'lat'))]
    pallas_call x0 -> x4, Pallas kernels: none -> 52.2 us  [the longest x1 17.9 us: core_partial(): pl.pallas_call(core_kernel, grid=(hours // HOURS,), in_specs=[pl.BlockSpe...]
    ppermute x0 -> x9, waiting for transfers between devices: none -> 32.9 us  [the longest x6 32.3 us: add_from(): return value + lax.ppermute(value, BOTH, pairs)]
    all_to_all x0 -> x2, starting transfers between devices: none -> 14.5 us  [the longest x1 8.06 us: on_device(): parts = lax.all_to_all(chip, BOTH, 0, 0, axis_index_groups=SAME_CORE)]
    ppermute x0 -> x9, starting transfers between devices: none -> 13.7 us  [the longest x6 13 us: add_from(): return value + lax.ppermute(value, BOTH, pairs)]
    psum x1 -> x0, waiting for transfers between devices: 11.8 us -> none  [on_device(): sketch_lat = lax.psum(lat_part, 'lon')]
  transfers between devices with their start and end apart: 4 -> 11, of which waited for: 3 -> 7; matrix products, arithmetic and copies ran while one was open for 29% -> 6% of each run, Pallas kernels for 0% -> 23%
where the time goes in v1:
time: 135 us; the launch traced here: 133 us
  Pallas kernels  52.2 us (39%)
  waiting for transfers between devices  39.3 us (29%)
  starting transfers between devices  28.2 us (21%)
  local copies, waits for them, and re-layouts  9.49 us (7%)
  other arithmetic  3.54 us (3%)
    ppermute x6, waiting for transfers between devices, add_from(): return value + lax.ppermute(value, BOTH, pairs)  32.3 us
    pallas_call x1, Pallas kernels, core_partial(): pl.pallas_call(core_kernel, grid=(hours // HOURS,), in_specs=[pl.BlockSpe...  17.9 us
    pallas_call x1, Pallas kernels, across_partial(): pl.pallas_call(across_kernel, grid=(hours // HOURS,), in_specs=[pl.BlockS...  15.5 us
    pallas_call x1, Pallas kernels, lon_partial(): pl.pallas_call(lon_kernel, grid=(hours // HOURS,), in_specs=[pl.BlockSpec...  15.5 us
    ppermute x6, starting transfers between devices, add_from(): return value + lax.ppermute(value, BOTH, pairs)  13 us
    all_to_all x1, starting transfers between devices, on_device(): parts = lax.all_to_all(chip, BOTH, 0, 0, axis_index_groups=SAME_CORE)  8.06 us
    unnamed x15, local copies, waits for them, and re-layouts  6.42 us
    all_to_all x1, starting transfers between devices, on_device(): shares = lax.all_to_all(lon_part.reshape(16, 32, 200), 'lat', 0, 0)  6.42 us
  transfers between devices with their start and end apart: 11, of which 7 were waited for; matrix products, arithmetic and copies ran while one was open for 6% of the time, Pallas kernels for 23%

profile of v1, /device:TPU:0, one launch (start us, length us, event | category | flops | bytes accessed | tf_op | source)
XLA Modules:
  0.0 133.5 jit_solution(9285488647170132831)
XLA Ops:
  0.6 0.8 reshape.23
  2.1 17.9 %core_partial.1 = (f32[8,8,48,128]{3,2,1,0:T(8,128)}, f32[8,8,48,128]{3,2,1,0:T(8,128)}) custom-call(f32[80,512,128]{2,1,0:T(8,128)} %field_ref.5, f32[96,512]{1,0:T(8,128)} %lon_ref.2, f32[96,128]{1,0:T(8,128)} %bitcast.18), custom_call_target="tpu_custom_call" | custom-call | flops 3019898880 | bytes 25165824 | tf_op jit(solution)/shard_map/core_partial/pallas_call | solution.py:71
  20.8 1.0 copy.20.lon_ref
  21.8 15.5 %across_partial.1 = f32[2,200,128]{2,1,0:T(8,128)} custom-call(f32[80,512,128]{2,1,0:T(8,128)} %field_ref.5, f32[512,200]{1,0:T(8,128)} %copy.20.lon_ref, f32[128,200]{1,0:T(8,128)} %copy.19.lat_ref, f32[80,200]{1,0:T(8,128)} %time_ref.4), custom_call_target="tpu_custom_call" | custom-call | flops 6291456000 | bytes 23068672 | tf_op jit(solution)/shard_map/across_partial/pallas_call | solution.py:123
  37.3 1.0 slice_bitcast_fusion.1
  38.9 15.5 %lon_partial.1 = f32[512,200]{1,0:T(8,128)} custom-call(f32[80,512,128]{2,1,0:T(8,128)} %field_ref.5, f32[128,200]{1,0:T(8,128)} %copy.19.lat_ref, f32[80,200]{1,0:T(8,128)} %time_ref.4), custom_call_target="tpu_custom_call" | custom-call | flops 6291456000 | bytes 23068672 | tf_op jit(solution)/shard_map/lon_partial/pallas_call | solution.py:158
  54.4 6.4 %all-to-all-start = ((f32[16,32,200]{2,1,0:T(8,128)}), f32[16,32,200]{2,1,0:T(8,128)S(1)}, u32[]{:S(2)}, u32[]{:S(2)}) async-start(f32[16,32,200]{2,1,0:T(8,128)} %bitcast.16), calls=%async_computation | async-start | bytes 1048576 | tf_op jit(solution)/shard_map/all_to_all | solution.py:249
  60.9 1.7 %collective-permute-start.1 = (f32[304,128]{1,0:T(8,128)S(1)}, f32[304,128]{1,0:T(8,128)S(1)}, u32[]{:S(2)}, u32[]{:S(2)}) collective-permute-start(f32[304,128]{1,0:T(8,128)S(1)} %pad_maximum_fusion), channel_id=1, source_target_pairs={{0,32},{1,33},{2,34},{3,35},{4,36},{5,37},{6,38},{7,39},{8,40},{9,... | collective-permute-start | bytes 466952 | tf_op jit(solution)/shard_map/ppermute | solution.py:220
  62.5 2.7 %add.44 = f32[8,8,48,128]{3,2,1,0:T(8,128)} add(f32[8,8,48,128]{3,2,1,0:T(8,128)S(1)} %copy-done.1, f32[8,8,48,128]{3,2,1,0:T(8,128)} %collective-permute-done.8) | non-fusion elementwise | flops 393216 | bytes 4718592 | tf_op jit(solution)/shard_map/add | solution.py:231
  65.3 6.4 %all-to-all-done = f32[16,32,200]{2,1,0:T(8,128)S(1)} async-done(((f32[16,32,200]{2,1,0:T(8,128)}), f32[16,32,200]{2,1,0:T(8,128)S(1)}, u32[]{:S(2)}, u32[]{:S(2)}) %all-to-all-start) | async-done | bytes 409632 | tf_op jit(solution)/shard_map/all_to_all | solution.py:249
  71.7 8.1 %all-to-all-start.1 = ((f32[64,48,128]{2,1,0:T(8,128)}), f32[64,48,128]{2,1,0:T(8,128)S(1)}, u32[]{:S(2)}, u32[]{:S(2)}) async-start(f32[64,48,128]{2,1,0:T(8,128)} %bitcast.8), calls=%async_computation.1 | async-start | bytes 3145728 | tf_op jit(solution)/shard_map/all_to_all | solution.py:232
  79.8 3.1 %collective-permute-start.2 = (f32[304,128]{1,0:T(8,128)S(1)}, f32[304,128]{1,0:T(8,128)S(1)}, u32[]{:S(2)}, u32[]{:S(2)}) collective-permute-start(f32[304,128]{1,0:T(8,128)S(1)} %fusion.1), channel_id=1, source_target_pairs={{0,96},{1,97},{2,98},{3,99},{4,100},{5,101},{6,102},{7,103},{8,104... | collective-permute-start | bytes 466952 | tf_op jit(solution)/shard_map/ppermute | solution.py:220
  82.9 20.7 %collective-permute-done.2 = f32[304,128]{1,0:T(8,128)S(1)} collective-permute-done((f32[304,128]{1,0:T(8,128)S(1)}, f32[304,128]{1,0:T(8,128)S(1)}, u32[]{:S(2)}, u32[]{:S(2)}) %collective-permute-start.2) | collective-permute-done | bytes 155680 | tf_op jit(solution)/shard_map/ppermute | solution.py:220
  103.6 3.1 %collective-permute-start.3 = (f32[304,128]{1,0:T(8,128)S(1)}, f32[304,128]{1,0:T(8,128)S(1)}, u32[]{:S(2)}, u32[]{:S(2)}) collective-permute-start(f32[304,128]{1,0:T(8,128)S(1)} %add.39), channel_id=1, source_target_pairs={{0,16},{1,17},{2,18},{3,19},{4,20},{5,21},{6,22},{7,23},{8,24},{9,... | collective-permute-start | bytes 466952 | tf_op jit(solution)/shard_map/ppermute | solution.py:220
  106.7 4.4 %collective-permute-done.3 = f32[304,128]{1,0:T(8,128)S(1)} collective-permute-done((f32[304,128]{1,0:T(8,128)S(1)}, f32[304,128]{1,0:T(8,128)S(1)}, u32[]{:S(2)}, u32[]{:S(2)}) %collective-permute-start.3) | collective-permute-done | bytes 155680 | tf_op jit(solution)/shard_map/ppermute | solution.py:220
  111.1 1.3 collective-permute-start.4
  112.4 2.9 %collective-permute-done.4 = f32[104,128]{1,0:T(8,128)S(1)} collective-permute-done((f32[104,128]{1,0:T(8,128)S(1)}, f32[104,128]{1,0:T(8,128)S(1)}, u32[]{:S(2)}, u32[]{:S(2)}) %collective-permute-start.4) | collective-permute-done | bytes 53280 | tf_op jit(solution)/shard_map/ppermute | solution.py:220
  115.3 2.2 %collective-permute-start.5 = (f32[104,128]{1,0:T(8,128)S(1)}, f32[104,128]{1,0:T(8,128)S(1)}, u32[]{:S(2)}, u32[]{:S(2)}) collective-permute-start(f32[104,128]{1,0:T(8,128)S(1)} %slice_add_fusion), channel_id=1, source_target_pairs={{0,6},{1,7},{2,4},{3,5},{4,2},{5,3},{6,0},{7,1},{8,14},{9,15},{10,... | collective-permute-start | bytes 159752 | tf_op jit(solution)/shard_map/ppermute | solution.py:220
  117.5 3.2 %collective-permute-done.5 = f32[104,128]{1,0:T(8,128)S(1)} collective-permute-done((f32[104,128]{1,0:T(8,128)S(1)}, f32[104,128]{1,0:T(8,128)S(1)}, u32[]{:S(2)}, u32[]{:S(2)}) %collective-permute-start.5) | collective-permute-done | bytes 53280 | tf_op jit(solution)/shard_map/ppermute | solution.py:220
  120.7 1.7 %collective-permute-start.6 = (f32[104,128]{1,0:T(8,128)S(1)}, f32[104,128]{1,0:T(8,128)S(1)}, u32[]{:S(2)}, u32[]{:S(2)}) collective-permute-start(f32[104,128]{1,0:T(8,128)S(1)} %add.42), channel_id=1, source_target_pairs={{0,8},{1,9},{2,10},{3,11},{4,12},{5,13},{6,14},{7,15},{8,0},{9,1},... | collective-permute-start | bytes 159752 | tf_op jit(solution)/shard_map/ppermute | solution.py:220
  123.7 1.2 collective-permute-done.6
  127.0 1.2 copy-done
  128.2 3.3 %finish_core.1 = f32[96,12,6]{2,1,0:T(8,128)} custom-call(f32[64,48,128]{2,1,0:T(8,128)} %copy-done, f32[96,80]{1,0:T(8,128)} %copy.23.time_ref), custom_call_target="tpu_custom_call" | custom-call | tf_op jit(solution)/shard_map/finish_core/pallas_call | solution.py:191
  131.5 2.0 %copy.25 = f32[96,12,6]{0,2,1:T(8,128)} copy(f32[96,12,6]{2,1,0:T(8,128)} %finish_core.1) | data formatting | bytes 55296
  (37 shorter events, 5.6 us)
Async XLA Ops:
  2.1 17.9 %copy-start.3 = (f32[128,200]{0,1:T(8,128)S(1)}, f32[128,200]{0,1:T(8,128)}, u32[]{:S(2)}) copy-start(f32[128,200]{0,1:T(8,128)} %param.9) | copy-start | bytes 307204
  2.1 18.7 %copy-start.2 = (f32[512,200]{0,1:T(8,128)S(1)}, f32[512,200]{0,1:T(8,128)}, u32[]{:S(2)}) copy-start(f32[512,200]{0,1:T(8,128)} %param.8) | copy-start | bytes 1228804
  20.0 42.5 %collective-permute-start.8 = (f32[8,8,48,128]{3,2,1,0:T(8,128)}, f32[8,8,48,128]{3,2,1,0:T(8,128)}, u32[]{:S(2)}, u32[]{:S(2)}) collective-permute-start(f32[8,8,48,128]{3,2,1,0:T(8,128)} %get-tuple-element.7), channel_id=1, source_target_pairs={{0,1},{1,0},{2,3},{3,2},{4,5},{5,4},{6,7},{7,6},{8,9},{9,8},{10,11... | collective-permute-start | bytes 4718600 | tf_op jit(solution)/shard_map/ppermute | solution.py:230
  38.3 22.5 %collective-permute-start = (f32[104,128]{1,0:T(8,128)S(1)}, f32[104,128]{1,0:T(8,128)S(1)}, u32[]{:S(2)}, u32[]{:S(2)}) collective-permute-start(f32[104,128]{1,0:T(8,128)S(1)} %dynamic-slice_bitcast_fusion), channel_id=1, source_target_pairs={{0,1},{1,0},{2,3},{3,2},{4,5},{5,4},{6,7},{7,6},{8,9},{9,8},{10,11... | collective-permute-start | bytes 159752 | tf_op jit(solution)/shard_map/ppermute | solution.py:235
  38.9 23.6 %copy-start.1 = (f32[8,8,48,128]{3,2,1,0:T(8,128)S(1)}, f32[8,8,48,128]{3,2,1,0:T(8,128)}, u32[]{:S(2)}) copy-start(f32[8,8,48,128]{3,2,1,0:T(8,128)} %get-tuple-element.6) | copy-start | bytes 4718596
  54.4 17.3 %all-to-all-start = ((f32[16,32,200]{2,1,0:T(8,128)}), f32[16,32,200]{2,1,0:T(8,128)S(1)}, u32[]{:S(2)}, u32[]{:S(2)}) async-start(f32[16,32,200]{2,1,0:T(8,128)} %bitcast.16), calls=%async_computation | async-start | bytes 1048576 | tf_op jit(solution)/shard_map/all_to_all | solution.py:249
  60.9 18.9 %collective-permute-start.1 = (f32[304,128]{1,0:T(8,128)S(1)}, f32[304,128]{1,0:T(8,128)S(1)}, u32[]{:S(2)}, u32[]{:S(2)}) collective-permute-start(f32[304,128]{1,0:T(8,128)S(1)} %pad_maximum_fusion), channel_id=1, source_target_pairs={{0,32},{1,33},{2,34},{3,35},{4,36},{5,37},{6,38},{7,39},{8,40},{9,... | collective-permute-start | bytes 466952 | tf_op jit(solution)/shard_map/ppermute | solution.py:220
  71.7 55.3 %all-to-all-start.1 = ((f32[64,48,128]{2,1,0:T(8,128)}), f32[64,48,128]{2,1,0:T(8,128)S(1)}, u32[]{:S(2)}, u32[]{:S(2)}) async-start(f32[64,48,128]{2,1,0:T(8,128)} %bitcast.8), calls=%async_computation.1 | async-start | bytes 3145728 | tf_op jit(solution)/shard_map/all_to_all | solution.py:232
  79.7 42.6 %copy-start.4 = (f32[96,80]{0,1:T(8,128)S(1)}, f32[96,80]{0,1:T(8,128)}, u32[]{:S(2)}) copy-start(f32[96,80]{0,1:T(8,128)} %param.13) | copy-start | bytes 92164
  79.8 23.7 %collective-permute-start.2 = (f32[304,128]{1,0:T(8,128)S(1)}, f32[304,128]{1,0:T(8,128)S(1)}, u32[]{:S(2)}, u32[]{:S(2)}) collective-permute-start(f32[304,128]{1,0:T(8,128)S(1)} %fusion.1), channel_id=1, source_target_pairs={{0,96},{1,97},{2,98},{3,99},{4,100},{5,101},{6,102},{7,103},{8,104... | collective-permute-start | bytes 466952 | tf_op jit(solution)/shard_map/ppermute | solution.py:220
  103.6 7.5 %collective-permute-start.3 = (f32[304,128]{1,0:T(8,128)S(1)}, f32[304,128]{1,0:T(8,128)S(1)}, u32[]{:S(2)}, u32[]{:S(2)}) collective-permute-start(f32[304,128]{1,0:T(8,128)S(1)} %add.39), channel_id=1, source_target_pairs={{0,16},{1,17},{2,18},{3,19},{4,20},{5,21},{6,22},{7,23},{8,24},{9,... | collective-permute-start | bytes 466952 | tf_op jit(solution)/shard_map/ppermute | solution.py:220
  111.1 4.2 %collective-permute-start.4 = (f32[104,128]{1,0:T(8,128)S(1)}, f32[104,128]{1,0:T(8,128)S(1)}, u32[]{:S(2)}, u32[]{:S(2)}) collective-permute-start(f32[104,128]{1,0:T(8,128)S(1)} %slice.28), channel_id=1, source_target_pairs={{0,2},{1,3},{2,0},{3,1},{4,6},{5,7},{6,4},{7,5},{8,10},{9,11},{10,... | collective-permute-start | bytes 159752 | tf_op jit(solution)/shard_map/ppermute | solution.py:220
  115.3 5.4 %collective-permute-start.5 = (f32[104,128]{1,0:T(8,128)S(1)}, f32[104,128]{1,0:T(8,128)S(1)}, u32[]{:S(2)}, u32[]{:S(2)}) collective-permute-start(f32[104,128]{1,0:T(8,128)S(1)} %slice_add_fusion), channel_id=1, source_target_pairs={{0,6},{1,7},{2,4},{3,5},{4,2},{5,3},{6,0},{7,1},{8,14},{9,15},{10,... | collective-permute-start | bytes 159752 | tf_op jit(solution)/shard_map/ppermute | solution.py:220
  120.7 4.2 %collective-permute-start.6 = (f32[104,128]{1,0:T(8,128)S(1)}, f32[104,128]{1,0:T(8,128)S(1)}, u32[]{:S(2)}, u32[]{:S(2)}) collective-permute-start(f32[104,128]{1,0:T(8,128)S(1)} %add.42), channel_id=1, source_target_pairs={{0,8},{1,9},{2,10},{3,11},{4,12},{5,13},{6,14},{7,15},{8,0},{9,1},... | collective-permute-start | bytes 159752 | tf_op jit(solution)/shard_map/ppermute | solution.py:220
  124.9 1.3 collective-permute-start.7
  127.0 1.2 copy-start

commit v2 on v0

v2 whole, which is shorter than its diff:
```python
import jax
import jax.numpy as jnp
from jax import lax
from jax.experimental import pallas as pl
from jax.experimental.pallas import tpu as pltpu
from jax.sharding import PartitionSpec as P

F32 = jnp.float32
BF16 = jnp.bfloat16
BOTH = ("lon", "lat")
HOURS = 8
VMEM = 48 * 1024 * 1024
MOST_VMEM = 62 * 1024 * 1024
SLOTS = (
    22, 12, 52, 3, 19, 5, 60, 58, 2, 33, 10, 8, 29, 26, 25, 9,
    44, 18, 62, 11, 47, 40, 15, 39, 56, 57, 32, 23, 49, 43, 21, 45,
    42, 34, 35, 46, 20, 61, 37, 14, 63, 53, 0, 38, 27, 50, 1, 55,
    6, 13, 24, 41, 30, 28, 59, 31, 7, 16, 4, 48, 51, 54, 36, 17,
)


def halves(value):
    top = value.astype(BF16)
    return top, (value - top.astype(F32)).astype(BF16)


def dot(left, right, dims=((1,), (0,))):
    return lax.dot_general(left, right, (dims, ((), ())), preferred_element_type=F32)


def stacked_dot(weights, rows, right_top, right_low):
    upper = dot(weights[...], right_top)
    return upper[:rows] + upper[rows:] + dot(weights[:rows], right_low)


def block_copy(field_hbm, field, arrived, at):
    part = pl.ds(at * HOURS, HOURS)
    return pltpu.make_async_copy(field_hbm.at[part], field.at[part], arrived.at[at])


def start_field(field_hbm, field, arrived, blocks):
    for at in blocks:
        block_copy(field_hbm, field, arrived, at).start()


def each_block(field_hbm, field, arrived, work):
    def step(at, carry):
        block_copy(field_hbm, field, arrived, at).wait()
        work(at)
        return carry

    lax.fori_loop(0, arrived.shape[0], step, 0)


def field_scratch(hours, lons, lats):
    return [pltpu.VMEM((hours, lons, lats), F32), pltpu.SemaphoreType.DMA((hours // HOURS,))]


def copies_in(sources, targets, arrived):
    copies = [pltpu.make_async_copy(a, b, arrived.at[i]) for i, (a, b) in enumerate(zip(sources, targets))]
    for copy in copies:
        copy.start()
    return copies


def in_vmem(count):
    return [pl.BlockSpec(memory_space=pltpu.VMEM)] * count


def in_hbm(count):
    return [pl.BlockSpec(memory_space=pltpu.HBM)] * count


def first_kernel(
    field_hbm, lon_core_hbm, lon_test_hbm, lat_test_hbm, time_hbm, lat_core_hbm, send_hbm, keep_hbm, sums_ref,
    field, arrived, lon_core, lon_test, lat_test, time_test, lat_core, small, weights, crossed, lat_sum, hour_sum,
    shares, sent,
):
    modes, rank = lon_core.shape[0], lon_test.shape[0]
    rows = modes + rank
    lane = lax.broadcasted_iota(jnp.int32, (rank, 128), 1)
    sources = (lon_core_hbm, lon_test_hbm, lat_test_hbm, time_hbm, lat_core_hbm)
    waits = copies_in(sources, (lon_core, lon_test, lat_test, time_test, lat_core), small)
    start_field(field_hbm, field, arrived, range(1))
    lat_sum[...] = jnp.zeros_like(lat_sum)
    hour_sum[...] = jnp.zeros_like(hour_sum)
    for copy in waits:
        copy.wait()
    start_field(field_hbm, field, arrived, range(1, arrived.shape[0]))
    top, low = halves(jnp.concatenate([lon_core[...], lon_test[...]], axis=0))
    weights[:rows] = top
    weights[rows:] = low

    def work(at):
        times = time_test[pl.ds(at * HOURS, HOURS), :].T
        lat_total, hour_total = lat_sum[...], hour_sum[...]
        for pair in range(0, HOURS, 2):
            first = at * HOURS + pair
            top, low = halves(jnp.concatenate([field[first], field[first + 1]], axis=1))
            both = stacked_dot(weights, rows, top, low)
            for part in range(2):
                hour = pair + part
                result = both[:, part * 128 : part * 128 + 128]
                crossed[:, at, hour, :] = result[:modes]
                across = result[modes:]
                lat_total = lat_total + across * times[:, hour : hour + 1]
                total = jnp.sum(across * lat_test[...], axis=1, keepdims=True)
                hour_total = jnp.where(lane == at * HOURS + hour, total, hour_total)
        lat_sum[...] = lat_total
        hour_sum[...] = hour_total

    each_block(field_hbm, field, arrived, work)

    core = lax.axis_index("lat") % 2
    of_core = [
        jnp.concatenate([lat_core[pl.ds(at * 6 + b, 8, stride=12), :] for b in range(6)], axis=0) for at in range(2)
    ]
    lat_rows = jnp.concatenate(
        [jnp.where(core == 0, of_core[0], of_core[1]), jnp.where(core == 0, of_core[1], of_core[0])], axis=0
    )
    lat_top, lat_low = halves(lat_rows)
    lats = jnp.concatenate(
        [jnp.concatenate([lat_top, lat_top], axis=1), jnp.concatenate([lat_low, jnp.zeros_like(lat_low)], axis=1)],
        axis=0,
    )

    def share_copies(owner):
        targets = ((1, send_hbm), (0, keep_hbm))
        return [pltpu.make_async_copy(shares.at[p, owner], out.at[owner], sent.at[p, owner]) for p, out in targets]

    def share(owner, carry):
        block = crossed[pl.ds(owner * 12, 12)].reshape(960, 128)
        block = jnp.concatenate([block, jnp.zeros((64, 128), F32)], axis=0)
        result = dot(lats, jnp.concatenate(halves(block), axis=1), ((1,), (1,)))
        result = result[:96] + result[96:]
        for part in (1, 0):
            for b in range(6):
                row = part * 48 + b * 8
                for q in range(8):
                    shares[part, owner, :, q * 6 + b, :] = result[row : row + 8, q * 128 : q * 128 + 128]
        for copy in share_copies(owner):
            copy.start()
        return carry

    lax.fori_loop(0, 8, share, 0)
    for group in range(25):
        for part, total in enumerate((lat_sum, hour_sum)):
            tile = total[group * 8 : group * 8 + 8]
            sums_ref[2 * group, part * 4 : part * 4 + 4] = tile[:4]
            sums_ref[2 * group + 1, part * 4 : part * 4 + 4] = tile[4:]
    sums_ref[50:] = jnp.zeros((14, 8, 128), F32)
    for owner in range(8):
        for copy in share_copies(owner):
            copy.wait()


def first_partials(field, lon_core, lon_test_t, lat_test_t, time_test, lat_core):
    hours, lons, lats = field.shape
    modes, rank = lon_core.shape[0], lon_test_t.shape[0]
    part = jax.ShapeDtypeStruct((8, 8, 48, 128), F32)
    return pl.pallas_call(
        first_kernel,
        in_specs=in_hbm(6),
        out_specs=in_hbm(2) + in_vmem(1),
        out_shape=[part, part, jax.ShapeDtypeStruct((64, 8, 128), F32)],
        scratch_shapes=field_scratch(hours, lons, lats)
        + [pltpu.VMEM(x.shape, F32) for x in (lon_core, lon_test_t, lat_test_t, time_test, lat_core)]
        + [
            pltpu.SemaphoreType.DMA((5,)),
            pltpu.VMEM((2 * (modes + rank), lons), BF16),
            pltpu.VMEM((modes, hours // HOURS, HOURS, lats), F32),
            pltpu.VMEM((rank, 128), F32),
            pltpu.VMEM((rank, 128), F32),
            pltpu.VMEM((2, 8, 8, 48, 128), F32),
            pltpu.SemaphoreType.DMA((2, 8)),
        ],
        compiler_params=pltpu.CompilerParams(vmem_limit_bytes=MOST_VMEM),
        cost_estimate=pl.CostEstimate(flops=20 * 10**9, bytes_accessed=28 << 20, transcendentals=0),
        name="first_partials",
    )(field, lon_core, lon_test_t, lat_test_t, time_test, lat_core)


def join_kernel(keep_hbm, arrived_hbm, sums_hbm, out_hbm, keep, arrived, sums, copied, out, sent):
    pieces = [pl.ds(at * 16, 16) for at in range(4)]
    waits = copies_in(
        [sums_hbm] + [ref.at[piece] for piece in pieces for ref in (keep_hbm, arrived_hbm)],
        [sums] + [ref.at[piece] for piece in pieces for ref in (keep, arrived)],
        copied,
    )
    waits[0].wait()
    for at in range(4):
        waits[1 + 2 * at].wait()
        waits[2 + 2 * at].wait()
        for chip in range(at * 16, at * 16 + 16):
            slot = SLOTS.index(chip)
            out[slot, :48] = keep[chip] + arrived[chip]
            out[slot, 48:] = sums[chip % 8]
    copies = []
    for at, piece in enumerate(pieces):
        copies.append(pltpu.make_async_copy(out.at[piece], out_hbm.at[piece], sent.at[at]))
        copies[-1].start()
    for copy in copies:
        copy.wait()


def join_shares(keep, arrived, sums):
    shape = (64, 56, 128)
    return pl.pallas_call(
        join_kernel,
        in_specs=[pl.BlockSpec(memory_space=pl.ANY)] * 3,
        out_specs=pl.BlockSpec(memory_space=pl.ANY),
        out_shape=jax.ShapeDtypeStruct(shape, F32),
        scratch_shapes=[pltpu.VMEM(x.shape, F32) for x in (keep, arrived, sums)]
        + [pltpu.SemaphoreType.DMA((9,)), pltpu.VMEM(shape, F32), pltpu.SemaphoreType.DMA((4,))],
        compiler_params=pltpu.CompilerParams(vmem_limit_bytes=MOST_VMEM),
        cost_estimate=pl.CostEstimate(flops=10**6, bytes_accessed=5 << 20, transcendentals=0),
        name="join_shares",
    )(keep, arrived, sums)


def lon_kernel(field_hbm, lat_ref, time_ref, keep_ref, send_ref, field, arrived, lat_test, total):
    start_field(field_hbm, field, arrived, range(arrived.shape[0]))
    total[...] = jnp.zeros_like(total)
    lat_test[...] = lat_ref[...].T
    lons = total.shape[0]

    def work(at):
        times = time_ref[pl.ds(at * HOURS, HOURS), :]
        tests = [lat_test[...] * times[hour : hour + 1, :] for hour in range(HOURS)]
        test_top, test_low = halves(jnp.concatenate(tests, axis=0))
        values = [halves(field[at * HOURS + hour]) for hour in range(HOURS)]
        top = jnp.concatenate([value[0] for value in values], axis=1)
        low = jnp.concatenate([value[1] for value in values], axis=1)
        upper = dot(jnp.concatenate([top, low], axis=0), test_top)
        total[...] += upper[:lons] + upper[lons:] + dot(top, test_low)

    each_block(field_hbm, field, arrived, work)
    place = lax.axis_index("lat")
    core, z, x_lo = place % 2, place // 2 % 4, place // 8
    for at in range(8):
        flip, step = at // 4, at % 4
        x = x_lo + flip - 2 * x_lo * flip
        owner = x * 8 + (z + step) % 4 * 2
        for out, of_core in ((keep_ref, core), (send_ref, 1 - core)):
            out[at] = total[pl.ds(pl.multiple_of((owner + of_core) * 32, 32), 32), :]


def lon_partial(field, lat_test_t, time_test):
    hours, lons, lats = field.shape
    rank = lat_test_t.shape[0]
    out = jax.ShapeDtypeStruct((8, 32, rank), F32)
    return pl.pallas_call(
        lon_kernel,
        in_specs=in_hbm(1) + in_vmem(2),
        out_specs=in_vmem(2),
        out_shape=[out, out],
        scratch_shapes=field_scratch(hours, lons, lats)
        + [pltpu.VMEM((lats, rank), F32), pltpu.VMEM((lons, rank), F32)],
        compiler_params=pltpu.CompilerParams(vmem_limit_bytes=VMEM),
        cost_estimate=pl.CostEstimate(flops=12 * 10**9, bytes_accessed=22 << 20, transcendentals=0),
        name="lon_partial",
    )(field, lat_test_t, time_test)


def finish_kernel(parts_ref, time_ref, core_ref, lat_ref, time_out_ref, columns):
    total = parts_ref[0, :48]
    for source in range(1, parts_ref.shape[0]):
        total = total + parts_ref[source, :48]
    modes = [jnp.concatenate([total[q * 6 : q * 6 + 6], jnp.zeros((2, 128), F32)], axis=0) for q in range(8)]
    modes = jnp.concatenate(modes, axis=1)
    rows = jnp.concatenate([modes[:, a * 80 : a * 80 + 80] for a in range(12)], axis=0)
    result = lax.dot_general(
        rows,
        time_ref[...],
        (((1,), (0,)), ((), ())),
        precision=lax.Precision.HIGHEST,
        preferred_element_type=F32,
    )
    for a in range(12):
        core_ref[a] = result[a * 8 : a * 8 + 6]
    for slot, chip in enumerate(SLOTS):
        if chip < 50:
            lat_ref[chip * 4 : chip * 4 + 4] = parts_ref[slot, 48:52]
            columns[chip * 4 : chip * 4 + 4] = parts_ref[slot, 52:]
    time_out_ref[...] = columns[...].T[:80]


def finish(parts, time_core_t):
    return pl.pallas_call(
        finish_kernel,
        out_shape=[
            jax.ShapeDtypeStruct((12, 6, 96), F32),
            jax.ShapeDtypeStruct((200, 128), F32),
            jax.ShapeDtypeStruct((80, 200), F32),
        ],
        scratch_shapes=[pltpu.VMEM((200, 128), F32)],
        compiler_params=pltpu.CompilerParams(vmem_limit_bytes=VMEM),
        cost_estimate=pl.CostEstimate(flops=10**8, bytes_accessed=2 << 20, transcendentals=0),
        name="finish",
    )(parts, time_core_t)


def places(move):
    pairs = []
    for source in range(128):
        lon, lat = divmod(source, 16)
        x, y, z, core = (lon % 2) * 2 + lat // 8, lon // 2, lat // 2 % 4, lat % 2
        x, y, z, core = move(x, y, z, core)
        pairs.append((source, (y * 2 + x // 2) * 16 + x % 2 * 8 + z * 2 + core))
    return pairs


OTHER_CORE = places(lambda x, y, z, core: (x, y, z, 1 - core))
CHIPS = [[lon * 16 + 2 * at + core for lon in range(8) for at in range(8)] for core in (0, 1)]
MIXED = [[chips[chip] for chip in SLOTS] for chips in CHIPS]


def on_device(field, lon_test, lat_test, time_test, lon_core, lat_core, time_core):
    send, keep, sums = first_partials(field, lon_core, lon_test.T, lat_test.T, time_test, lat_core)
    other = lax.ppermute(send, BOTH, OTHER_CORE)

    shares = lax.all_to_all(sums, BOTH, 0, 0, axis_index_groups=CHIPS)
    by_lat = jnp.sum(shares.reshape(8, 8, 8, 128), axis=0)
    by_hour = jnp.sum(by_lat, axis=0)
    by_hour = by_hour + lax.ppermute(by_hour, BOTH, OTHER_CORE)
    is_lat = lax.broadcasted_iota(jnp.int32, (8, 8, 128), 1) < 4
    sums = jnp.where(is_lat, by_lat, by_hour)

    chip = join_shares(keep.reshape(64, 48, 128), other.reshape(64, 48, 128), sums)
    parts = lax.all_to_all(chip, BOTH, 0, 0, axis_index_groups=MIXED)

    field, _ = lax.optimization_barrier((field, chip))
    keep, send = lon_partial(field, lat_test.T, time_test)
    shares = keep + lax.ppermute(send, BOTH, OTHER_CORE)
    sketch_lon = shares[0]
    for at in range(1, 8):
        pairs = places(lambda x, y, z, core: (x ^ (at // 4), y, (z + at) % 4, core))
        sketch_lon = sketch_lon + lax.ppermute(shares[at], BOTH, pairs)

    core_sketch, sketch_lat, sketch_time = finish(parts, time_core.T)
    return (sketch_lon, sketch_lat.T, sketch_time, core_sketch.transpose(2, 0, 1))


def solution(mesh):
    return jax.shard_map(
        on_device,
        mesh=mesh,
        in_specs=(
            P(None, "lon", "lat"),
            P("lon", None),
            P("lat", None),
            P(),
            P(None, "lon"),
            P(None, "lat"),
            P(),
        ),
        out_specs=(P(("lon", "lat"), None), P("lat", None), P(), P(None, "lon", "lat")),
        check_vma=False,
    )
```

time: 448 us -> 92.1 us (0.21)
  matrix products: 191 us -> 0 us
  waiting for transfers between devices: 163 us -> 7.17 us
  blocking collectives: 66.3 us -> 22.7 us
  Pallas kernels: 0 us -> 37.9 us
  starting transfers between devices: 0.16 us -> 20.6 us
  between operations: 14.7 us -> 0.77 us
  local copies, waits for them, and re-layouts: 11.2 us -> 1.21 us
    dot_general x7 -> x0, matrix products: 191 us -> none  [the longest x1 53.1 us: on_device(): hour_part = jnp.einsum('tik,ik->tk', mixed, lon_test, precision=highest)]
    reduce_scatter x2 -> x0, waiting for transfers between devices: 151 us -> none  [the longest x1 90 us: sum_core(): lax.psum_scatter(partial_value, 'lon', scatter_dimension=1, tiled=True)]
    psum x1 -> x0, blocking collectives: 66.3 us -> none  [on_device(): sketch_time = lax.psum(hour_part, ('lon', 'lat'))]
    pallas_call x0 -> x4, Pallas kernels: none -> 37.9 us  [the longest x1 21.5 us: first_partials(): pl.pallas_call(first_kernel, in_specs=in_hbm(6), out_specs=in_hbm(2) + in...]
    all_to_all x0 -> x1, blocking collectives: none -> 22.7 us  [on_device(): shares = lax.all_to_all(sums, BOTH, 0, 0, axis_index_groups=CHIPS)]
    ppermute x0 -> x10, starting transfers between devices: none -> 13.1 us  [the longest x7 12.9 us: on_device(): sketch_lon = sketch_lon + lax.ppermute(shares[at], BOTH, pairs)]
    psum x1 -> x0, waiting for transfers between devices: 11.8 us -> none  [on_device(): sketch_lat = lax.psum(lat_part, 'lon')]
    all_to_all x0 -> x1, starting transfers between devices: none -> 7.47 us  [on_device(): parts = lax.all_to_all(chip, BOTH, 0, 0, axis_index_groups=MIXED)]
  transfers between devices with their start and end apart: 4 -> 11, of which waited for: 3 -> 5; matrix products, arithmetic and copies ran while one was open for 29% -> 2% of each run, Pallas kernels for 0% -> 13%
where the time goes in v2:
time: 92.1 us; the launch traced here: 91.8 us
  Pallas kernels  37.9 us (41%)
  blocking collectives  22.7 us (25%)
  starting transfers between devices  20.6 us (22%)
  waiting for transfers between devices  7.17 us (8%)
  other arithmetic  1.46 us (2%)
  local copies, waits for them, and re-layouts  1.21 us (1%)
    all_to_all x1, blocking collectives, on_device(): shares = lax.all_to_all(sums, BOTH, 0, 0, axis_index_groups=CHIPS)  22.7 us
    pallas_call x1, Pallas kernels, first_partials(): pl.pallas_call(first_kernel, in_specs=in_hbm(6), out_specs=in_hbm(2) + in...  21.5 us
    ppermute x7, starting transfers between devices, on_device(): sketch_lon = sketch_lon + lax.ppermute(shares[at], BOTH, pairs)  12.9 us
    pallas_call x1, Pallas kernels, lon_partial(): pl.pallas_call(lon_kernel, in_specs=in_hbm(1) + in_vmem(2), out_specs=in_...  12.2 us
    all_to_all x1, starting transfers between devices, on_device(): parts = lax.all_to_all(chip, BOTH, 0, 0, axis_index_groups=MIXED)  7.47 us
    ppermute x7, waiting for transfers between devices, on_device(): sketch_lon = sketch_lon + lax.ppermute(shares[at], BOTH, pairs)  4.53 us
    pallas_call x1, Pallas kernels, join_shares(): pl.pallas_call(join_kernel, in_specs=[pl.BlockSpec(memory_space=pl.ANY)]...  3.27 us
  transfers between devices with their start and end apart: 11, of which 5 were waited for; matrix products, arithmetic and copies ran while one was open for 2% of the time, Pallas kernels for 13%

profile of v2, /device:TPU:0, one launch (start us, length us, event | category | flops | bytes accessed | tf_op | source)
XLA Modules:
  0.0 91.8 jit_solution(17116556668516376038)
XLA Ops:
  0.6 21.5 %first_partials.1 = (f32[8,8,48,128]{3,2,1,0:T(8,128)}, f32[8,8,48,128]{3,2,1,0:T(8,128)}, f32[64,8,128]{2,1,0:T(8,128)}) custom-call(f32[80,512,128]{2,1,0:T(8,128)} %field_hbm.2, f32[96,512]{1,0:T(8,128)} %lon_core_hbm.1, f32[200,512]{1,0:T(8,128)} %bitcast.44, f32[200,128]{1,0:T(8,128)} %bitcast.39, f32[80,200]{1,0:T(8,128)} %time_ref.1, ...), custom_call_target="tpu_custom_call" | custom-call | flops 20000000000 | bytes 29360128 | tf_op jit(solution)/shard_map/first_partials/pallas_call | solution.py:161
  22.1 0.1 collective-permute-start
  22.2 22.7 %all_to_all.10 = f32[64,8,128]{2,1,0:T(8,128)S(1)} all-to-all(f32[64,8,128]{2,1,0:T(8,128)} %get-tuple-element.15), channel_id=1, replica_groups={{0,2,4,6,8,10,12,14,16,18,20,22,24,26,28,30,32,34,36,38,40,42,44,46,48,..., dimensions={0} | all-to-all | bytes 524288 | tf_op jit(solution)/shard_map/all_to_all | solution.py:322
  44.9 0.1 reduce_sum.19
  45.0 0.1 collective-permute-start.1
  45.1 1.1 %collective-permute-done.1 = f32[8,128]{1,0:T(8,128)S(1)} collective-permute-done((f32[8,128]{1,0:T(8,128)S(1)}, f32[8,128]{1,0:T(8,128)S(1)}, u32[]{:S(2)}, u32[]{:S(2)}) %collective-permute-start.1) | collective-permute-done | bytes 4128 | tf_op jit(solution)/shard_map/ppermute | solution.py:325
  46.2 0.7 broadcast_select_fusion.sums_hbm
  46.9 1.2 %copy-done.3 = f32[8,8,48,128]{3,2,1,0:T(8,128)} copy-done((f32[8,8,48,128]{3,2,1,0:T(8,128)}, f32[8,8,48,128]{3,2,1,0:T(8,128)S(1)}, u32[]{:S(2)}) %copy-start.3) | copy-done | bytes 1572888
  48.1 3.3 %join_shares.1 = f32[64,56,128]{2,1,0:T(8,128)} custom-call(f32[64,48,128]{2,1,0:T(8,128)} %bitcast.42, f32[64,48,128]{2,1,0:T(8,128)} %bitcast.43, f32[8,8,128]{2,1,0:T(8,128)} %broadcast_select_fusion.sums_hbm), custom_call_target="tpu_custom_call" | custom-call | flops 1000000 | bytes 5242880 | tf_op jit(solution)/shard_map/join_shares/pallas_call | solution.py:208
  51.4 7.5 %all-to-all-start.1 = ((f32[64,56,128]{2,1,0:T(8,128)}), f32[64,56,128]{2,1,0:T(8,128)S(1)}, u32[]{:S(2)}, u32[]{:S(2)}) async-start(f32[64,56,128]{2,1,0:T(8,128)} %join_shares.1), calls=%async_computation.1 | async-start | bytes 3670016 | tf_op jit(solution)/shard_map/all_to_all | solution.py:330
  58.9 12.2 %lon_partial.1 = (f32[8,32,200]{2,1,0:T(8,128)S(1)}, f32[8,32,200]{2,1,0:T(8,128)S(1)}) custom-call(f32[80,512,128]{2,1,0:T(8,128)} %field_hbm.2, f32[200,128]{1,0:T(8,128)S(1)} %bitcast.40, f32[80,200]{1,0:T(8,128)S(1)} %copy-done.2), custom_call_target="tpu_custom_call" | custom-call | flops 12000000000 | bytes 23068672 | tf_op jit(solution)/shard_map/lon_partial/pallas_call | solution.py:252
  71.1 0.1 collective-permute-start.2
  71.2 1.5 %collective-permute-done.2 = f32[8,32,200]{2,1,0:T(8,128)S(1)} collective-permute-done((f32[8,32,200]{2,1,0:T(8,128)S(1)}, f32[8,32,200]{2,1,0:T(8,128)S(1)}, u32[]{:S(2)}, u32[]{:S(2)}) %collective-permute-start.2) | collective-permute-done | bytes 204832 | tf_op jit(solution)/shard_map/ppermute | solution.py:334
  72.8 0.1 collective-permute-start.3
  72.9 3.3 %collective-permute-start.9 = (f32[32,200]{1,0:T(8,128)S(1)}, f32[32,200]{1,0:T(8,128)S(1)}, u32[]{:S(2)}, u32[]{:S(2)}) collective-permute-start(f32[32,200]{1,0:T(8,128)S(1)} %get-tuple-element.23), channel_id=1, source_target_pairs={{0,14},{1,15},{2,8},{3,9},{4,10},{5,11},{6,12},{7,13},{8,6},{9,7},... | collective-permute-start | bytes 76808 | tf_op jit(solution)/shard_map/ppermute | solution.py:338
  76.2 1.6 %collective-permute-start.7 = (f32[32,200]{1,0:T(8,128)S(1)}, f32[32,200]{1,0:T(8,128)S(1)}, u32[]{:S(2)}, u32[]{:S(2)}) collective-permute-start(f32[32,200]{1,0:T(8,128)S(1)} %get-tuple-element.25), channel_id=1, source_target_pairs={{0,10},{1,11},{2,12},{3,13},{4,14},{5,15},{6,8},{7,9},{8,2},{9,3},... | collective-permute-start | bytes 76808 | tf_op jit(solution)/shard_map/ppermute | solution.py:338
  77.8 0.7 collective-permute-start.6
  78.5 0.6 collective-permute-done.3
  79.1 5.6 %collective-permute-start.5 = (f32[32,200]{1,0:T(8,128)S(1)}, f32[32,200]{1,0:T(8,128)S(1)}, u32[]{:S(2)}, u32[]{:S(2)}) collective-permute-start(f32[32,200]{1,0:T(8,128)S(1)} %get-tuple-element.27), channel_id=1, source_target_pairs={{0,6},{1,7},{2,0},{3,1},{4,2},{5,3},{6,4},{7,5},{8,14},{9,15},{10,... | collective-permute-start | bytes 76808 | tf_op jit(solution)/shard_map/ppermute | solution.py:338
  84.8 1.5 %collective-permute-start.4 = (f32[32,200]{1,0:T(8,128)S(1)}, f32[32,200]{1,0:T(8,128)S(1)}, u32[]{:S(2)}, u32[]{:S(2)}) collective-permute-start(f32[32,200]{1,0:T(8,128)S(1)} %get-tuple-element.28), channel_id=1, source_target_pairs={{0,4},{1,5},{2,6},{3,7},{4,0},{5,1},{6,2},{7,3},{8,12},{9,13},{10,... | collective-permute-start | bytes 76808 | tf_op jit(solution)/shard_map/ppermute | solution.py:338
  86.3 0.1 collective-permute-done.5
  86.4 3.8 %collective-permute-done.4 = f32[32,200]{1,0:T(8,128)S(1)} collective-permute-done((f32[32,200]{1,0:T(8,128)S(1)}, f32[32,200]{1,0:T(8,128)S(1)}, u32[]{:S(2)}, u32[]{:S(2)}) %collective-permute-start.4) | collective-permute-done | bytes 25632 | tf_op jit(solution)/shard_map/ppermute | solution.py:338
  90.2 0.6 fusion.6
  90.8 1.0 %finish.1 = (f32[12,6,96]{2,1,0:T(8,128)}, f32[200,128]{1,0:T(8,128)}, f32[80,200]{1,0:T(8,128)}) custom-call(f32[64,56,128]{2,1,0:T(8,128)S(1)} %all-to-all-done.1.parts_ref, f32[80,96]{1,0:T(8,128)S(1)} %bitcast.38), custom_call_target="tpu_custom_call" | custom-call | flops 100000000 | bytes 2097152 | tf_op jit(solution)/shard_map/finish/pallas_call | solution.py:289
  (19 shorter events, 0.1 us)
Async XLA Ops:
  22.1 24.8 %collective-permute-start = (f32[8,8,48,128]{3,2,1,0:T(8,128)}, f32[8,8,48,128]{3,2,1,0:T(8,128)S(1)}, u32[]{:S(2)}, u32[]{:S(2)}) collective-permute-start(f32[8,8,48,128]{3,2,1,0:T(8,128)} %get-tuple-element.14), channel_id=1, source_target_pairs={{0,1},{1,0},{2,3},{3,2},{4,5},{5,4},{6,7},{7,6},{8,9},{9,8},{10,11... | collective-permute-start | bytes 4718600 | tf_op jit(solution)/shard_map/ppermute | solution.py:320
  45.0 1.2 %collective-permute-start.1 = (f32[8,128]{1,0:T(8,128)S(1)}, f32[8,128]{1,0:T(8,128)S(1)}, u32[]{:S(2)}, u32[]{:S(2)}) collective-permute-start(f32[8,128]{1,0:T(8,128)S(1)} %reduce_sum.19), channel_id=1, source_target_pairs={{0,1},{1,0},{2,3},{3,2},{4,5},{5,4},{6,7},{7,6},{8,9},{9,8},{10,11... | collective-permute-start | bytes 12296 | tf_op jit(solution)/shard_map/ppermute | solution.py:325
  46.9 1.2 %copy-start.3 = (f32[8,8,48,128]{3,2,1,0:T(8,128)}, f32[8,8,48,128]{3,2,1,0:T(8,128)S(1)}, u32[]{:S(2)}) copy-start(f32[8,8,48,128]{3,2,1,0:T(8,128)S(1)} %collective-permute-done) | copy-start | bytes 4718596
  51.4 7.5 %copy-start.1 = (f32[128,200]{0,1:T(8,128)S(1)}, f32[128,200]{0,1:T(8,128)}, u32[]{:S(2)}) copy-start(f32[128,200]{0,1:T(8,128)} %param.9) | copy-start | bytes 307204
  51.4 7.5 %copy-start.2 = (f32[80,200]{1,0:T(8,128)S(1)}, f32[80,200]{1,0:T(8,128)}, u32[]{:S(2)}) copy-start(f32[80,200]{1,0:T(8,128)} %time_ref.1) | copy-start | bytes 192004
  51.4 39.4 %all-to-all-start.1 = ((f32[64,56,128]{2,1,0:T(8,128)}), f32[64,56,128]{2,1,0:T(8,128)S(1)}, u32[]{:S(2)}, u32[]{:S(2)}) async-start(f32[64,56,128]{2,1,0:T(8,128)} %join_shares.1), calls=%async_computation.1 | async-start | bytes 3670016 | tf_op jit(solution)/shard_map/all_to_all | solution.py:330
  58.9 31.9 %copy-start = (f32[96,80]{0,1:T(8,128)S(1)}, f32[96,80]{0,1:T(8,128)}, u32[]{:S(2)}) copy-start(f32[96,80]{0,1:T(8,128)} %param.13) | copy-start | bytes 92164
  71.1 1.6 %collective-permute-start.2 = (f32[8,32,200]{2,1,0:T(8,128)S(1)}, f32[8,32,200]{2,1,0:T(8,128)S(1)}, u32[]{:S(2)}, u32[]{:S(2)}) collective-permute-start(f32[8,32,200]{2,1,0:T(8,128)S(1)} %get-tuple-element.18), channel_id=1, source_target_pairs={{0,1},{1,0},{2,3},{3,2},{4,5},{5,4},{6,7},{7,6},{8,9},{9,8},{10,11... | collective-permute-start | bytes 614408 | tf_op jit(solution)/shard_map/ppermute | solution.py:334
  72.8 6.3 %collective-permute-start.3 = (f32[32,200]{1,0:T(8,128)S(1)}, f32[32,200]{1,0:T(8,128)S(1)}, u32[]{:S(2)}, u32[]{:S(2)}) collective-permute-start(f32[32,200]{1,0:T(8,128)S(1)} %get-tuple-element.22), channel_id=1, source_target_pairs={{0,2},{1,3},{2,4},{3,5},{4,6},{5,7},{6,0},{7,1},{8,10},{9,11},{10,... | collective-permute-start | bytes 76808 | tf_op jit(solution)/shard_map/ppermute | solution.py:338
  72.9 11.9 %collective-permute-start.9 = (f32[32,200]{1,0:T(8,128)S(1)}, f32[32,200]{1,0:T(8,128)S(1)}, u32[]{:S(2)}, u32[]{:S(2)}) collective-permute-start(f32[32,200]{1,0:T(8,128)S(1)} %get-tuple-element.23), channel_id=1, source_target_pairs={{0,14},{1,15},{2,8},{3,9},{4,10},{5,11},{6,12},{7,13},{8,6},{9,7},... | collective-permute-start | bytes 76808 | tf_op jit(solution)/shard_map/ppermute | solution.py:338
  76.2 10.1 %collective-permute-start.8 = (f32[32,200]{1,0:T(8,128)S(1)}, f32[32,200]{1,0:T(8,128)S(1)}, u32[]{:S(2)}, u32[]{:S(2)}) collective-permute-start(f32[32,200]{1,0:T(8,128)S(1)} %get-tuple-element.24), channel_id=1, source_target_pairs={{0,12},{1,13},{2,14},{3,15},{4,8},{5,9},{6,10},{7,11},{8,4},{9,5},... | collective-permute-start | bytes 76808 | tf_op jit(solution)/shard_map/ppermute | solution.py:338
  76.2 10.1 %collective-permute-start.7 = (f32[32,200]{1,0:T(8,128)S(1)}, f32[32,200]{1,0:T(8,128)S(1)}, u32[]{:S(2)}, u32[]{:S(2)}) collective-permute-start(f32[32,200]{1,0:T(8,128)S(1)} %get-tuple-element.25), channel_id=1, source_target_pairs={{0,10},{1,11},{2,12},{3,13},{4,14},{5,15},{6,8},{7,9},{8,2},{9,3},... | collective-permute-start | bytes 76808 | tf_op jit(solution)/shard_map/ppermute | solution.py:338
  77.8 8.4 %collective-permute-start.6 = (f32[32,200]{1,0:T(8,128)S(1)}, f32[32,200]{1,0:T(8,128)S(1)}, u32[]{:S(2)}, u32[]{:S(2)}) collective-permute-start(f32[32,200]{1,0:T(8,128)S(1)} %get-tuple-element.26), channel_id=1, source_target_pairs={{0,8},{1,9},{2,10},{3,11},{4,12},{5,13},{6,14},{7,15},{8,0},{9,1},... | collective-permute-start | bytes 76808 | tf_op jit(solution)/shard_map/ppermute | solution.py:338
  79.1 7.2 %collective-permute-start.5 = (f32[32,200]{1,0:T(8,128)S(1)}, f32[32,200]{1,0:T(8,128)S(1)}, u32[]{:S(2)}, u32[]{:S(2)}) collective-permute-start(f32[32,200]{1,0:T(8,128)S(1)} %get-tuple-element.27), channel_id=1, source_target_pairs={{0,6},{1,7},{2,0},{3,1},{4,2},{5,3},{6,4},{7,5},{8,14},{9,15},{10,... | collective-permute-start | bytes 76808 | tf_op jit(solution)/shard_map/ppermute | solution.py:338
  84.8 5.4 %collective-permute-start.4 = (f32[32,200]{1,0:T(8,128)S(1)}, f32[32,200]{1,0:T(8,128)S(1)}, u32[]{:S(2)}, u32[]{:S(2)}) collective-permute-start(f32[32,200]{1,0:T(8,128)S(1)} %get-tuple-element.28), channel_id=1, source_target_pairs={{0,4},{1,5},{2,6},{3,7},{4,0},{5,1},{6,2},{7,3},{8,12},{9,13},{10,... | collective-permute-start | bytes 76808 | tf_op jit(solution)/shard_map/ppermute | solution.py:338

commit v3 on v2

v3 whole, which is shorter than its diff:
```python
import jax
import jax.numpy as jnp
from jax import lax
from jax.experimental import pallas as pl
from jax.experimental.pallas import tpu as pltpu
from jax.sharding import PartitionSpec as P

F32 = jnp.float32
BF16 = jnp.bfloat16
BOTH = ("lon", "lat")
HOURS = 8
VMEM = 48 * 1024 * 1024
MOST_VMEM = 62 * 1024 * 1024
MUCH_VMEM = 40 * 1024 * 1024
SLOTS = sorted(range(64), key=lambda chip: (chip % 4, chip // 16, chip // 8 % 2 * 2 + chip // 4 % 2))


def halves(value):
    top = value.astype(BF16)
    return top, (value - top.astype(F32)).astype(BF16)


def dot(left, right, dims=((1,), (0,))):
    return lax.dot_general(left, right, (dims, ((), ())), preferred_element_type=F32)


def stacked_dot(weights, rows, right_top, right_low):
    upper = dot(weights[...], right_top)
    return upper[:rows] + upper[rows:] + dot(weights[:rows], right_low)


def block_copy(field_hbm, field, arrived, at):
    part = pl.ds(at * HOURS, HOURS)
    return pltpu.make_async_copy(field_hbm.at[part], field.at[part], arrived.at[at])


def start_field(field_hbm, field, arrived, blocks):
    for at in blocks:
        block_copy(field_hbm, field, arrived, at).start()


def each_block(field_hbm, field, arrived, work):
    def step(at, carry):
        block_copy(field_hbm, field, arrived, at).wait()
        work(at)
        return carry

    lax.fori_loop(0, arrived.shape[0], step, 0)


def field_scratch(hours, lons, lats):
    return [pltpu.VMEM((hours, lons, lats), F32), pltpu.SemaphoreType.DMA((hours // HOURS,))]


def copies_in(sources, targets, arrived):
    copies = [pltpu.make_async_copy(a, b, arrived.at[i]) for i, (a, b) in enumerate(zip(sources, targets))]
    for copy in copies:
        copy.start()
    return copies


def in_vmem(count):
    return [pl.BlockSpec(memory_space=pltpu.VMEM)] * count


def in_hbm(count):
    return [pl.BlockSpec(memory_space=pltpu.HBM)] * count


def split_rows(values, weights):
    rows = values.shape[0]
    top, low = halves(values)
    weights[:rows] = top
    weights[rows:] = low


def products(weights, top, low):
    both = stacked_dot(weights, weights.shape[0] // 2, top, low)
    return both[:, :128], both[:, 128:]


def sketch_kernel(
    field_hbm, lon_hbm, lat_hbm, time_hbm, sums_ref,
    field, arrived, lon_test, lat_test_t, time_test, small, weights, lat_test, lat_sum, hour_sum, lon_sum,
):
    rank, lons = lon_test.shape
    lane = lax.broadcasted_iota(jnp.int32, (rank, 128), 1)
    waits = copies_in((lon_hbm, lat_hbm, time_hbm), (lon_test, lat_test_t, time_test), small)
    start_field(field_hbm, field, arrived, range(1))
    for total in (lat_sum, hour_sum, lon_sum):
        total[...] = jnp.zeros_like(total)
    for copy in waits:
        copy.wait()
    start_field(field_hbm, field, arrived, range(1, arrived.shape[0]))
    split_rows(lon_test[...], weights)
    lat_test[...] = lat_test_t[...].T

    def work(at):
        times = time_test[pl.ds(at * HOURS, HOURS), :]
        times_t = times.T
        lat_total, hour_total = lat_sum[...], hour_sum[...]
        values = [halves(field[at * HOURS + hour]) for hour in range(HOURS)]

        for pair in range(0, HOURS, 2):
            top, low = (jnp.concatenate([values[pair][i], values[pair + 1][i]], axis=1) for i in range(2))
            for hour, across in enumerate(products(weights, top, low), pair):
                lat_total = lat_total + across * times_t[:, hour : hour + 1]
                total = jnp.sum(across * lat_test_t[...], axis=1, keepdims=True)
                hour_total = jnp.where(lane == at * HOURS + hour, total, hour_total)
        lat_sum[...] = lat_total
        hour_sum[...] = hour_total

        tests = [lat_test[...] * times[hour : hour + 1, :] for hour in range(HOURS)]
        test_top, test_low = halves(jnp.concatenate(tests, axis=0))
        top = jnp.concatenate([value[0] for value in values], axis=1)
        low = jnp.concatenate([value[1] for value in values], axis=1)
        upper = dot(jnp.concatenate([top, low], axis=0), test_top)
        lon_sum[...] += upper[:lons] + upper[lons:] + dot(top, test_low)

    each_block(field_hbm, field, arrived, work)
    lon_t = lon_sum[...].T
    for place in range(rank // 2):
        columns = slice(place * 2, place * 2 + 2)
        sums_ref[place, 0, :2] = lat_sum[columns]
        sums_ref[place, 0, 2:] = hour_sum[columns]
        for part in range(4):
            row = part % 2 * 2
            sums_ref[place, 1 + part // 2, row : row + 2] = lon_t[columns, part * 128 : part * 128 + 128]
    sums_ref[rank // 2 :] = jnp.zeros((128 - rank // 2, 3, 4, 128), F32)


def sketch_partials(field, lon_test_t, lat_test_t, time_test):
    hours, lons, lats = field.shape
    rank = lon_test_t.shape[0]
    return pl.pallas_call(
        sketch_kernel,
        in_specs=in_hbm(4),
        out_specs=pl.BlockSpec(memory_space=pltpu.VMEM),
        out_shape=jax.ShapeDtypeStruct((128, 3, 4, 128), F32),
        scratch_shapes=field_scratch(hours, lons, lats)
        + [pltpu.VMEM(x.shape, F32) for x in (lon_test_t, lat_test_t, time_test)]
        + [
            pltpu.SemaphoreType.DMA((3,)),
            pltpu.VMEM((2 * rank, lons), BF16),
            pltpu.VMEM((lats, rank), F32),
            pltpu.VMEM((rank, 128), F32),
            pltpu.VMEM((rank, 128), F32),
            pltpu.VMEM((lons, rank), F32),
        ],
        compiler_params=pltpu.CompilerParams(vmem_limit_bytes=MOST_VMEM),
        cost_estimate=pl.CostEstimate(flops=24 * 10**9, bytes_accessed=22 << 20, transcendentals=0),
        name="sketch_partials",
    )(field, lon_test_t, lat_test_t, time_test)


def sum_kernel(shares_ref, keep_ref, send_ref):
    core = lax.axis_index("lat") % 2
    mine = lax.broadcasted_iota(jnp.int32, (4, 128), 0) // 2 == core

    def spread(rows):
        return jnp.where(mine, jnp.concatenate([rows, rows], axis=0), 0.0)

    hour = jnp.zeros((4, 128), F32)
    for at in range(8):
        lats = []
        for lat in (at * 2, at * 2 + 1):
            total = shares_ref[lat, 0]
            for lon in range(1, 8):
                total = total + shares_ref[lon * 16 + lat, 0]
            hour = hour + total
            lats.append(spread(total[:2]))
        tile, row = 17 + at // 2, at % 2 * 4
        keep_ref[tile, row : row + 4] = jnp.where(core == 0, lats[0], lats[1])
        send_ref[tile, row : row + 4] = jnp.where(core == 0, lats[1], lats[0])
    hour = spread(hour[2:])
    for out in (keep_ref, send_ref):
        out[16, :4] = hour
        out[16, 4:] = hour
    for lon in range(8):
        for half in range(2):
            total = shares_ref[lon * 16, 1 + half]
            for lat in range(1, 16):
                total = total + shares_ref[lon * 16 + lat, 1 + half]
            for out in (keep_ref, send_ref):
                out[lon * 2 + half, :4] = spread(total[:2])
                out[lon * 2 + half, 4:] = spread(total[2:])


def sum_shares(shares):
    return pl.pallas_call(
        sum_kernel,
        out_shape=[jax.ShapeDtypeStruct((21, 8, 128), F32)] * 2,
        compiler_params=pltpu.CompilerParams(vmem_limit_bytes=MUCH_VMEM),
        cost_estimate=pl.CostEstimate(flops=10**6, bytes_accessed=1 << 20, transcendentals=0),
        name="sum_shares",
    )(shares)


def core_kernel(
    field_hbm, lon_core, lat_core, send_ref, keep_ref, field, arrived, weights, crossed
):
    start_field(field_hbm, field, arrived, range(arrived.shape[0]))
    split_rows(lon_core[...], weights)

    def work(at):
        for pair in range(0, HOURS, 2):
            first = at * HOURS + pair
            top, low = halves(jnp.concatenate([field[first], field[first + 1]], axis=1))
            for hour, result in enumerate(products(weights, top, low), pair):
                crossed[:, at, hour, :] = result

    each_block(field_hbm, field, arrived, work)

    core = lax.axis_index("lat") % 2
    of_core = [
        jnp.concatenate([lat_core[pl.ds(at * 6 + b, 8, stride=12), :] for b in range(6)], axis=0) for at in range(2)
    ]
    lat_rows = jnp.concatenate(
        [jnp.where(core == 0, of_core[0], of_core[1]), jnp.where(core == 0, of_core[1], of_core[0])], axis=0
    )
    lat_top, lat_low = halves(lat_rows)
    lats = jnp.concatenate(
        [jnp.concatenate([lat_top, lat_top], axis=1), jnp.concatenate([lat_low, jnp.zeros_like(lat_low)], axis=1)],
        axis=0,
    )

    def share(owner, carry):
        block = crossed[pl.ds(owner * 12, 12)].reshape(960, 128)
        block = jnp.concatenate([block, jnp.zeros((64, 128), F32)], axis=0)
        result = dot(lats, jnp.concatenate(halves(block), axis=1), ((1,), (1,)))
        result = result[:96] + result[96:]
        for part, out in enumerate((keep_ref, send_ref)):
            for b in range(6):
                row = part * 48 + b * 8
                for q in range(8):
                    out[owner, :, q * 6 + b, :] = result[row : row + 8, q * 128 : q * 128 + 128]
        return carry

    lax.fori_loop(0, 8, share, 0)


def core_partials(field, lon_core, lat_core):
    hours, lons, lats = field.shape
    modes = lon_core.shape[0]
    part = jax.ShapeDtypeStruct((8, 8, 48, 128), F32)
    return pl.pallas_call(
        core_kernel,
        in_specs=in_hbm(1) + in_vmem(2),
        out_specs=in_vmem(2),
        out_shape=[part, part],
        scratch_shapes=field_scratch(hours, lons, lats)
        + [
            pltpu.VMEM((2 * modes, lons), BF16),
            pltpu.VMEM((modes, hours // HOURS, HOURS, lats), F32),
        ],
        compiler_params=pltpu.CompilerParams(vmem_limit_bytes=MUCH_VMEM),
        cost_estimate=pl.CostEstimate(flops=30 * 10**9, bytes_accessed=28 << 20, transcendentals=0),
        name="core_partials",
    )(field, lon_core, lat_core)


def join_kernel(keep_ref, arrived_ref, mine_ref, other_ref, out_ref, rolled, lats):
    core = lax.axis_index("lat") % 2
    rest = (mine_ref[...] + other_ref[...]).reshape(21 * 8, 128)
    hour = rest[16 * 8 : 16 * 8 + 4]
    lats[...] = rest[17 * 8 :]
    for odd in range(2):
        rolled[odd] = jnp.where(core == 0, *[pltpu.roll(rest[:128], (96 - 64 * odd - 32 * c) % 128, 1) for c in range(2)])
    lane = lax.broadcasted_iota(jnp.int32, (4, 128), 1)
    for slot, chip in enumerate(SLOTS):
        lon, lat = divmod(chip, 8)
        out_ref[slot, :48] = keep_ref[chip] + arrived_ref[chip]
        out_ref[slot, 48:52] = lats[lat * 4 : lat * 4 + 4]
        row = lon * 16 + lat // 2 * 4
        out_ref[slot, 52:] = jnp.where(lane < 96, hour, rolled[lat % 2, row : row + 4])


def join_shares(keep, arrived, mine, other):
    shape = (64, 56, 128)
    return pl.pallas_call(
        join_kernel,
        in_specs=in_vmem(4),
        out_specs=pl.BlockSpec(memory_space=pltpu.VMEM),
        out_shape=jax.ShapeDtypeStruct(shape, F32),
        scratch_shapes=[pltpu.VMEM((2, 128, 128), F32), pltpu.VMEM((32, 128), F32)],
        compiler_params=pltpu.CompilerParams(vmem_limit_bytes=MUCH_VMEM),
        cost_estimate=pl.CostEstimate(flops=10**6, bytes_accessed=5 << 20, transcendentals=0),
        name="join_shares",
    )(keep, arrived, mine, other)


def finish_kernel(parts_ref, time_ref, core_ref, lat_ref, hour_ref, lon_ref, columns):
    total = parts_ref[0, :48]
    for source in range(1, parts_ref.shape[0]):
        total = total + parts_ref[source, :48]
    modes = [jnp.concatenate([total[q * 6 : q * 6 + 6], jnp.zeros((2, 128), F32)], axis=0) for q in range(8)]
    modes = jnp.concatenate(modes, axis=1)
    rows = jnp.concatenate([modes[:, a * 80 : a * 80 + 80] for a in range(12)], axis=0)
    result = lax.dot_general(
        rows,
        time_ref[...],
        (((1,), (0,)), ((), ())),
        precision=lax.Precision.HIGHEST,
        preferred_element_type=F32,
    )
    for a in range(12):
        core_ref[a] = result[a * 8 : a * 8 + 6]
    for slot, chip in enumerate(SLOTS):
        if chip < 50:
            lat_ref[chip * 4 : chip * 4 + 4] = parts_ref[slot, 48:52]
            columns[chip * 4 : chip * 4 + 4] = parts_ref[slot, 52:]
    rows = columns[...].T
    hour_ref[...] = rows[:80]
    lon_ref[...] = rows[96:]


def finish(parts, time_core_t):
    return pl.pallas_call(
        finish_kernel,
        out_shape=[
            jax.ShapeDtypeStruct((12, 6, 96), F32),
            jax.ShapeDtypeStruct((200, 128), F32),
            jax.ShapeDtypeStruct((80, 200), F32),
            jax.ShapeDtypeStruct((32, 200), F32),
        ],
        scratch_shapes=[pltpu.VMEM((200, 128), F32)],
        compiler_params=pltpu.CompilerParams(vmem_limit_bytes=VMEM),
        cost_estimate=pl.CostEstimate(flops=10**8, bytes_accessed=2 << 20, transcendentals=0),
        name="finish",
    )(parts, time_core_t)


def places(move):
    pairs = []
    for source in range(128):
        lon, lat = divmod(source, 16)
        x, y, z, core = (lon % 2) * 2 + lat // 8, lon // 2, lat // 2 % 4, lat % 2
        x, y, z, core = move(x, y, z, core)
        pairs.append((source, (y * 2 + x // 2) * 16 + x % 2 * 8 + z * 2 + core))
    return pairs


OTHER_CORE = places(lambda x, y, z, core: (x, y, z, 1 - core))
CHIPS = [[lon * 16 + 2 * at + core for lon in range(8) for at in range(8)] for core in (0, 1)]
MIXED = [[chips[chip] for chip in SLOTS] for chips in CHIPS]


def on_device(field, lon_test, lat_test, time_test, lon_core, lat_core, time_core):
    sums = sketch_partials(field, lon_test.T, lat_test.T, time_test)

    core_field, sums = lax.optimization_barrier((field, sums))
    shares = lax.all_to_all(sums, BOTH, 0, 0)
    send, keep = core_partials(core_field, lon_core, lat_core)
    shares, send, keep = lax.optimization_barrier((shares, send, keep))
    other = lax.ppermute(send, BOTH, OTHER_CORE)
    mine, others = sum_shares(shares)
    others = lax.ppermute(others, BOTH, OTHER_CORE)

    chip = join_shares(keep.reshape(64, 48, 128), other.reshape(64, 48, 128), mine, others)
    parts = lax.all_to_all(chip, BOTH, 0, 0, axis_index_groups=MIXED)
    core_sketch, sketch_lat, sketch_time, sketch_lon = finish(parts, time_core.T)
    return (sketch_lon, sketch_lat.T, sketch_time, core_sketch.transpose(2, 0, 1))


def solution(mesh):
    return jax.shard_map(
        on_device,
        mesh=mesh,
        in_specs=(
            P(None, "lon", "lat"),
            P("lon", None),
            P("lat", None),
            P(),
            P(None, "lon"),
            P(None, "lat"),
            P(),
        ),
        out_specs=(P(("lon", "lat"), None), P("lat", None), P(), P(None, "lon", "lat")),
        check_vma=False,
    )
```

time: 92.1 us -> 89.2 us (0.969)
  blocking collectives: 22.7 us -> 34.6 us
  starting transfers between devices: 20.6 us -> 11.7 us
  Pallas kernels: 37.9 us -> 34.9 us
  other arithmetic: 1.46 us -> 0 us
  waiting for transfers between devices: 7.17 us -> 5.78 us
    ppermute x9 -> x1, starting transfers between devices: 13 us -> 0.59 us  [on_device(): others = lax.ppermute(others, BOTH, OTHER_CORE)]
    all_to_all x1, blocking collectives: 22.7 us -> 34.6 us  [on_device(): parts = lax.all_to_all(chip, BOTH, 0, 0, axis_index_groups=MIXED)]
    ppermute x9 -> x1, waiting for transfers between devices: 7.16 us -> 2.61 us  [on_device(): others = lax.ppermute(others, BOTH, OTHER_CORE)]
    all_to_all x1, starting transfers between devices: 7.47 us -> 11.1 us  [on_device(): shares = lax.all_to_all(sums, BOTH, 0, 0)]
    pallas_call x3 -> x4, Pallas kernels: 36.9 us -> 33.9 us  [the longest x1 21 us: sketch_partials(): pl.pallas_call(sketch_kernel, in_specs=in_hbm(4), out_specs=pl.BlockSpec(...]
    all_to_all x1, waiting for transfers between devices: 0.01 us -> 2.73 us  [on_device(): shares = lax.all_to_all(sums, BOTH, 0, 0)]
  transfers between devices with their start and end apart: 11 -> 3, of which waited for: 5 -> 3; matrix products, arithmetic and copies ran while one was open for 2% -> 0% of each run, Pallas kernels for 13% -> 14%
where the time goes in v3:
time: 89.2 us; the launch traced here: 88.9 us
  Pallas kernels  34.9 us (39%)
  blocking collectives  34.6 us (39%)
  starting transfers between devices  11.7 us (13%)
  waiting for transfers between devices  5.78 us (6%)
  local copies, waits for them, and re-layouts  1.16 us (1%)
    all_to_all x1, blocking collectives, on_device(): parts = lax.all_to_all(chip, BOTH, 0, 0, axis_index_groups=MIXED)  34.6 us
    pallas_call x1, Pallas kernels, sketch_partials(): pl.pallas_call(sketch_kernel, in_specs=in_hbm(4), out_specs=pl.BlockSpec(...  21 us
    pallas_call x1, Pallas kernels, core_partials(): pl.pallas_call(core_kernel, in_specs=in_hbm(1) + in_vmem(2), out_specs=in...  12.6 us
    all_to_all x1, starting transfers between devices, on_device(): shares = lax.all_to_all(sums, BOTH, 0, 0)  11.1 us
    all_to_all x1, waiting for transfers between devices, on_device(): shares = lax.all_to_all(sums, BOTH, 0, 0)  2.73 us
    ppermute x1, waiting for transfers between devices, on_device(): others = lax.ppermute(others, BOTH, OTHER_CORE)  2.61 us
  transfers between devices with their start and end apart: 3, of which 3 were waited for; matrix products, arithmetic and copies ran while one was open for 0% of the time, Pallas kernels for 14%

profile of v3, /device:TPU:0, one launch (start us, length us, event | category | flops | bytes accessed | tf_op | source)
XLA Modules:
  0.0 88.9 jit_solution(115362732365471520)
XLA Ops:
  0.6 0.0 copy-start.2
  0.6 0.0 copy-start.3
  0.7 21.0 %sketch_partials.1 = f32[128,3,4,128]{3,2,1,0:T(4,128)} custom-call(f32[80,512,128]{2,1,0:T(8,128)} %field_hbm.2, f32[200,512]{1,0:T(8,128)} %bitcast.10, f32[200,128]{1,0:T(8,128)} %bitcast.11, f32[80,200]{1,0:T(8,128)} %time_hbm.1), custom_call_target="tpu_custom_call" | custom-call | flops 24000000000 | bytes 23068672 | tf_op jit(solution)/shard_map/sketch_partials/pallas_call | solution.py:135
  21.6 11.1 %all-to-all-start = ((f32[128,3,4,128]{3,2,1,0:T(4,128)}), f32[128,3,4,128]{3,2,1,0:T(4,128)S(1)}, u32[]{:S(2)}, u32[]{:S(2)}) async-start(f32[128,3,4,128]{3,2,1,0:T(4,128)} %sketch_partials.1), calls=%async_computation | async-start | bytes 1572864 | tf_op jit(solution)/shard_map/all_to_all | solution.py:352
  32.8 0.0 copy-done.2
  32.8 0.0 copy-done.3
  32.8 12.6 %core_partials.1 = (f32[8,8,48,128]{3,2,1,0:T(8,128)S(1)}, f32[8,8,48,128]{3,2,1,0:T(8,128)S(1)}) custom-call(f32[80,512,128]{2,1,0:T(8,128)} %field_hbm.2, f32[96,512]{1,0:T(8,128)S(1)} %copy-done.2, f32[96,128]{1,0:T(8,128)S(1)} %copy-done.3), custom_call_target="tpu_custom_call" | custom-call | flops 30000001024 | bytes 29360128 | tf_op jit(solution)/shard_map/core_partials/pallas_call | solution.py:246
  45.4 0.0 copy-start.1
  45.4 1.1 %copy-done.1 = f32[8,8,48,128]{3,2,1,0:T(8,128)} copy-done((f32[8,8,48,128]{3,2,1,0:T(8,128)}, f32[8,8,48,128]{3,2,1,0:T(8,128)S(1)}, u32[]{:S(2)}) %copy-start.1) | copy-done | bytes 1572888
  46.5 2.7 %all-to-all-done.shares_ref = f32[128,3,4,128]{3,2,1,0:T(4,128)S(1)} async-done(((f32[128,3,4,128]{3,2,1,0:T(4,128)}), f32[128,3,4,128]{3,2,1,0:T(4,128)S(1)}, u32[]{:S(2)}, u32[]{:S(2)}) %all-to-all-start) | async-done | bytes 786464 | tf_op jit(solution)/shard_map/all_to_all | solution.py:352
  49.3 0.0 collective-permute-start
  49.3 0.1 sum_shares.1
  49.4 0.6 collective-permute-start.1
  50.0 2.6 %collective-permute-done.1.other_ref = f32[21,8,128]{2,1,0:T(8,128)S(1)} collective-permute-done((f32[21,8,128]{2,1,0:T(8,128)S(1)}, f32[21,8,128]{2,1,0:T(8,128)S(1)}, u32[]{:S(2)}, u32[]{:S(2)}) %collective-permute-start.1) | collective-permute-done | bytes 86048 | tf_op jit(solution)/shard_map/ppermute | solution.py:357
  52.6 0.4 collective-permute-done
  53.0 0.2 join_shares.1
  53.3 0.0 copy-start
  53.3 34.6 %all_to_all.10.parts_ref = f32[64,56,128]{2,1,0:T(8,128)S(1)} all-to-all(f32[64,56,128]{2,1,0:T(8,128)S(1)} %join_shares.1), channel_id=1, replica_groups={{0,8,16,24,32,40,48,56,64,72,80,88,96,104,112,120,2,10,18,26,34,42,50,5..., dimensions={0} | all-to-all | bytes 3670016 | tf_op jit(solution)/shard_map/all_to_all | solution.py:360
  87.9 0.0 copy-done
  87.9 1.0 %finish.1 = (f32[12,6,96]{2,1,0:T(8,128)}, f32[200,128]{1,0:T(8,128)}, f32[80,200]{1,0:T(8,128)}, f32[32,200]{1,0:T(8,128)}) custom-call(f32[64,56,128]{2,1,0:T(8,128)S(1)} %all_to_all.10.parts_ref, f32[80,96]{1,0:T(8,128)S(1)} %bitcast.9), custom_call_target="tpu_custom_call" | custom-call | flops 100000000 | bytes 2097152 | tf_op jit(solution)/shard_map/finish/pallas_call | solution.py:318
Async XLA Ops:
  0.6 32.1 %copy-start.2 = (f32[96,512]{1,0:T(8,128)S(1)}, f32[96,512]{1,0:T(8,128)}, u32[]{:S(2)}) copy-start(f32[96,512]{1,0:T(8,128)} %lon_core.1) | copy-start | bytes 589828
  0.6 32.1 %copy-start.3 = (f32[96,128]{1,0:T(8,128)S(1)}, f32[96,128]{1,0:T(8,128)}, u32[]{:S(2)}) copy-start(f32[96,128]{1,0:T(8,128)} %lat_core.1) | copy-start | bytes 147460
  21.6 27.7 %all-to-all-start = ((f32[128,3,4,128]{3,2,1,0:T(4,128)}), f32[128,3,4,128]{3,2,1,0:T(4,128)S(1)}, u32[]{:S(2)}, u32[]{:S(2)}) async-start(f32[128,3,4,128]{3,2,1,0:T(4,128)} %sketch_partials.1), calls=%async_computation | async-start | bytes 1572864 | tf_op jit(solution)/shard_map/all_to_all | solution.py:352
  45.4 1.2 %copy-start.1 = (f32[8,8,48,128]{3,2,1,0:T(8,128)}, f32[8,8,48,128]{3,2,1,0:T(8,128)S(1)}, u32[]{:S(2)}) copy-start(f32[8,8,48,128]{3,2,1,0:T(8,128)S(1)} %get-tuple-element.22) | copy-start | bytes 4718596
  49.3 3.7 %collective-permute-start = (f32[8,8,48,128]{3,2,1,0:T(8,128)}, f32[8,8,48,128]{3,2,1,0:T(8,128)S(1)}, u32[]{:S(2)}, u32[]{:S(2)}) collective-permute-start(f32[8,8,48,128]{3,2,1,0:T(8,128)} %copy-done.1), channel_id=1, source_target_pairs={{0,1},{1,0},{2,3},{3,2},{4,5},{5,4},{6,7},{7,6},{8,9},{9,8},{10,11... | collective-permute-start | bytes 4718600 | tf_op jit(solution)/shard_map/ppermute | solution.py:355
  49.4 3.2 %collective-permute-start.1 = (f32[21,8,128]{2,1,0:T(8,128)S(1)}, f32[21,8,128]{2,1,0:T(8,128)S(1)}, u32[]{:S(2)}, u32[]{:S(2)}) collective-permute-start(f32[21,8,128]{2,1,0:T(8,128)S(1)} %get-tuple-element.25), channel_id=1, source_target_pairs={{0,1},{1,0},{2,3},{3,2},{4,5},{5,4},{6,7},{7,6},{8,9},{9,8},{10,11... | collective-permute-start | bytes 258056 | tf_op jit(solution)/shard_map/ppermute | solution.py:357
  53.3 34.6 %copy-start = (f32[96,80]{0,1:T(8,128)S(1)}, f32[96,80]{0,1:T(8,128)}, u32[]{:S(2)}) copy-start(f32[96,80]{0,1:T(8,128)} %param.13) | copy-start | bytes 92164

commit v4 on v3

v4 whole, which is shorter than its diff:
```python
import jax
import jax.numpy as jnp
from jax import lax
from jax.experimental import pallas as pl
from jax.experimental.pallas import tpu as pltpu
from jax.sharding import PartitionSpec as P

F32 = jnp.float32
BF16 = jnp.bfloat16
BOTH = ("lon", "lat")
HOURS = 16
VMEM = 48 * 1024 * 1024
MOST_VMEM = 62 * 1024 * 1024
MUCH_VMEM = 40 * 1024 * 1024
SLOTS = sorted(range(64), key=lambda chip: (chip % 4, chip // 16, chip // 8 % 2 * 2 + chip // 4 % 2))


def halves(value):
    top = value.astype(BF16)
    return top, (value - top.astype(F32)).astype(BF16)


def dot(left, right, dims=((1,), (0,))):
    return lax.dot_general(left, right, (dims, ((), ())), preferred_element_type=F32)


def stacked_dot(weights, rows, right_top, right_low):
    upper = dot(weights[...], right_top)
    return upper[:rows] + upper[rows:] + dot(weights[:rows], right_low)


def block_copy(field_hbm, field, arrived, at):
    part = pl.ds(at * HOURS, HOURS)
    return pltpu.make_async_copy(field_hbm.at[part], field.at[part], arrived.at[at])


def start_field(field_hbm, field, arrived, blocks):
    for at in blocks:
        block_copy(field_hbm, field, arrived, at).start()


def each_block(field_hbm, field, arrived, work):
    def step(at, carry):
        block_copy(field_hbm, field, arrived, at).wait()
        work(at)
        return carry

    lax.fori_loop(0, arrived.shape[0], step, 0)


def field_scratch(hours, lons, lats):
    return [pltpu.VMEM((hours, lons, lats), F32), pltpu.SemaphoreType.DMA((hours // HOURS,))]


def copies_in(sources, targets, arrived):
    copies = [pltpu.make_async_copy(a, b, arrived.at[i]) for i, (a, b) in enumerate(zip(sources, targets))]
    for copy in copies:
        copy.start()
    return copies


def in_vmem(count):
    return [pl.BlockSpec(memory_space=pltpu.VMEM)] * count


def in_hbm(count):
    return [pl.BlockSpec(memory_space=pltpu.HBM)] * count


def split_rows(values, weights):
    rows = values.shape[0]
    top, low = halves(values)
    weights[:rows] = top
    weights[rows:] = low


def products(weights, top, low):
    both = stacked_dot(weights, weights.shape[0] // 2, top, low)
    return both[:, :128], both[:, 128:]


def first_kernel(
    field_hbm, modes_hbm, lon_hbm, lat_hbm, time_hbm, crossed_hbm, sums_ref,
    field, arrived, lon_core, lon_test, lat_test, time_test, small, weights, crossed, sent, lat_sum, hour_sum,
):
    modes, rank = lon_core.shape[0], lon_test.shape[0]
    lane = lax.broadcasted_iota(jnp.int32, (rank, 128), 1)
    waits = copies_in((modes_hbm, lon_hbm, lat_hbm, time_hbm), (lon_core, lon_test, lat_test, time_test), small)
    start_field(field_hbm, field, arrived, range(1))
    for total in (lat_sum, hour_sum):
        total[...] = jnp.zeros_like(total)
    for copy in waits:
        copy.wait()
    start_field(field_hbm, field, arrived, range(1, arrived.shape[0]))
    split_rows(jnp.concatenate([lon_core[...], lon_test[...]], axis=0), weights)

    def crossed_copy(at):
        return pltpu.make_async_copy(crossed.at[:, at], crossed_hbm.at[:, at], sent.at[at])

    def work(at):
        times = time_test[pl.ds(at * HOURS, HOURS), :].T
        lat_total, hour_total = lat_sum[...], hour_sum[...]
        for pair in range(0, HOURS, 2):
            first = at * HOURS + pair
            top, low = halves(jnp.concatenate([field[first], field[first + 1]], axis=1))
            for hour, result in enumerate(products(weights, top, low), pair):
                crossed[:, at, hour, :] = result[:modes]
                across = result[modes:]
                lat_total = lat_total + across * times[:, hour : hour + 1]
                total = jnp.sum(across * lat_test[...], axis=1, keepdims=True)
                hour_total = jnp.where(lane == at * HOURS + hour, total, hour_total)
        lat_sum[...] = lat_total
        hour_sum[...] = hour_total
        crossed_copy(at).start()

    each_block(field_hbm, field, arrived, work)
    for place in range(rank // 2):
        columns = slice(place * 2, place * 2 + 2)
        sums_ref[place, 0, :2] = lat_sum[columns]
        sums_ref[place, 0, 2:] = hour_sum[columns]
    sums_ref[rank // 2 :] = jnp.zeros((128 - rank // 2, 1, 4, 128), F32)
    for at in range(arrived.shape[0]):
        crossed_copy(at).wait()


def first_partials(field, lon_core, lon_test_t, lat_test_t, time_test):
    hours, lons, lats = field.shape
    modes, rank = lon_core.shape[0], lon_test_t.shape[0]
    blocks = hours // HOURS
    crossed = (modes, blocks, HOURS, lats)
    return pl.pallas_call(
        first_kernel,
        in_specs=in_hbm(5),
        out_specs=[pl.BlockSpec(memory_space=pl.ANY)] + in_vmem(1),
        out_shape=[jax.ShapeDtypeStruct(crossed, F32), jax.ShapeDtypeStruct((128, 1, 4, 128), F32)],
        scratch_shapes=field_scratch(hours, lons, lats)
        + [pltpu.VMEM(x.shape, F32) for x in (lon_core, lon_test_t, lat_test_t, time_test)]
        + [
            pltpu.SemaphoreType.DMA((4,)),
            pltpu.VMEM((2 * (modes + rank), lons), BF16),
            pltpu.VMEM(crossed, F32),
            pltpu.SemaphoreType.DMA((blocks,)),
            pltpu.VMEM((rank, 128), F32),
            pltpu.VMEM((rank, 128), F32),
        ],
        compiler_params=pltpu.CompilerParams(vmem_limit_bytes=MOST_VMEM),
        cost_estimate=pl.CostEstimate(flops=18 * 10**9, bytes_accessed=26 << 20, transcendentals=0),
        name="first_partials",
    )(field, lon_core, lon_test_t, lat_test_t, time_test)


def sum_kernel(shares_ref, keep_ref, send_ref):
    core = lax.axis_index("lat") % 2
    mine = lax.broadcasted_iota(jnp.int32, (4, 128), 0) // 2 == core

    def spread(rows):
        return jnp.where(mine, jnp.concatenate([rows, rows], axis=0), 0.0)

    hour = jnp.zeros((4, 128), F32)
    for at in range(8):
        lats = []
        for lat in (at * 2, at * 2 + 1):
            total = shares_ref[lat, 0]
            for lon in range(1, 8):
                total = total + shares_ref[lon * 16 + lat, 0]
            hour = hour + total
            lats.append(spread(total[:2]))
        tile, row = at // 2, at % 2 * 4
        keep_ref[tile, row : row + 4] = jnp.where(core == 0, lats[0], lats[1])
        send_ref[tile, row : row + 4] = jnp.where(core == 0, lats[1], lats[0])
    hour = spread(hour[2:])
    for out in (keep_ref, send_ref):
        out[4, :4] = hour
        out[4, 4:] = hour


def sum_shares(shares):
    return pl.pallas_call(
        sum_kernel,
        out_shape=[jax.ShapeDtypeStruct((5, 8, 128), F32)] * 2,
        compiler_params=pltpu.CompilerParams(vmem_limit_bytes=MUCH_VMEM),
        cost_estimate=pl.CostEstimate(flops=10**6, bytes_accessed=1 << 20, transcendentals=0),
        name="sum_shares",
    )(shares)


def core_kernel(crossed, lat_core, send_ref, keep_ref):
    core = lax.axis_index("lat") % 2
    of_core = [
        jnp.concatenate([lat_core[pl.ds(at * 6 + b, 8, stride=12), :] for b in range(6)], axis=0) for at in range(2)
    ]
    lat_rows = jnp.concatenate(
        [jnp.where(core == 0, of_core[0], of_core[1]), jnp.where(core == 0, of_core[1], of_core[0])], axis=0
    )
    lat_top, lat_low = halves(lat_rows)
    lats = jnp.concatenate(
        [jnp.concatenate([lat_top, lat_top], axis=1), jnp.concatenate([lat_low, jnp.zeros_like(lat_low)], axis=1)],
        axis=0,
    )

    def share(owner, carry):
        block = crossed[pl.ds(owner * 12, 12)].reshape(960, 128)
        block = jnp.concatenate([block, jnp.zeros((64, 128), F32)], axis=0)
        result = dot(lats, jnp.concatenate(halves(block), axis=1), ((1,), (1,)))
        result = result[:96] + result[96:]
        for part, out in enumerate((keep_ref, send_ref)):
            for b in range(6):
                row = part * 48 + b * 8
                for q in range(8):
                    out[owner, :, q * 6 + b, :] = result[row : row + 8, q * 128 : q * 128 + 128]
        return carry

    lax.fori_loop(0, 8, share, 0)


def core_partials(crossed, lat_core):
    part = jax.ShapeDtypeStruct((8, 8, 48, 128), F32)
    return pl.pallas_call(
        core_kernel,
        in_specs=in_vmem(2),
        out_specs=in_vmem(2),
        out_shape=[part, part],
        compiler_params=pltpu.CompilerParams(vmem_limit_bytes=MUCH_VMEM),
        cost_estimate=pl.CostEstimate(flops=20 * 10**9, bytes_accessed=8 << 20, transcendentals=0),
        name="core_partials",
    )(crossed, lat_core)


def join_kernel(keep_ref, arrived_ref, mine_ref, other_ref, out_ref, sums):
    sums[...] = mine_ref[...] + other_ref[...]
    for slot, chip in enumerate(SLOTS):
        lat = chip % 8
        row = lat % 2 * 4
        out_ref[slot, :48] = keep_ref[chip] + arrived_ref[chip]
        out_ref[slot, 48:52] = sums[lat // 2, row : row + 4]
        out_ref[slot, 52:] = sums[4, :4]


def join_shares(keep, arrived, mine, other):
    return pl.pallas_call(
        join_kernel,
        in_specs=in_vmem(4),
        out_specs=pl.BlockSpec(memory_space=pltpu.VMEM),
        out_shape=jax.ShapeDtypeStruct((64, 56, 128), F32),
        scratch_shapes=[pltpu.VMEM(mine.shape, F32)],
        compiler_params=pltpu.CompilerParams(vmem_limit_bytes=MUCH_VMEM),
        cost_estimate=pl.CostEstimate(flops=10**6, bytes_accessed=5 << 20, transcendentals=0),
        name="join_shares",
    )(keep, arrived, mine, other)


def lon_kernel(field_hbm, lat_ref, time_ref, keep_ref, send_ref, field, arrived, lat_test, total):
    start_field(field_hbm, field, arrived, range(arrived.shape[0]))
    total[...] = jnp.zeros_like(total)
    lat_test[...] = lat_ref[...].T
    lons = total.shape[0]

    def work(at):
        times = time_ref[pl.ds(at * HOURS, HOURS), :]
        tests = [lat_test[...] * times[hour : hour + 1, :] for hour in range(HOURS)]
        test_top, test_low = halves(jnp.concatenate(tests, axis=0))
        values = [halves(field[at * HOURS + hour]) for hour in range(HOURS)]
        top = jnp.concatenate([value[0] for value in values], axis=1)
        low = jnp.concatenate([value[1] for value in values], axis=1)
        upper = dot(jnp.concatenate([top, low], axis=0), test_top)
        total[...] += upper[:lons] + upper[lons:] + dot(top, test_low)

    each_block(field_hbm, field, arrived, work)
    place = lax.axis_index("lat")
    core, z, x_lo = place % 2, place // 2 % 4, place // 8
    for step in range(4):
        for flip in range(2):
            x = x_lo + flip - 2 * x_lo * flip
            owner = x * 8 + (z + step) % 4 * 2
            for out, of_core in ((keep_ref, core), (send_ref, 1 - core)):
                out[step, flip] = total[pl.ds(pl.multiple_of((owner + of_core) * 32, 32), 32), :]


def lon_partial(field, lat_test_t, time_test):
    hours, lons, lats = field.shape
    rank = lat_test_t.shape[0]
    out = jax.ShapeDtypeStruct((4, 2, 32, rank), F32)
    return pl.pallas_call(
        lon_kernel,
        in_specs=in_hbm(1) + in_vmem(2),
        out_specs=in_vmem(2),
        out_shape=[out, out],
        scratch_shapes=field_scratch(hours, lons, lats)
        + [pltpu.VMEM((lats, rank), F32), pltpu.VMEM((lons, rank), F32)],
        compiler_params=pltpu.CompilerParams(vmem_limit_bytes=MUCH_VMEM),
        cost_estimate=pl.CostEstimate(flops=12 * 10**9, bytes_accessed=22 << 20, transcendentals=0),
        name="lon_partial",
    )(field, lat_test_t, time_test)


def finish_kernel(parts_ref, time_ref, core_ref, lat_ref, hour_ref, columns):
    total = parts_ref[0, :48]
    for source in range(1, parts_ref.shape[0]):
        total = total + parts_ref[source, :48]
    modes = [jnp.concatenate([total[q * 6 : q * 6 + 6], jnp.zeros((2, 128), F32)], axis=0) for q in range(8)]
    modes = jnp.concatenate(modes, axis=1)
    rows = jnp.concatenate([modes[:, a * 80 : a * 80 + 80] for a in range(12)], axis=0)
    result = lax.dot_general(
        rows,
        time_ref[...],
        (((1,), (0,)), ((), ())),
        precision=lax.Precision.HIGHEST,
        preferred_element_type=F32,
    )
    for a in range(12):
        core_ref[a] = result[a * 8 : a * 8 + 6]
    for slot, chip in enumerate(SLOTS):
        if chip < 50:
            lat_ref[chip * 4 : chip * 4 + 4] = parts_ref[slot, 48:52]
            columns[chip * 4 : chip * 4 + 4] = parts_ref[slot, 52:]
    hour_ref[...] = columns[...].T[:80]


def finish(parts, time_core_t):
    return pl.pallas_call(
        finish_kernel,
        out_shape=[
            jax.ShapeDtypeStruct((12, 6, 96), F32),
            jax.ShapeDtypeStruct((200, 128), F32),
            jax.ShapeDtypeStruct((80, 200), F32),
        ],
        scratch_shapes=[pltpu.VMEM((200, 128), F32)],
        compiler_params=pltpu.CompilerParams(vmem_limit_bytes=VMEM),
        cost_estimate=pl.CostEstimate(flops=10**8, bytes_accessed=2 << 20, transcendentals=0),
        name="finish",
    )(parts, time_core_t)


def places(move):
    pairs = []
    for source in range(128):
        lon, lat = divmod(source, 16)
        x, y, z, core = (lon % 2) * 2 + lat // 8, lon // 2, lat // 2 % 4, lat % 2
        x, y, z, core = move(x, y, z, core)
        pairs.append((source, (y * 2 + x // 2) * 16 + x % 2 * 8 + z * 2 + core))
    return pairs


OTHER_CORE = places(lambda x, y, z, core: (x, y, z, 1 - core))
Z_STEPS = [places(lambda x, y, z, core: (x, y, (z + step) % 4, core)) for step in range(4)]
X_FLIP = places(lambda x, y, z, core: (x ^ 1, y, z, core))
CHIPS = [[chip // 8 * 16 + chip % 8 * 2 + core for chip in SLOTS] for core in (0, 1)]


def on_device(field, lon_test, lat_test, time_test, lon_core, lat_core, time_core):
    crossed, sums = first_partials(field, lon_core, lon_test.T, lat_test.T, time_test)

    shares = lax.all_to_all(sums, BOTH, 0, 0)
    send, keep = core_partials(crossed, lat_core)
    shares, send, keep = lax.optimization_barrier((shares, send, keep))
    other = lax.ppermute(send, BOTH, OTHER_CORE)
    mine, others = sum_shares(shares)
    others = lax.ppermute(others, BOTH, OTHER_CORE)

    chip = join_shares(keep.reshape(64, 48, 128), other.reshape(64, 48, 128), mine, others)
    parts = lax.all_to_all(chip, BOTH, 0, 0, axis_index_groups=CHIPS)

    field, _ = lax.optimization_barrier((field, chip))
    keep, send = lon_partial(field, lat_test.T, time_test)
    rows = keep + lax.ppermute(send, BOTH, OTHER_CORE)
    total = rows[0]
    for step in range(1, 4):
        total = total + lax.ppermute(rows[step], BOTH, Z_STEPS[step])
    total, parts = lax.optimization_barrier((total, parts))
    sketch_lon = total[0] + lax.ppermute(total[1], BOTH, X_FLIP)

    core_sketch, sketch_lat, sketch_time = finish(parts, time_core.T)
    return (sketch_lon, sketch_lat.T, sketch_time, core_sketch.transpose(2, 0, 1))


def solution(mesh):
    return jax.shard_map(
        on_device,
        mesh=mesh,
        in_specs=(
            P(None, "lon", "lat"),
            P("lon", None),
            P("lat", None),
            P(),
            P(None, "lon"),
            P(None, "lat"),
            P(),
        ),
        out_specs=(P(("lon", "lat"), None), P("lat", None), P(), P(None, "lon", "lat")),
        check_vma=False,
    )
```

time: 89.2 us -> 83 us (0.930)
  blocking collectives: 34.6 us -> 0 us
  waiting for transfers between devices: 5.78 us -> 22.1 us
  starting transfers between devices: 11.7 us -> 23 us
  local copies, waits for them, and re-layouts: 1.16 us -> 3.41 us
  Pallas kernels: 34.9 us -> 32.8 us
    all_to_all x1 -> x0, blocking collectives: 34.6 us -> none  [on_device(): parts = lax.all_to_all(chip, BOTH, 0, 0, axis_index_groups=MIXED)]
    ppermute x0 -> x5, waiting for transfers between devices: none -> 14 us  [the longest x3 10.3 us: on_device(): total = total + lax.ppermute(rows[step], BOTH, Z_STEPS[step])]
    ppermute x0 -> x5, starting transfers between devices: none -> 6.13 us  [the longest x3 5.28 us: on_device(): total = total + lax.ppermute(rows[step], BOTH, Z_STEPS[step])]
    all_to_all x0 -> x1, starting transfers between devices: none -> 5.12 us  [on_device(): parts = lax.all_to_all(chip, BOTH, 0, 0, axis_index_groups=CHIPS)]
    all_to_all x1, waiting for transfers between devices: 2.73 us -> 5.21 us  [on_device(): shares = lax.all_to_all(sums, BOTH, 0, 0)]
    unnamed x8 -> x12, local copies, waits for them, and re-layouts: 1.16 us -> 3.39 us
    pallas_call x3 -> x4, Pallas kernels: 33.6 us -> 31.6 us  [the longest x1 16.6 us: first_partials(): pl.pallas_call(first_kernel, in_specs=in_hbm(5), out_specs=[pl.BlockSpec(...]
  transfers between devices with their start and end apart: 3 -> 9, of which waited for: 3 -> 6; matrix products, arithmetic and copies ran while one was open for 0% -> 0% of each run, Pallas kernels for 14% -> 19%
where the time goes in v4:
time: 83 us; the launch traced here: 82.7 us
  Pallas kernels  32.8 us (40%)
  starting transfers between devices  23 us (28%)
  waiting for transfers between devices  22.1 us (27%)
  local copies, waits for them, and re-layouts  3.41 us (4%)
    pallas_call x1, Pallas kernels, first_partials(): pl.pallas_call(first_kernel, in_specs=in_hbm(5), out_specs=[pl.BlockSpec(...  16.6 us
    pallas_call x1, Pallas kernels, lon_partial(): pl.pallas_call(lon_kernel, in_specs=in_hbm(1) + in_vmem(2), out_specs=in_...  11.4 us
    all_to_all x1, starting transfers between devices, on_device(): shares = lax.all_to_all(sums, BOTH, 0, 0)  11.1 us
    ppermute x3, waiting for transfers between devices, on_device(): total = total + lax.ppermute(rows[step], BOTH, Z_STEPS[step])  10.3 us
    ppermute x3, starting transfers between devices, on_device(): total = total + lax.ppermute(rows[step], BOTH, Z_STEPS[step])  5.28 us
    all_to_all x1, waiting for transfers between devices, on_device(): shares = lax.all_to_all(sums, BOTH, 0, 0)  5.21 us
    all_to_all x1, starting transfers between devices, on_device(): parts = lax.all_to_all(chip, BOTH, 0, 0, axis_index_groups=CHIPS)  5.12 us
    pallas_call x1, Pallas kernels, core_partials(): pl.pallas_call(core_kernel, in_specs=in_vmem(2), out_specs=in_vmem(2), ou...  3.58 us
  transfers between devices with their start and end apart: 9, of which 6 were waited for; matrix products, arithmetic and copies ran while one was open for 0% of the time, Pallas kernels for 19%

profile of v4, /device:TPU:0, one launch (start us, length us, event | category | flops | bytes accessed | tf_op | source)
XLA Modules:
  0.0 82.7 jit_solution(15522780961905462517)
XLA Ops:
  0.6 16.6 %first_partials.1 = (f32[96,5,16,128]{3,2,1,0:T(8,128)}, f32[128,1,4,128]{3,2,1,0:T(4,128)}) custom-call(f32[80,512,128]{2,1,0:T(8,128)} %field_hbm.2, f32[96,512]{1,0:T(8,128)} %modes_hbm.1, f32[200,512]{1,0:T(8,128)} %bitcast.30, f32[200,128]{1,0:T(8,128)} %bitcast.28, f32[80,200]{1,0:T(8,128)} %time_ref.1), custom_call_target="tpu_custom_call" | custom-call | flops 17999998976 | bytes 27262976 | tf_op jit(solution)/shard_map/first_partials/pallas_call | solution.py:131
  17.3 11.1 %all-to-all-start = ((f32[128,1,4,128]{3,2,1,0:T(4,128)}), f32[128,1,4,128]{3,2,1,0:T(4,128)S(1)}, u32[]{:S(2)}, u32[]{:S(2)}) async-start(f32[128,1,4,128]{3,2,1,0:T(4,128)} %get-tuple-element.21), calls=%async_computation | async-start | bytes 524288 | tf_op jit(solution)/shard_map/all_to_all | solution.py:353
  28.4 2.1 %copy-done.5 = f32[96,5,16,128]{3,2,1,0:T(8,128)S(1)} copy-done((f32[96,5,16,128]{3,2,1,0:T(8,128)S(1)}, f32[96,5,16,128]{3,2,1,0:T(8,128)}, u32[]{:S(2)}) %copy-start.5) | copy-done | bytes 3932184
  30.5 3.6 %core_partials.1 = (f32[8,8,48,128]{3,2,1,0:T(8,128)S(1)}, f32[8,8,48,128]{3,2,1,0:T(8,128)S(1)}) custom-call(f32[96,5,16,128]{3,2,1,0:T(8,128)S(1)} %copy-done.5, f32[96,128]{1,0:T(8,128)S(1)} %copy-done.4), custom_call_target="tpu_custom_call" | custom-call | flops 20000000000 | bytes 8388608 | tf_op jit(solution)/shard_map/core_partials/pallas_call | solution.py:218
  34.1 5.2 %all-to-all-done.shares_ref = f32[128,1,4,128]{3,2,1,0:T(4,128)S(1)} async-done(((f32[128,1,4,128]{3,2,1,0:T(4,128)}), f32[128,1,4,128]{3,2,1,0:T(4,128)S(1)}, u32[]{:S(2)}, u32[]{:S(2)}) %all-to-all-start) | async-done | bytes 262176 | tf_op jit(solution)/shard_map/all_to_all | solution.py:353
  39.4 0.0 collective-permute-start
  39.4 0.6 collective-permute-start.1
  40.0 2.8 %collective-permute-done.1.other_ref = f32[5,8,128]{2,1,0:T(8,128)S(1)} collective-permute-done((f32[5,8,128]{2,1,0:T(8,128)S(1)}, f32[5,8,128]{2,1,0:T(8,128)S(1)}, u32[]{:S(2)}, u32[]{:S(2)}) %collective-permute-start.1) | collective-permute-done | bytes 20512 | tf_op jit(solution)/shard_map/ppermute | solution.py:358
  42.8 0.2 join_shares.1
  43.0 1.3 %copy-done = f32[64,56,128]{2,1,0:T(8,128)} copy-done((f32[64,56,128]{2,1,0:T(8,128)}, f32[64,56,128]{2,1,0:T(8,128)S(1)}, u32[]{:S(2)}) %copy-start) | copy-done | bytes 1835032
  44.3 5.1 %all-to-all-start.1 = ((f32[64,56,128]{2,1,0:T(8,128)}), f32[64,56,128]{2,1,0:T(8,128)S(1)}, u32[]{:S(2)}, u32[]{:S(2)}) async-start(f32[64,56,128]{2,1,0:T(8,128)} %copy-done), calls=%async_computation.1 | async-start | bytes 3670016 | tf_op jit(solution)/shard_map/all_to_all | solution.py:361
  49.4 0.0 copy-start.1
  49.4 11.4 %lon_partial.1 = (f32[4,2,32,200]{3,2,1,0:T(8,128)S(1)}, f32[4,2,32,200]{3,2,1,0:T(8,128)S(1)}) custom-call(f32[80,512,128]{2,1,0:T(8,128)} %field_hbm.2, f32[200,128]{1,0:T(8,128)S(1)} %bitcast.29, f32[80,200]{1,0:T(8,128)S(1)} %copy-done.3), custom_call_target="tpu_custom_call" | custom-call | flops 12000000000 | bytes 23068672 | tf_op jit(solution)/shard_map/lon_partial/pallas_call | solution.py:283
  60.8 0.1 collective-permute-start.2
  60.9 1.5 %collective-permute-done.2 = f32[4,2,32,200]{3,2,1,0:T(8,128)S(1)} collective-permute-done((f32[4,2,32,200]{3,2,1,0:T(8,128)S(1)}, f32[4,2,32,200]{3,2,1,0:T(8,128)S(1)}, u32[]{:S(2)}, u32[]{:S(2)}) %collective-permute-start.2) | collective-permute-done | bytes 204832 | tf_op jit(solution)/shard_map/ppermute | solution.py:365
  62.5 1.6 %collective-permute-start.3 = (f32[2,32,200]{2,1,0:T(8,128)S(1)}, f32[2,32,200]{2,1,0:T(8,128)S(1)}, u32[]{:S(2)}, u32[]{:S(2)}) collective-permute-start(f32[2,32,200]{2,1,0:T(8,128)S(1)} %get-tuple-element.38), channel_id=1, source_target_pairs={{0,2},{1,3},{2,4},{3,5},{4,6},{5,7},{6,0},{7,1},{8,10},{9,11},{10,... | collective-permute-start | bytes 153608 | tf_op jit(solution)/shard_map/ppermute | solution.py:368
  64.2 1.7 %collective-permute-start.5 = (f32[2,32,200]{2,1,0:T(8,128)S(1)}, f32[2,32,200]{2,1,0:T(8,128)S(1)}, u32[]{:S(2)}, u32[]{:S(2)}) collective-permute-start(f32[2,32,200]{2,1,0:T(8,128)S(1)} %get-tuple-element.39), channel_id=1, source_target_pairs={{0,6},{1,7},{2,0},{3,1},{4,2},{5,3},{6,4},{7,5},{8,14},{9,15},{10,... | collective-permute-start | bytes 153608 | tf_op jit(solution)/shard_map/ppermute | solution.py:368
  65.8 2.0 %collective-permute-start.4 = (f32[2,32,200]{2,1,0:T(8,128)S(1)}, f32[2,32,200]{2,1,0:T(8,128)S(1)}, u32[]{:S(2)}, u32[]{:S(2)}) collective-permute-start(f32[2,32,200]{2,1,0:T(8,128)S(1)} %get-tuple-element.40), channel_id=1, source_target_pairs={{0,4},{1,5},{2,6},{3,7},{4,0},{5,1},{6,2},{7,3},{8,12},{9,13},{10,... | collective-permute-start | bytes 153608 | tf_op jit(solution)/shard_map/ppermute | solution.py:368
  67.8 7.0 %collective-permute-done.3 = f32[2,32,200]{2,1,0:T(8,128)S(1)} collective-permute-done((f32[2,32,200]{2,1,0:T(8,128)S(1)}, f32[2,32,200]{2,1,0:T(8,128)S(1)}, u32[]{:S(2)}, u32[]{:S(2)}) %collective-permute-start.3) | collective-permute-done | bytes 51232 | tf_op jit(solution)/shard_map/ppermute | solution.py:368
  74.8 3.3 %collective-permute-done.4 = f32[2,32,200]{2,1,0:T(8,128)S(1)} collective-permute-done((f32[2,32,200]{2,1,0:T(8,128)S(1)}, f32[2,32,200]{2,1,0:T(8,128)S(1)}, u32[]{:S(2)}, u32[]{:S(2)}) %collective-permute-start.4) | collective-permute-done | bytes 51232 | tf_op jit(solution)/shard_map/ppermute | solution.py:368
  78.1 0.8 collective-permute-start.6
  78.9 1.0 %finish.1 = (f32[12,6,96]{2,1,0:T(8,128)}, f32[200,128]{1,0:T(8,128)}, f32[80,200]{1,0:T(8,128)}) custom-call(f32[64,56,128]{2,1,0:T(8,128)S(1)} %all-to-all-done.1.parts_ref, f32[80,96]{1,0:T(8,128)S(1)} %bitcast.27), custom_call_target="tpu_custom_call" | custom-call | flops 100000000 | bytes 2097152 | tf_op jit(solution)/shard_map/finish/pallas_call | solution.py:320
  79.9 2.2 %collective-permute-done.6 = f32[32,200]{1,0:T(8,128)S(1)} collective-permute-done((f32[32,200]{1,0:T(8,128)S(1)}, f32[32,200]{1,0:T(8,128)S(1)}, u32[]{:S(2)}, u32[]{:S(2)}) %collective-permute-start.6) | collective-permute-done | bytes 25632 | tf_op jit(solution)/shard_map/ppermute | solution.py:370
  82.1 0.6 bitcast_add_fusion
  (17 shorter events, 0.1 us)
Async XLA Ops:
  0.6 27.8 %copy-start.4 = (f32[96,128]{1,0:T(8,128)S(1)}, f32[96,128]{1,0:T(8,128)}, u32[]{:S(2)}) copy-start(f32[96,128]{1,0:T(8,128)} %lat_core.1) | copy-start | bytes 147460
  17.3 22.1 %all-to-all-start = ((f32[128,1,4,128]{3,2,1,0:T(4,128)}), f32[128,1,4,128]{3,2,1,0:T(4,128)S(1)}, u32[]{:S(2)}, u32[]{:S(2)}) async-start(f32[128,1,4,128]{3,2,1,0:T(4,128)} %get-tuple-element.21), calls=%async_computation | async-start | bytes 524288 | tf_op jit(solution)/shard_map/all_to_all | solution.py:353
  28.4 2.1 %copy-start.5 = (f32[96,5,16,128]{3,2,1,0:T(8,128)S(1)}, f32[96,5,16,128]{3,2,1,0:T(8,128)}, u32[]{:S(2)}) copy-start(f32[96,5,16,128]{3,2,1,0:T(8,128)} %get-tuple-element.22.crossed) | copy-start | bytes 11796484
  39.4 3.4 %collective-permute-start = (f32[8,8,48,128]{3,2,1,0:T(8,128)S(1)}, f32[8,8,48,128]{3,2,1,0:T(8,128)S(1)}, u32[]{:S(2)}, u32[]{:S(2)}) collective-permute-start(f32[8,8,48,128]{3,2,1,0:T(8,128)S(1)} %get-tuple-element.26), channel_id=1, source_target_pairs={{0,1},{1,0},{2,3},{3,2},{4,5},{5,4},{6,7},{7,6},{8,9},{9,8},{10,11... | collective-permute-start | bytes 4718600 | tf_op jit(solution)/shard_map/ppermute | solution.py:356
  39.4 3.4 %collective-permute-start.1 = (f32[5,8,128]{2,1,0:T(8,128)S(1)}, f32[5,8,128]{2,1,0:T(8,128)S(1)}, u32[]{:S(2)}, u32[]{:S(2)}) collective-permute-start(f32[5,8,128]{2,1,0:T(8,128)S(1)} %get-tuple-element.29), channel_id=1, source_target_pairs={{0,1},{1,0},{2,3},{3,2},{4,5},{5,4},{6,7},{7,6},{8,9},{9,8},{10,11... | collective-permute-start | bytes 61448 | tf_op jit(solution)/shard_map/ppermute | solution.py:358
  43.0 1.3 %copy-start = (f32[64,56,128]{2,1,0:T(8,128)}, f32[64,56,128]{2,1,0:T(8,128)S(1)}, u32[]{:S(2)}) copy-start(f32[64,56,128]{2,1,0:T(8,128)S(1)} %join_shares.1) | copy-start | bytes 5505028
  44.3 5.1 %copy-start.2 = (f32[128,200]{0,1:T(8,128)S(1)}, f32[128,200]{0,1:T(8,128)}, u32[]{:S(2)}) copy-start(f32[128,200]{0,1:T(8,128)} %param.9) | copy-start | bytes 307204
  44.3 5.1 %copy-start.3 = (f32[80,200]{1,0:T(8,128)S(1)}, f32[80,200]{1,0:T(8,128)}, u32[]{:S(2)}) copy-start(f32[80,200]{1,0:T(8,128)} %time_ref.1) | copy-start | bytes 192004
  44.3 33.8 %all-to-all-start.1 = ((f32[64,56,128]{2,1,0:T(8,128)}), f32[64,56,128]{2,1,0:T(8,128)S(1)}, u32[]{:S(2)}, u32[]{:S(2)}) async-start(f32[64,56,128]{2,1,0:T(8,128)} %copy-done), calls=%async_computation.1 | async-start | bytes 3670016 | tf_op jit(solution)/shard_map/all_to_all | solution.py:361
  49.4 29.5 %copy-start.1 = (f32[96,80]{0,1:T(8,128)S(1)}, f32[96,80]{0,1:T(8,128)}, u32[]{:S(2)}) copy-start(f32[96,80]{0,1:T(8,128)} %param.13) | copy-start | bytes 92164
  60.8 1.6 %collective-permute-start.2 = (f32[4,2,32,200]{3,2,1,0:T(8,128)S(1)}, f32[4,2,32,200]{3,2,1,0:T(8,128)S(1)}, u32[]{:S(2)}, u32[]{:S(2)}) collective-permute-start(f32[4,2,32,200]{3,2,1,0:T(8,128)S(1)} %get-tuple-element.32), channel_id=1, source_target_pairs={{0,1},{1,0},{2,3},{3,2},{4,5},{5,4},{6,7},{7,6},{8,9},{9,8},{10,11... | collective-permute-start | bytes 614408 | tf_op jit(solution)/shard_map/ppermute | solution.py:365
  62.5 12.3 %collective-permute-start.3 = (f32[2,32,200]{2,1,0:T(8,128)S(1)}, f32[2,32,200]{2,1,0:T(8,128)S(1)}, u32[]{:S(2)}, u32[]{:S(2)}) collective-permute-start(f32[2,32,200]{2,1,0:T(8,128)S(1)} %get-tuple-element.38), channel_id=1, source_target_pairs={{0,2},{1,3},{2,4},{3,5},{4,6},{5,7},{6,0},{7,1},{8,10},{9,11},{10,... | collective-permute-start | bytes 153608 | tf_op jit(solution)/shard_map/ppermute | solution.py:368
  64.2 10.6 %collective-permute-start.5 = (f32[2,32,200]{2,1,0:T(8,128)S(1)}, f32[2,32,200]{2,1,0:T(8,128)S(1)}, u32[]{:S(2)}, u32[]{:S(2)}) collective-permute-start(f32[2,32,200]{2,1,0:T(8,128)S(1)} %get-tuple-element.39), channel_id=1, source_target_pairs={{0,6},{1,7},{2,0},{3,1},{4,2},{5,3},{6,4},{7,5},{8,14},{9,15},{10,... | collective-permute-start | bytes 153608 | tf_op jit(solution)/shard_map/ppermute | solution.py:368
  65.8 12.2 %collective-permute-start.4 = (f32[2,32,200]{2,1,0:T(8,128)S(1)}, f32[2,32,200]{2,1,0:T(8,128)S(1)}, u32[]{:S(2)}, u32[]{:S(2)}) collective-permute-start(f32[2,32,200]{2,1,0:T(8,128)S(1)} %get-tuple-element.40), channel_id=1, source_target_pairs={{0,4},{1,5},{2,6},{3,7},{4,0},{5,1},{6,2},{7,3},{8,12},{9,13},{10,... | collective-permute-start | bytes 153608 | tf_op jit(solution)/shard_map/ppermute | solution.py:368
  78.1 4.0 %collective-permute-start.6 = (f32[32,200]{1,0:T(8,128)S(1)}, f32[32,200]{1,0:T(8,128)S(1)}, u32[]{:S(2)}, u32[]{:S(2)}) collective-permute-start(f32[32,200]{1,0:T(8,128)S(1)} %slice_bitcast_fusion.4), channel_id=1, source_target_pairs={{0,8},{1,9},{2,10},{3,11},{4,12},{5,13},{6,14},{7,15},{8,0},{9,1},... | collective-permute-start | bytes 76808 | tf_op jit(solution)/shard_map/ppermute | solution.py:370

commit v5 on v4

--- a/solution.py
+++ b/solution.py
@@ -12,7 +12,7 @@
 VMEM = 48 * 1024 * 1024
 MOST_VMEM = 62 * 1024 * 1024
 MUCH_VMEM = 40 * 1024 * 1024
-SLOTS = sorted(range(64), key=lambda chip: (chip % 4, chip // 16, chip // 8 % 2 * 2 + chip // 4 % 2))
+SLOTS = sorted(range(64), key=lambda chip: (chip // 16, chip % 4, chip // 8 % 2 * 2 + chip // 4 % 2))
 
 
 def halves(value):
@@ -184,7 +184,10 @@
     )(shares)
 
 
-def core_kernel(crossed, lat_core, send_ref, keep_ref):
+def core_kernel(crossed, lat_ref, send_ref, keep_ref, lat_core):
+    lat_core[:96] = lat_ref[...]
+    lat_core[96:] = jnp.zeros((16, 128), F32)
+
     core = lax.axis_index("lat") % 2
     of_core = [
         jnp.concatenate([lat_core[pl.ds(at * 6 + b, 8, stride=12), :] for b in range(6)], axis=0) for at in range(2)
@@ -220,6 +223,7 @@
         in_specs=in_vmem(2),
         out_specs=in_vmem(2),
         out_shape=[part, part],
+        scratch_shapes=[pltpu.VMEM((112, 128), F32)],
         compiler_params=pltpu.CompilerParams(vmem_limit_bytes=MUCH_VMEM),
         cost_estimate=pl.CostEstimate(flops=20 * 10**9, bytes_accessed=8 << 20, transcendentals=0),
         name="core_partials",

time: 83 us -> 82.4 us (level)
  waiting for transfers between devices: 22.1 us -> 20.3 us
  starting transfers between devices: 23 us -> 23.9 us
    ppermute x3, waiting for transfers between devices: 10.3 us -> 8.85 us  [on_device(): total = total + lax.ppermute(rows[step], BOTH, Z_STEPS[step])]
    ppermute x1, waiting for transfers between devices: 2.24 us -> 1.12 us  [on_device(): sketch_lon = total[0] + lax.ppermute(total[1], BOTH, X_FLIP)]
    ppermute x1, starting transfers between devices: 0.77 us -> 1.81 us  [on_device(): sketch_lon = total[0] + lax.ppermute(total[1], BOTH, X_FLIP)]
  transfers between devices with their start and end apart: 9 -> 9, of which waited for: 6 -> 8; matrix products, arithmetic and copies ran while one was open for 0% -> 0% of each run, Pallas kernels for 19% -> 20%
where the time goes in v5:
time: 82.4 us; the launch traced here: 81.9 us
  Pallas kernels  32.8 us (40%)
  starting transfers between devices  23.9 us (29%)
  waiting for transfers between devices  20.3 us (25%)
  local copies, waits for them, and re-layouts  3.41 us (4%)
    pallas_call x1, Pallas kernels, first_partials(): pl.pallas_call(first_kernel, in_specs=in_hbm(5), out_specs=[pl.BlockSpec(...  16.6 us
    pallas_call x1, Pallas kernels, lon_partial(): pl.pallas_call(lon_kernel, in_specs=in_hbm(1) + in_vmem(2), out_specs=in_...  11.4 us
    all_to_all x1, starting transfers between devices, on_device(): shares = lax.all_to_all(sums, BOTH, 0, 0)  11.1 us
    ppermute x3, waiting for transfers between devices, on_device(): total = total + lax.ppermute(rows[step], BOTH, Z_STEPS[step])  8.85 us
    all_to_all x1, waiting for transfers between devices, on_device(): shares = lax.all_to_all(sums, BOTH, 0, 0)  5.21 us
    ppermute x3, starting transfers between devices, on_device(): total = total + lax.ppermute(rows[step], BOTH, Z_STEPS[step])  5.17 us
    all_to_all x1, starting transfers between devices, on_device(): parts = lax.all_to_all(chip, BOTH, 0, 0, axis_index_groups=CHIPS)  5.13 us
    pallas_call x1, Pallas kernels, core_partials(): pl.pallas_call(core_kernel, in_specs=in_vmem(2), out_specs=in_vmem(2), ou...  3.59 us
  transfers between devices with their start and end apart: 9, of which 8 were waited for; matrix products, arithmetic and copies ran while one was open for 0% of the time, Pallas kernels for 20%

profile of v5, /device:TPU:0, one launch (start us, length us, event | category | flops | bytes accessed | tf_op | source)
XLA Modules:
  0.0 81.9 jit_solution(14280977253707248179)
XLA Ops:
  0.6 16.6 %first_partials.1 = (f32[96,5,16,128]{3,2,1,0:T(8,128)}, f32[128,1,4,128]{3,2,1,0:T(4,128)}) custom-call(f32[80,512,128]{2,1,0:T(8,128)} %field_hbm.2, f32[96,512]{1,0:T(8,128)} %modes_hbm.1, f32[200,512]{1,0:T(8,128)} %bitcast.30, f32[200,128]{1,0:T(8,128)} %bitcast.28, f32[80,200]{1,0:T(8,128)} %time_ref.1), custom_call_target="tpu_custom_call" | custom-call | flops 17999998976 | bytes 27262976 | tf_op jit(solution)/shard_map/first_partials/pallas_call | solution.py:131
  17.3 11.1 %all-to-all-start = ((f32[128,1,4,128]{3,2,1,0:T(4,128)}), f32[128,1,4,128]{3,2,1,0:T(4,128)S(1)}, u32[]{:S(2)}, u32[]{:S(2)}) async-start(f32[128,1,4,128]{3,2,1,0:T(4,128)} %get-tuple-element.21), calls=%async_computation | async-start | bytes 524288 | tf_op jit(solution)/shard_map/all_to_all | solution.py:357
  28.4 2.1 %copy-done.5 = f32[96,5,16,128]{3,2,1,0:T(8,128)S(1)} copy-done((f32[96,5,16,128]{3,2,1,0:T(8,128)S(1)}, f32[96,5,16,128]{3,2,1,0:T(8,128)}, u32[]{:S(2)}) %copy-start.5) | copy-done | bytes 3932184
  30.5 3.6 %core_partials.1 = (f32[8,8,48,128]{3,2,1,0:T(8,128)S(1)}, f32[8,8,48,128]{3,2,1,0:T(8,128)S(1)}) custom-call(f32[96,5,16,128]{3,2,1,0:T(8,128)S(1)} %copy-done.5, f32[96,128]{1,0:T(8,128)S(1)} %copy-done.4), custom_call_target="tpu_custom_call" | custom-call | flops 20000000000 | bytes 8388608 | tf_op jit(solution)/shard_map/core_partials/pallas_call | solution.py:221
  34.1 5.2 %all-to-all-done.shares_ref = f32[128,1,4,128]{3,2,1,0:T(4,128)S(1)} async-done(((f32[128,1,4,128]{3,2,1,0:T(4,128)}), f32[128,1,4,128]{3,2,1,0:T(4,128)S(1)}, u32[]{:S(2)}, u32[]{:S(2)}) %all-to-all-start) | async-done | bytes 262176 | tf_op jit(solution)/shard_map/all_to_all | solution.py:357
  39.4 0.6 collective-permute-start.1
  40.0 2.8 %collective-permute-done.1.other_ref = f32[5,8,128]{2,1,0:T(8,128)S(1)} collective-permute-done((f32[5,8,128]{2,1,0:T(8,128)S(1)}, f32[5,8,128]{2,1,0:T(8,128)S(1)}, u32[]{:S(2)}, u32[]{:S(2)}) %collective-permute-start.1) | collective-permute-done | bytes 20512 | tf_op jit(solution)/shard_map/ppermute | solution.py:362
  42.8 0.2 join_shares.1
  43.0 1.3 %copy-done = f32[64,56,128]{2,1,0:T(8,128)} copy-done((f32[64,56,128]{2,1,0:T(8,128)}, f32[64,56,128]{2,1,0:T(8,128)S(1)}, u32[]{:S(2)}) %copy-start) | copy-done | bytes 1835032
  44.3 5.1 %all-to-all-start.1 = ((f32[64,56,128]{2,1,0:T(8,128)}), f32[64,56,128]{2,1,0:T(8,128)S(1)}, u32[]{:S(2)}, u32[]{:S(2)}) async-start(f32[64,56,128]{2,1,0:T(8,128)} %copy-done), calls=%async_computation.1 | async-start | bytes 3670016 | tf_op jit(solution)/shard_map/all_to_all | solution.py:365
  49.4 11.4 %lon_partial.1 = (f32[4,2,32,200]{3,2,1,0:T(8,128)S(1)}, f32[4,2,32,200]{3,2,1,0:T(8,128)S(1)}) custom-call(f32[80,512,128]{2,1,0:T(8,128)} %field_hbm.2, f32[200,128]{1,0:T(8,128)S(1)} %bitcast.29, f32[80,200]{1,0:T(8,128)S(1)} %copy-done.3), custom_call_target="tpu_custom_call" | custom-call | flops 12000000000 | bytes 23068672 | tf_op jit(solution)/shard_map/lon_partial/pallas_call | solution.py:287
  60.9 0.1 collective-permute-start.2
  60.9 1.5 %collective-permute-done.2 = f32[4,2,32,200]{3,2,1,0:T(8,128)S(1)} collective-permute-done((f32[4,2,32,200]{3,2,1,0:T(8,128)S(1)}, f32[4,2,32,200]{3,2,1,0:T(8,128)S(1)}, u32[]{:S(2)}, u32[]{:S(2)}) %collective-permute-start.2) | collective-permute-done | bytes 204832 | tf_op jit(solution)/shard_map/ppermute | solution.py:369
  62.5 1.6 %collective-permute-start.3 = (f32[2,32,200]{2,1,0:T(8,128)S(1)}, f32[2,32,200]{2,1,0:T(8,128)S(1)}, u32[]{:S(2)}, u32[]{:S(2)}) collective-permute-start(f32[2,32,200]{2,1,0:T(8,128)S(1)} %get-tuple-element.38), channel_id=1, source_target_pairs={{0,2},{1,3},{2,4},{3,5},{4,6},{5,7},{6,0},{7,1},{8,10},{9,11},{10,... | collective-permute-start | bytes 153608 | tf_op jit(solution)/shard_map/ppermute | solution.py:372
  64.2 1.7 %collective-permute-start.5 = (f32[2,32,200]{2,1,0:T(8,128)S(1)}, f32[2,32,200]{2,1,0:T(8,128)S(1)}, u32[]{:S(2)}, u32[]{:S(2)}) collective-permute-start(f32[2,32,200]{2,1,0:T(8,128)S(1)} %get-tuple-element.39), channel_id=1, source_target_pairs={{0,6},{1,7},{2,0},{3,1},{4,2},{5,3},{6,4},{7,5},{8,14},{9,15},{10,... | collective-permute-start | bytes 153608 | tf_op jit(solution)/shard_map/ppermute | solution.py:372
  65.8 1.9 %collective-permute-start.4 = (f32[2,32,200]{2,1,0:T(8,128)S(1)}, f32[2,32,200]{2,1,0:T(8,128)S(1)}, u32[]{:S(2)}, u32[]{:S(2)}) collective-permute-start(f32[2,32,200]{2,1,0:T(8,128)S(1)} %get-tuple-element.40), channel_id=1, source_target_pairs={{0,4},{1,5},{2,6},{3,7},{4,0},{5,1},{6,2},{7,3},{8,12},{9,13},{10,... | collective-permute-start | bytes 153608 | tf_op jit(solution)/shard_map/ppermute | solution.py:372
  67.7 4.7 %collective-permute-done.3 = f32[2,32,200]{2,1,0:T(8,128)S(1)} collective-permute-done((f32[2,32,200]{2,1,0:T(8,128)S(1)}, f32[2,32,200]{2,1,0:T(8,128)S(1)}, u32[]{:S(2)}, u32[]{:S(2)}) %collective-permute-start.3) | collective-permute-done | bytes 51232 | tf_op jit(solution)/shard_map/ppermute | solution.py:372
  72.4 2.3 %collective-permute-done.5 = f32[2,32,200]{2,1,0:T(8,128)S(1)} collective-permute-done((f32[2,32,200]{2,1,0:T(8,128)S(1)}, f32[2,32,200]{2,1,0:T(8,128)S(1)}, u32[]{:S(2)}, u32[]{:S(2)}) %collective-permute-start.5) | collective-permute-done | bytes 51232 | tf_op jit(solution)/shard_map/ppermute | solution.py:372
  74.7 1.9 %collective-permute-done.4 = f32[2,32,200]{2,1,0:T(8,128)S(1)} collective-permute-done((f32[2,32,200]{2,1,0:T(8,128)S(1)}, f32[2,32,200]{2,1,0:T(8,128)S(1)}, u32[]{:S(2)}, u32[]{:S(2)}) %collective-permute-start.4) | collective-permute-done | bytes 51232 | tf_op jit(solution)/shard_map/ppermute | solution.py:372
  76.6 0.8 all-to-all-done.1.parts_ref
  77.3 1.8 %collective-permute-start.6 = (f32[32,200]{1,0:T(8,128)S(1)}, f32[32,200]{1,0:T(8,128)S(1)}, u32[]{:S(2)}, u32[]{:S(2)}) collective-permute-start(f32[32,200]{1,0:T(8,128)S(1)} %slice_bitcast_fusion.4), channel_id=1, source_target_pairs={{0,8},{1,9},{2,10},{3,11},{4,12},{5,13},{6,14},{7,15},{8,0},{9,1},... | collective-permute-start | bytes 76808 | tf_op jit(solution)/shard_map/ppermute | solution.py:374
  79.2 1.0 %finish.1 = (f32[12,6,96]{2,1,0:T(8,128)}, f32[200,128]{1,0:T(8,128)}, f32[80,200]{1,0:T(8,128)}) custom-call(f32[64,56,128]{2,1,0:T(8,128)S(1)} %all-to-all-done.1.parts_ref, f32[80,96]{1,0:T(8,128)S(1)} %bitcast.27), custom_call_target="tpu_custom_call" | custom-call | flops 100000000 | bytes 2097152 | tf_op jit(solution)/shard_map/finish/pallas_call | solution.py:324
  80.1 1.1 %collective-permute-done.6 = f32[32,200]{1,0:T(8,128)S(1)} collective-permute-done((f32[32,200]{1,0:T(8,128)S(1)}, f32[32,200]{1,0:T(8,128)S(1)}, u32[]{:S(2)}, u32[]{:S(2)}) %collective-permute-start.6) | collective-permute-done | bytes 25632 | tf_op jit(solution)/shard_map/ppermute | solution.py:374
  81.3 0.6 bitcast_add_fusion
  (17 shorter events, 0.1 us)
Async XLA Ops:
  0.6 27.8 %copy-start.4 = (f32[96,128]{1,0:T(8,128)S(1)}, f32[96,128]{1,0:T(8,128)}, u32[]{:S(2)}) copy-start(f32[96,128]{1,0:T(8,128)} %lat_ref.1) | copy-start | bytes 147460
  17.3 22.1 %all-to-all-start = ((f32[128,1,4,128]{3,2,1,0:T(4,128)}), f32[128,1,4,128]{3,2,1,0:T(4,128)S(1)}, u32[]{:S(2)}, u32[]{:S(2)}) async-start(f32[128,1,4,128]{3,2,1,0:T(4,128)} %get-tuple-element.21), calls=%async_computation | async-start | bytes 524288 | tf_op jit(solution)/shard_map/all_to_all | solution.py:357
  28.4 2.1 %copy-start.5 = (f32[96,5,16,128]{3,2,1,0:T(8,128)S(1)}, f32[96,5,16,128]{3,2,1,0:T(8,128)}, u32[]{:S(2)}) copy-start(f32[96,5,16,128]{3,2,1,0:T(8,128)} %get-tuple-element.22.crossed) | copy-start | bytes 11796484
  39.4 3.4 %collective-permute-start = (f32[8,8,48,128]{3,2,1,0:T(8,128)S(1)}, f32[8,8,48,128]{3,2,1,0:T(8,128)S(1)}, u32[]{:S(2)}, u32[]{:S(2)}) collective-permute-start(f32[8,8,48,128]{3,2,1,0:T(8,128)S(1)} %get-tuple-element.26), channel_id=1, source_target_pairs={{0,1},{1,0},{2,3},{3,2},{4,5},{5,4},{6,7},{7,6},{8,9},{9,8},{10,11... | collective-permute-start | bytes 4718600 | tf_op jit(solution)/shard_map/ppermute | solution.py:360
  39.4 3.4 %collective-permute-start.1 = (f32[5,8,128]{2,1,0:T(8,128)S(1)}, f32[5,8,128]{2,1,0:T(8,128)S(1)}, u32[]{:S(2)}, u32[]{:S(2)}) collective-permute-start(f32[5,8,128]{2,1,0:T(8,128)S(1)} %get-tuple-element.29), channel_id=1, source_target_pairs={{0,1},{1,0},{2,3},{3,2},{4,5},{5,4},{6,7},{7,6},{8,9},{9,8},{10,11... | collective-permute-start | bytes 61448 | tf_op jit(solution)/shard_map/ppermute | solution.py:362
  43.0 1.3 %copy-start = (f32[64,56,128]{2,1,0:T(8,128)}, f32[64,56,128]{2,1,0:T(8,128)S(1)}, u32[]{:S(2)}) copy-start(f32[64,56,128]{2,1,0:T(8,128)S(1)} %join_shares.1) | copy-start | bytes 5505028
  44.3 5.1 %copy-start.2 = (f32[128,200]{0,1:T(8,128)S(1)}, f32[128,200]{0,1:T(8,128)}, u32[]{:S(2)}) copy-start(f32[128,200]{0,1:T(8,128)} %param.9) | copy-start | bytes 307204
  44.3 5.2 %copy-start.3 = (f32[80,200]{1,0:T(8,128)S(1)}, f32[80,200]{1,0:T(8,128)}, u32[]{:S(2)}) copy-start(f32[80,200]{1,0:T(8,128)} %time_ref.1) | copy-start | bytes 192004
  44.3 33.1 %all-to-all-start.1 = ((f32[64,56,128]{2,1,0:T(8,128)}), f32[64,56,128]{2,1,0:T(8,128)S(1)}, u32[]{:S(2)}, u32[]{:S(2)}) async-start(f32[64,56,128]{2,1,0:T(8,128)} %copy-done), calls=%async_computation.1 | async-start | bytes 3670016 | tf_op jit(solution)/shard_map/all_to_all | solution.py:365
  49.4 29.7 %copy-start.1 = (f32[96,80]{0,1:T(8,128)S(1)}, f32[96,80]{0,1:T(8,128)}, u32[]{:S(2)}) copy-start(f32[96,80]{0,1:T(8,128)} %param.13) | copy-start | bytes 92164
  60.9 1.6 %collective-permute-start.2 = (f32[4,2,32,200]{3,2,1,0:T(8,128)S(1)}, f32[4,2,32,200]{3,2,1,0:T(8,128)S(1)}, u32[]{:S(2)}, u32[]{:S(2)}) collective-permute-start(f32[4,2,32,200]{3,2,1,0:T(8,128)S(1)} %get-tuple-element.32), channel_id=1, source_target_pairs={{0,1},{1,0},{2,3},{3,2},{4,5},{5,4},{6,7},{7,6},{8,9},{9,8},{10,11... | collective-permute-start | bytes 614408 | tf_op jit(solution)/shard_map/ppermute | solution.py:369
  62.5 9.9 %collective-permute-start.3 = (f32[2,32,200]{2,1,0:T(8,128)S(1)}, f32[2,32,200]{2,1,0:T(8,128)S(1)}, u32[]{:S(2)}, u32[]{:S(2)}) collective-permute-start(f32[2,32,200]{2,1,0:T(8,128)S(1)} %get-tuple-element.38), channel_id=1, source_target_pairs={{0,2},{1,3},{2,4},{3,5},{4,6},{5,7},{6,0},{7,1},{8,10},{9,11},{10,... | collective-permute-start | bytes 153608 | tf_op jit(solution)/shard_map/ppermute | solution.py:372
  64.2 10.5 %collective-permute-start.5 = (f32[2,32,200]{2,1,0:T(8,128)S(1)}, f32[2,32,200]{2,1,0:T(8,128)S(1)}, u32[]{:S(2)}, u32[]{:S(2)}) collective-permute-start(f32[2,32,200]{2,1,0:T(8,128)S(1)} %get-tuple-element.39), channel_id=1, source_target_pairs={{0,6},{1,7},{2,0},{3,1},{4,2},{5,3},{6,4},{7,5},{8,14},{9,15},{10,... | collective-permute-start | bytes 153608 | tf_op jit(solution)/shard_map/ppermute | solution.py:372
  65.8 10.7 %collective-permute-start.4 = (f32[2,32,200]{2,1,0:T(8,128)S(1)}, f32[2,32,200]{2,1,0:T(8,128)S(1)}, u32[]{:S(2)}, u32[]{:S(2)}) collective-permute-start(f32[2,32,200]{2,1,0:T(8,128)S(1)} %get-tuple-element.40), channel_id=1, source_target_pairs={{0,4},{1,5},{2,6},{3,7},{4,0},{5,1},{6,2},{7,3},{8,12},{9,13},{10,... | collective-permute-start | bytes 153608 | tf_op jit(solution)/shard_map/ppermute | solution.py:372
  77.3 3.9 %collective-permute-start.6 = (f32[32,200]{1,0:T(8,128)S(1)}, f32[32,200]{1,0:T(8,128)S(1)}, u32[]{:S(2)}, u32[]{:S(2)}) collective-permute-start(f32[32,200]{1,0:T(8,128)S(1)} %slice_bitcast_fusion.4), channel_id=1, source_target_pairs={{0,8},{1,9},{2,10},{3,11},{4,12},{5,13},{6,14},{7,15},{8,0},{9,1},... | collective-permute-start | bytes 76808 | tf_op jit(solution)/shard_map/ppermute | solution.py:374

commit v6 on v5

--- a/solution.py
+++ b/solution.py
@@ -12,6 +12,7 @@
 VMEM = 48 * 1024 * 1024
 MOST_VMEM = 62 * 1024 * 1024
 MUCH_VMEM = 40 * 1024 * 1024
+MORE_VMEM = 50 * 1024 * 1024
 SLOTS = sorted(range(64), key=lambda chip: (chip // 16, chip % 4, chip // 8 % 2 * 2 + chip // 4 % 2))
 
 
@@ -184,7 +185,13 @@
     )(shares)
 
 
-def core_kernel(crossed, lat_ref, send_ref, keep_ref, lat_core):
+def core_kernel(crossed_hbm, lat_ref, send_ref, keep_ref, lat_core, crossed, arrived):
+    def crossed_copy(owner):
+        part = pl.ds(owner * 12, 12)
+        return pltpu.make_async_copy(crossed_hbm.at[part], crossed.at[part], arrived.at[owner])
+
+    for owner in range(8):
+        crossed_copy(owner).start()
     lat_core[:96] = lat_ref[...]
     lat_core[96:] = jnp.zeros((16, 128), F32)
 
@@ -202,6 +209,7 @@
     )
 
     def share(owner, carry):
+        crossed_copy(owner).wait()
         block = crossed[pl.ds(owner * 12, 12)].reshape(960, 128)
         block = jnp.concatenate([block, jnp.zeros((64, 128), F32)], axis=0)
         result = dot(lats, jnp.concatenate(halves(block), axis=1), ((1,), (1,)))
@@ -220,34 +228,46 @@
     part = jax.ShapeDtypeStruct((8, 8, 48, 128), F32)
     return pl.pallas_call(
         core_kernel,
-        in_specs=in_vmem(2),
+        in_specs=[pl.BlockSpec(memory_space=pl.ANY)] + in_vmem(1),
         out_specs=in_vmem(2),
         out_shape=[part, part],
-        scratch_shapes=[pltpu.VMEM((112, 128), F32)],
-        compiler_params=pltpu.CompilerParams(vmem_limit_bytes=MUCH_VMEM),
+        scratch_shapes=[
+            pltpu.VMEM((112, 128), F32),
+            pltpu.VMEM(crossed.shape, F32),
+            pltpu.SemaphoreType.DMA((8,)),
+        ],
+        compiler_params=pltpu.CompilerParams(vmem_limit_bytes=MORE_VMEM),
         cost_estimate=pl.CostEstimate(flops=20 * 10**9, bytes_accessed=8 << 20, transcendentals=0),
         name="core_partials",
     )(crossed, lat_core)
 
 
-def join_kernel(keep_ref, arrived_ref, mine_ref, other_ref, out_ref, sums):
+def join_kernel(keep_ref, arrived_ref, mine_ref, other_ref, out_hbm, out, sums, sent):
     sums[...] = mine_ref[...] + other_ref[...]
+    copies = []
     for slot, chip in enumerate(SLOTS):
         lat = chip % 8
         row = lat % 2 * 4
-        out_ref[slot, :48] = keep_ref[chip] + arrived_ref[chip]
-        out_ref[slot, 48:52] = sums[lat // 2, row : row + 4]
-        out_ref[slot, 52:] = sums[4, :4]
+        out[slot, :48] = keep_ref[chip] + arrived_ref[chip]
+        out[slot, 48:52] = sums[lat // 2, row : row + 4]
+        out[slot, 52:] = sums[4, :4]
+        if slot % 8 == 7:
+            piece = pl.ds(slot - 7, 8)
+            copies.append(pltpu.make_async_copy(out.at[piece], out_hbm.at[piece], sent.at[slot // 8]))
+            copies[-1].start()
+    for copy in copies:
+        copy.wait()
 
 
 def join_shares(keep, arrived, mine, other):
+    shape = (64, 56, 128)
     return pl.pallas_call(
         join_kernel,
         in_specs=in_vmem(4),
-        out_specs=pl.BlockSpec(memory_space=pltpu.VMEM),
-        out_shape=jax.ShapeDtypeStruct((64, 56, 128), F32),
-        scratch_shapes=[pltpu.VMEM(mine.shape, F32)],
-        compiler_params=pltpu.CompilerParams(vmem_limit_bytes=MUCH_VMEM),
+        out_specs=pl.BlockSpec(memory_space=pl.ANY),
+        out_shape=jax.ShapeDtypeStruct(shape, F32),
+        scratch_shapes=[pltpu.VMEM(shape, F32), pltpu.VMEM(mine.shape, F32), pltpu.SemaphoreType.DMA((8,))],
+        compiler_params=pltpu.CompilerParams(vmem_limit_bytes=MORE_VMEM),
         cost_estimate=pl.CostEstimate(flops=10**6, bytes_accessed=5 << 20, transcendentals=0),
         name="join_shares",
     )(keep, arrived, mine, other)

time: 82.4 us -> 82.2 us (level)
  local copies, waits for them, and re-layouts: 3.41 us -> 0.04 us
  Pallas kernels: 32.8 us -> 35 us
  waiting for transfers between devices: 20.3 us -> 21.4 us
    unnamed x12 -> x8, local copies, waits for them, and re-layouts: 3.39 us -> 0.02 us
    pallas_call x1, Pallas kernels: 0.19 us -> 1.35 us  [join_shares(): pl.pallas_call(join_kernel, in_specs=in_vmem(4), out_specs=pl.BlockSpec(m...]
    pallas_call x1, Pallas kernels: 3.59 us -> 4.69 us  [core_partials(): pl.pallas_call(core_kernel, in_specs=[pl.BlockSpec(memory_space=pl.ANY)]...]
    all_to_all x1, waiting for transfers between devices: 5.21 us -> 6.22 us  [on_device(): shares = lax.all_to_all(sums, BOTH, 0, 0)]
  transfers between devices with their start and end apart: 9 -> 9, of which waited for: 8 -> 8; matrix products, arithmetic and copies ran while one was open for 0% -> 0% of each run, Pallas kernels for 20% -> 21%
where the time goes in v6:
time: 82.2 us; the launch traced here: 81.7 us
  Pallas kernels  35 us (43%)
  starting transfers between devices  23.8 us (29%)
  waiting for transfers between devices  21.4 us (26%)
    pallas_call x1, Pallas kernels, first_partials(): pl.pallas_call(first_kernel, in_specs=in_hbm(5), out_specs=[pl.BlockSpec(...  16.6 us
    pallas_call x1, Pallas kernels, lon_partial(): pl.pallas_call(lon_kernel, in_specs=in_hbm(1) + in_vmem(2), out_specs=in_...  11.4 us
    all_to_all x1, starting transfers between devices, on_device(): shares = lax.all_to_all(sums, BOTH, 0, 0)  11.1 us
    ppermute x3, waiting for transfers between devices, on_device(): total = total + lax.ppermute(rows[step], BOTH, Z_STEPS[step])  9.2 us
    all_to_all x1, waiting for transfers between devices, on_device(): shares = lax.all_to_all(sums, BOTH, 0, 0)  6.22 us
    ppermute x3, starting transfers between devices, on_device(): total = total + lax.ppermute(rows[step], BOTH, Z_STEPS[step])  5.17 us
    all_to_all x1, starting transfers between devices, on_device(): parts = lax.all_to_all(chip, BOTH, 0, 0, axis_index_groups=CHIPS)  4.99 us
    pallas_call x1, Pallas kernels, core_partials(): pl.pallas_call(core_kernel, in_specs=[pl.BlockSpec(memory_space=pl.ANY)]...  4.69 us
  transfers between devices with their start and end apart: 9, of which 8 were waited for; matrix products, arithmetic and copies ran while one was open for 0% of the time, Pallas kernels for 21%

profile of v6, /device:TPU:0, one launch (start us, length us, event | category | flops | bytes accessed | tf_op | source)
XLA Modules:
  0.0 81.7 jit_solution(1406507752590804888)
XLA Ops:
  0.6 16.6 %first_partials.1 = (f32[96,5,16,128]{3,2,1,0:T(8,128)}, f32[128,1,4,128]{3,2,1,0:T(4,128)}) custom-call(f32[80,512,128]{2,1,0:T(8,128)} %field_hbm.2, f32[96,512]{1,0:T(8,128)} %modes_hbm.1, f32[200,512]{1,0:T(8,128)} %bitcast.30, f32[200,128]{1,0:T(8,128)} %bitcast.28, f32[80,200]{1,0:T(8,128)} %time_ref.1), custom_call_target="tpu_custom_call" | custom-call | flops 17999998976 | bytes 27262976 | tf_op jit(solution)/shard_map/first_partials/pallas_call | solution.py:132
  17.2 11.1 %all-to-all-start = ((f32[128,1,4,128]{3,2,1,0:T(4,128)}), f32[128,1,4,128]{3,2,1,0:T(4,128)S(1)}, u32[]{:S(2)}, u32[]{:S(2)}) async-start(f32[128,1,4,128]{3,2,1,0:T(4,128)} %get-tuple-element.21), calls=%async_computation | async-start | bytes 524288 | tf_op jit(solution)/shard_map/all_to_all | solution.py:377
  28.4 4.7 %core_partials.1 = (f32[8,8,48,128]{3,2,1,0:T(8,128)S(1)}, f32[8,8,48,128]{3,2,1,0:T(8,128)S(1)}) custom-call(f32[96,5,16,128]{3,2,1,0:T(8,128)} %get-tuple-element.22.crossed_hbm, f32[96,128]{1,0:T(8,128)S(1)} %copy-done.3), custom_call_target="tpu_custom_call" | custom-call | flops 20000000000 | bytes 8388608 | tf_op jit(solution)/shard_map/core_partials/pallas_call | solution.py:229
  33.1 6.2 %all-to-all-done.shares_ref = f32[128,1,4,128]{3,2,1,0:T(4,128)S(1)} async-done(((f32[128,1,4,128]{3,2,1,0:T(4,128)}), f32[128,1,4,128]{3,2,1,0:T(4,128)S(1)}, u32[]{:S(2)}, u32[]{:S(2)}) %all-to-all-start) | async-done | bytes 262176 | tf_op jit(solution)/shard_map/all_to_all | solution.py:377
  39.3 0.6 collective-permute-start.1
  39.9 2.8 %collective-permute-done.1.other_ref = f32[5,8,128]{2,1,0:T(8,128)S(1)} collective-permute-done((f32[5,8,128]{2,1,0:T(8,128)S(1)}, f32[5,8,128]{2,1,0:T(8,128)S(1)}, u32[]{:S(2)}, u32[]{:S(2)}) %collective-permute-start.1) | collective-permute-done | bytes 20512 | tf_op jit(solution)/shard_map/ppermute | solution.py:382
  42.7 1.3 %join_shares.1 = f32[64,56,128]{2,1,0:T(8,128)} custom-call(f32[64,48,128]{2,1,0:T(8,128)S(1)} %bitcast.25, f32[64,48,128]{2,1,0:T(8,128)S(1)} %bitcast.26, f32[5,8,128]{2,1,0:T(8,128)S(1)} %get-tuple-element.28.mine_ref, f32[5,8,128]{2,1,0:T(8,128)S(1)} %collective-permute-done.1.other_ref), custom_call_target="tpu_custom_call" | custom-call | flops 1000000 | bytes 5242880 | tf_op jit(solution)/shard_map/join_shares/pallas_call | solution.py:264
  44.1 0.0 copy-start.1
  44.1 5.0 %all-to-all-start.1 = ((f32[64,56,128]{2,1,0:T(8,128)}), f32[64,56,128]{2,1,0:T(8,128)S(1)}, u32[]{:S(2)}, u32[]{:S(2)}) async-start(f32[64,56,128]{2,1,0:T(8,128)} %join_shares.1), calls=%async_computation.1 | async-start | bytes 3670016 | tf_op jit(solution)/shard_map/all_to_all | solution.py:385
  49.1 0.0 copy-start
  49.1 11.4 %lon_partial.1 = (f32[4,2,32,200]{3,2,1,0:T(8,128)S(1)}, f32[4,2,32,200]{3,2,1,0:T(8,128)S(1)}) custom-call(f32[80,512,128]{2,1,0:T(8,128)} %field_hbm.2, f32[200,128]{1,0:T(8,128)S(1)} %bitcast.29, f32[80,200]{1,0:T(8,128)S(1)} %copy-done.2), custom_call_target="tpu_custom_call" | custom-call | flops 12000000000 | bytes 23068672 | tf_op jit(solution)/shard_map/lon_partial/pallas_call | solution.py:307
  60.6 0.1 collective-permute-start.2
  60.6 1.5 %collective-permute-done.2 = f32[4,2,32,200]{3,2,1,0:T(8,128)S(1)} collective-permute-done((f32[4,2,32,200]{3,2,1,0:T(8,128)S(1)}, f32[4,2,32,200]{3,2,1,0:T(8,128)S(1)}, u32[]{:S(2)}, u32[]{:S(2)}) %collective-permute-start.2) | collective-permute-done | bytes 204832 | tf_op jit(solution)/shard_map/ppermute | solution.py:389
  62.2 1.6 %collective-permute-start.3 = (f32[2,32,200]{2,1,0:T(8,128)S(1)}, f32[2,32,200]{2,1,0:T(8,128)S(1)}, u32[]{:S(2)}, u32[]{:S(2)}) collective-permute-start(f32[2,32,200]{2,1,0:T(8,128)S(1)} %get-tuple-element.38), channel_id=1, source_target_pairs={{0,2},{1,3},{2,4},{3,5},{4,6},{5,7},{6,0},{7,1},{8,10},{9,11},{10,... | collective-permute-start | bytes 153608 | tf_op jit(solution)/shard_map/ppermute | solution.py:392
  63.9 1.7 %collective-permute-start.5 = (f32[2,32,200]{2,1,0:T(8,128)S(1)}, f32[2,32,200]{2,1,0:T(8,128)S(1)}, u32[]{:S(2)}, u32[]{:S(2)}) collective-permute-start(f32[2,32,200]{2,1,0:T(8,128)S(1)} %get-tuple-element.39), channel_id=1, source_target_pairs={{0,6},{1,7},{2,0},{3,1},{4,2},{5,3},{6,4},{7,5},{8,14},{9,15},{10,... | collective-permute-start | bytes 153608 | tf_op jit(solution)/shard_map/ppermute | solution.py:392
  65.5 1.9 %collective-permute-start.4 = (f32[2,32,200]{2,1,0:T(8,128)S(1)}, f32[2,32,200]{2,1,0:T(8,128)S(1)}, u32[]{:S(2)}, u32[]{:S(2)}) collective-permute-start(f32[2,32,200]{2,1,0:T(8,128)S(1)} %get-tuple-element.40), channel_id=1, source_target_pairs={{0,4},{1,5},{2,6},{3,7},{4,0},{5,1},{6,2},{7,3},{8,12},{9,13},{10,... | collective-permute-start | bytes 153608 | tf_op jit(solution)/shard_map/ppermute | solution.py:392
  67.4 4.9 %collective-permute-done.3 = f32[2,32,200]{2,1,0:T(8,128)S(1)} collective-permute-done((f32[2,32,200]{2,1,0:T(8,128)S(1)}, f32[2,32,200]{2,1,0:T(8,128)S(1)}, u32[]{:S(2)}, u32[]{:S(2)}) %collective-permute-start.3) | collective-permute-done | bytes 51232 | tf_op jit(solution)/shard_map/ppermute | solution.py:392
  72.3 2.2 %collective-permute-done.5 = f32[2,32,200]{2,1,0:T(8,128)S(1)} collective-permute-done((f32[2,32,200]{2,1,0:T(8,128)S(1)}, f32[2,32,200]{2,1,0:T(8,128)S(1)}, u32[]{:S(2)}, u32[]{:S(2)}) %collective-permute-start.5) | collective-permute-done | bytes 51232 | tf_op jit(solution)/shard_map/ppermute | solution.py:392
  74.5 2.1 %collective-permute-done.4 = f32[2,32,200]{2,1,0:T(8,128)S(1)} collective-permute-done((f32[2,32,200]{2,1,0:T(8,128)S(1)}, f32[2,32,200]{2,1,0:T(8,128)S(1)}, u32[]{:S(2)}, u32[]{:S(2)}) %collective-permute-start.4) | collective-permute-done | bytes 51232 | tf_op jit(solution)/shard_map/ppermute | solution.py:392
  76.6 0.5 all-to-all-done.1.parts_ref
  77.2 1.8 %collective-permute-start.6 = (f32[32,200]{1,0:T(8,128)S(1)}, f32[32,200]{1,0:T(8,128)S(1)}, u32[]{:S(2)}, u32[]{:S(2)}) collective-permute-start(f32[32,200]{1,0:T(8,128)S(1)} %slice_bitcast_fusion.4), channel_id=1, source_target_pairs={{0,8},{1,9},{2,10},{3,11},{4,12},{5,13},{6,14},{7,15},{8,0},{9,1},... | collective-permute-start | bytes 76808 | tf_op jit(solution)/shard_map/ppermute | solution.py:394
  79.0 1.0 %finish.1 = (f32[12,6,96]{2,1,0:T(8,128)}, f32[200,128]{1,0:T(8,128)}, f32[80,200]{1,0:T(8,128)}) custom-call(f32[64,56,128]{2,1,0:T(8,128)S(1)} %all-to-all-done.1.parts_ref, f32[80,96]{1,0:T(8,128)S(1)} %bitcast.27), custom_call_target="tpu_custom_call" | custom-call | flops 100000000 | bytes 2097152 | tf_op jit(solution)/shard_map/finish/pallas_call | solution.py:344
  80.0 1.1 %collective-permute-done.6 = f32[32,200]{1,0:T(8,128)S(1)} collective-permute-done((f32[32,200]{1,0:T(8,128)S(1)}, f32[32,200]{1,0:T(8,128)S(1)}, u32[]{:S(2)}, u32[]{:S(2)}) %collective-permute-start.6) | collective-permute-done | bytes 25632 | tf_op jit(solution)/shard_map/ppermute | solution.py:394
  81.1 0.6 bitcast_add_fusion
  (13 shorter events, 0.1 us)
Async XLA Ops:
  0.6 27.7 %copy-start.3 = (f32[96,128]{1,0:T(8,128)S(1)}, f32[96,128]{1,0:T(8,128)}, u32[]{:S(2)}) copy-start(f32[96,128]{1,0:T(8,128)} %lat_ref.1) | copy-start | bytes 147460
  17.2 22.1 %all-to-all-start = ((f32[128,1,4,128]{3,2,1,0:T(4,128)}), f32[128,1,4,128]{3,2,1,0:T(4,128)S(1)}, u32[]{:S(2)}, u32[]{:S(2)}) async-start(f32[128,1,4,128]{3,2,1,0:T(4,128)} %get-tuple-element.21), calls=%async_computation | async-start | bytes 524288 | tf_op jit(solution)/shard_map/all_to_all | solution.py:377
  39.3 3.4 %collective-permute-start = (f32[8,8,48,128]{3,2,1,0:T(8,128)S(1)}, f32[8,8,48,128]{3,2,1,0:T(8,128)S(1)}, u32[]{:S(2)}, u32[]{:S(2)}) collective-permute-start(f32[8,8,48,128]{3,2,1,0:T(8,128)S(1)} %get-tuple-element.26), channel_id=1, source_target_pairs={{0,1},{1,0},{2,3},{3,2},{4,5},{5,4},{6,7},{7,6},{8,9},{9,8},{10,11... | collective-permute-start | bytes 4718600 | tf_op jit(solution)/shard_map/ppermute | solution.py:380
  39.3 3.4 %collective-permute-start.1 = (f32[5,8,128]{2,1,0:T(8,128)S(1)}, f32[5,8,128]{2,1,0:T(8,128)S(1)}, u32[]{:S(2)}, u32[]{:S(2)}) collective-permute-start(f32[5,8,128]{2,1,0:T(8,128)S(1)} %get-tuple-element.29), channel_id=1, source_target_pairs={{0,1},{1,0},{2,3},{3,2},{4,5},{5,4},{6,7},{7,6},{8,9},{9,8},{10,11... | collective-permute-start | bytes 61448 | tf_op jit(solution)/shard_map/ppermute | solution.py:382
  44.1 5.0 %copy-start.1 = (f32[128,200]{0,1:T(8,128)S(1)}, f32[128,200]{0,1:T(8,128)}, u32[]{:S(2)}) copy-start(f32[128,200]{0,1:T(8,128)} %param.9) | copy-start | bytes 307204
  44.1 5.0 %copy-start.2 = (f32[80,200]{1,0:T(8,128)S(1)}, f32[80,200]{1,0:T(8,128)}, u32[]{:S(2)}) copy-start(f32[80,200]{1,0:T(8,128)} %time_ref.1) | copy-start | bytes 192004
  44.1 33.0 %all-to-all-start.1 = ((f32[64,56,128]{2,1,0:T(8,128)}), f32[64,56,128]{2,1,0:T(8,128)S(1)}, u32[]{:S(2)}, u32[]{:S(2)}) async-start(f32[64,56,128]{2,1,0:T(8,128)} %join_shares.1), calls=%async_computation.1 | async-start | bytes 3670016 | tf_op jit(solution)/shard_map/all_to_all | solution.py:385
  49.1 29.9 %copy-start = (f32[96,80]{0,1:T(8,128)S(1)}, f32[96,80]{0,1:T(8,128)}, u32[]{:S(2)}) copy-start(f32[96,80]{0,1:T(8,128)} %param.13) | copy-start | bytes 92164
  60.6 1.6 %collective-permute-start.2 = (f32[4,2,32,200]{3,2,1,0:T(8,128)S(1)}, f32[4,2,32,200]{3,2,1,0:T(8,128)S(1)}, u32[]{:S(2)}, u32[]{:S(2)}) collective-permute-start(f32[4,2,32,200]{3,2,1,0:T(8,128)S(1)} %get-tuple-element.32), channel_id=1, source_target_pairs={{0,1},{1,0},{2,3},{3,2},{4,5},{5,4},{6,7},{7,6},{8,9},{9,8},{10,11... | collective-permute-start | bytes 614408 | tf_op jit(solution)/shard_map/ppermute | solution.py:389
  62.2 10.1 %collective-permute-start.3 = (f32[2,32,200]{2,1,0:T(8,128)S(1)}, f32[2,32,200]{2,1,0:T(8,128)S(1)}, u32[]{:S(2)}, u32[]{:S(2)}) collective-permute-start(f32[2,32,200]{2,1,0:T(8,128)S(1)} %get-tuple-element.38), channel_id=1, source_target_pairs={{0,2},{1,3},{2,4},{3,5},{4,6},{5,7},{6,0},{7,1},{8,10},{9,11},{10,... | collective-permute-start | bytes 153608 | tf_op jit(solution)/shard_map/ppermute | solution.py:392
  63.9 10.6 %collective-permute-start.5 = (f32[2,32,200]{2,1,0:T(8,128)S(1)}, f32[2,32,200]{2,1,0:T(8,128)S(1)}, u32[]{:S(2)}, u32[]{:S(2)}) collective-permute-start(f32[2,32,200]{2,1,0:T(8,128)S(1)} %get-tuple-element.39), channel_id=1, source_target_pairs={{0,6},{1,7},{2,0},{3,1},{4,2},{5,3},{6,4},{7,5},{8,14},{9,15},{10,... | collective-permute-start | bytes 153608 | tf_op jit(solution)/shard_map/ppermute | solution.py:392
  65.5 11.1 %collective-permute-start.4 = (f32[2,32,200]{2,1,0:T(8,128)S(1)}, f32[2,32,200]{2,1,0:T(8,128)S(1)}, u32[]{:S(2)}, u32[]{:S(2)}) collective-permute-start(f32[2,32,200]{2,1,0:T(8,128)S(1)} %get-tuple-element.40), channel_id=1, source_target_pairs={{0,4},{1,5},{2,6},{3,7},{4,0},{5,1},{6,2},{7,3},{8,12},{9,13},{10,... | collective-permute-start | bytes 153608 | tf_op jit(solution)/shard_map/ppermute | solution.py:392
  77.2 3.9 %collective-permute-start.6 = (f32[32,200]{1,0:T(8,128)S(1)}, f32[32,200]{1,0:T(8,128)S(1)}, u32[]{:S(2)}, u32[]{:S(2)}) collective-permute-start(f32[32,200]{1,0:T(8,128)S(1)} %slice_bitcast_fusion.4), channel_id=1, source_target_pairs={{0,8},{1,9},{2,10},{3,11},{4,12},{5,13},{6,14},{7,15},{8,0},{9,1},... | collective-permute-start | bytes 76808 | tf_op jit(solution)/shard_map/ppermute | solution.py:394

commit v7 on v6

--- a/solution.py
+++ b/solution.py
@@ -43,6 +43,11 @@
 def each_block(field_hbm, field, arrived, work):
     def step(at, carry):
         block_copy(field_hbm, field, arrived, at).wait()
+
+        @pl.when(at + 2 < arrived.shape[0])
+        def _():
+            block_copy(field_hbm, field, arrived, at + 2).start()
+
         work(at)
         return carry
 
@@ -92,7 +97,7 @@
         total[...] = jnp.zeros_like(total)
     for copy in waits:
         copy.wait()
-    start_field(field_hbm, field, arrived, range(1, arrived.shape[0]))
+    start_field(field_hbm, field, arrived, range(1, 2))
     split_rows(jnp.concatenate([lon_core[...], lon_test[...]], axis=0), weights)
 
     def crossed_copy(at):
@@ -274,7 +279,7 @@
 
 
 def lon_kernel(field_hbm, lat_ref, time_ref, keep_ref, send_ref, field, arrived, lat_test, total):
-    start_field(field_hbm, field, arrived, range(arrived.shape[0]))
+    start_field(field_hbm, field, arrived, range(2))
     total[...] = jnp.zeros_like(total)
     lat_test[...] = lat_ref[...].T
     lons = total.shape[0]

time: 82.2 us -> 82.3 us (level)
  no operation moved by 1% of the time
where the time goes in v7:
time: 82.3 us; the launch traced here: 81.8 us
  Pallas kernels  35.1 us (43%)
  starting transfers between devices  23.8 us (29%)
  waiting for transfers between devices  21.4 us (26%)
    pallas_call x1, Pallas kernels, first_partials(): pl.pallas_call(first_kernel, in_specs=in_hbm(5), out_specs=[pl.BlockSpec(...  16.6 us
    pallas_call x1, Pallas kernels, lon_partial(): pl.pallas_call(lon_kernel, in_specs=in_hbm(1) + in_vmem(2), out_specs=in_...  11.4 us
    all_to_all x1, starting transfers between devices, on_device(): shares = lax.all_to_all(sums, BOTH, 0, 0)  11.2 us
    ppermute x3, waiting for transfers between devices, on_device(): total = total + lax.ppermute(rows[step], BOTH, Z_STEPS[step])  9.23 us
    all_to_all x1, waiting for transfers between devices, on_device(): shares = lax.all_to_all(sums, BOTH, 0, 0)  6.22 us
    ppermute x3, starting transfers between devices, on_device(): total = total + lax.ppermute(rows[step], BOTH, Z_STEPS[step])  5.17 us
    all_to_all x1, starting transfers between devices, on_device(): parts = lax.all_to_all(chip, BOTH, 0, 0, axis_index_groups=CHIPS)  4.99 us
    pallas_call x1, Pallas kernels, core_partials(): pl.pallas_call(core_kernel, in_specs=[pl.BlockSpec(memory_space=pl.ANY)]...  4.69 us
  transfers between devices with their start and end apart: 9, of which 8 were waited for; matrix products, arithmetic and copies ran while one was open for 0% of the time, Pallas kernels for 21%

profile of v7, /device:TPU:0, one launch (start us, length us, event | category | flops | bytes accessed | tf_op | source)
XLA Modules:
  0.0 81.8 jit_solution(8662977875782234957)
XLA Ops:
  0.6 16.6 %first_partials.1 = (f32[96,5,16,128]{3,2,1,0:T(8,128)}, f32[128,1,4,128]{3,2,1,0:T(4,128)}) custom-call(f32[80,512,128]{2,1,0:T(8,128)} %field_hbm.2, f32[96,512]{1,0:T(8,128)} %modes_hbm.1, f32[200,512]{1,0:T(8,128)} %bitcast.30, f32[200,128]{1,0:T(8,128)} %bitcast.28, f32[80,200]{1,0:T(8,128)} %time_ref.1), custom_call_target="tpu_custom_call" | custom-call | flops 17999998976 | bytes 27262976 | tf_op jit(solution)/shard_map/first_partials/pallas_call | solution.py:137
  17.3 11.2 %all-to-all-start = ((f32[128,1,4,128]{3,2,1,0:T(4,128)}), f32[128,1,4,128]{3,2,1,0:T(4,128)S(1)}, u32[]{:S(2)}, u32[]{:S(2)}) async-start(f32[128,1,4,128]{3,2,1,0:T(4,128)} %get-tuple-element.21), calls=%async_computation | async-start | bytes 524288 | tf_op jit(solution)/shard_map/all_to_all | solution.py:382
  28.5 4.7 %core_partials.1 = (f32[8,8,48,128]{3,2,1,0:T(8,128)S(1)}, f32[8,8,48,128]{3,2,1,0:T(8,128)S(1)}) custom-call(f32[96,5,16,128]{3,2,1,0:T(8,128)} %get-tuple-element.22.crossed_hbm, f32[96,128]{1,0:T(8,128)S(1)} %copy-done.3), custom_call_target="tpu_custom_call" | custom-call | flops 20000000000 | bytes 8388608 | tf_op jit(solution)/shard_map/core_partials/pallas_call | solution.py:234
  33.2 6.2 %all-to-all-done.shares_ref = f32[128,1,4,128]{3,2,1,0:T(4,128)S(1)} async-done(((f32[128,1,4,128]{3,2,1,0:T(4,128)}), f32[128,1,4,128]{3,2,1,0:T(4,128)S(1)}, u32[]{:S(2)}, u32[]{:S(2)}) %all-to-all-start) | async-done | bytes 262176 | tf_op jit(solution)/shard_map/all_to_all | solution.py:382
  39.4 0.6 collective-permute-start.1
  40.0 2.8 %collective-permute-done.1.other_ref = f32[5,8,128]{2,1,0:T(8,128)S(1)} collective-permute-done((f32[5,8,128]{2,1,0:T(8,128)S(1)}, f32[5,8,128]{2,1,0:T(8,128)S(1)}, u32[]{:S(2)}, u32[]{:S(2)}) %collective-permute-start.1) | collective-permute-done | bytes 20512 | tf_op jit(solution)/shard_map/ppermute | solution.py:387
  42.8 1.3 %join_shares.1 = f32[64,56,128]{2,1,0:T(8,128)} custom-call(f32[64,48,128]{2,1,0:T(8,128)S(1)} %bitcast.25, f32[64,48,128]{2,1,0:T(8,128)S(1)} %bitcast.26, f32[5,8,128]{2,1,0:T(8,128)S(1)} %get-tuple-element.28.mine_ref, f32[5,8,128]{2,1,0:T(8,128)S(1)} %collective-permute-done.1.other_ref), custom_call_target="tpu_custom_call" | custom-call | flops 1000000 | bytes 5242880 | tf_op jit(solution)/shard_map/join_shares/pallas_call | solution.py:269
  44.2 0.0 copy-start.1
  44.2 0.0 copy-start.2
  44.2 5.0 %all-to-all-start.1 = ((f32[64,56,128]{2,1,0:T(8,128)}), f32[64,56,128]{2,1,0:T(8,128)S(1)}, u32[]{:S(2)}, u32[]{:S(2)}) async-start(f32[64,56,128]{2,1,0:T(8,128)} %join_shares.1), calls=%async_computation.1 | async-start | bytes 3670016 | tf_op jit(solution)/shard_map/all_to_all | solution.py:390
  49.2 11.4 %lon_partial.1 = (f32[4,2,32,200]{3,2,1,0:T(8,128)S(1)}, f32[4,2,32,200]{3,2,1,0:T(8,128)S(1)}) custom-call(f32[80,512,128]{2,1,0:T(8,128)} %field_hbm.2, f32[200,128]{1,0:T(8,128)S(1)} %bitcast.29, f32[80,200]{1,0:T(8,128)S(1)} %copy-done.2), custom_call_target="tpu_custom_call" | custom-call | flops 12000000000 | bytes 23068672 | tf_op jit(solution)/shard_map/lon_partial/pallas_call | solution.py:312
  60.6 0.1 collective-permute-start.2
  60.7 1.5 %collective-permute-done.2 = f32[4,2,32,200]{3,2,1,0:T(8,128)S(1)} collective-permute-done((f32[4,2,32,200]{3,2,1,0:T(8,128)S(1)}, f32[4,2,32,200]{3,2,1,0:T(8,128)S(1)}, u32[]{:S(2)}, u32[]{:S(2)}) %collective-permute-start.2) | collective-permute-done | bytes 204832 | tf_op jit(solution)/shard_map/ppermute | solution.py:394
  62.3 1.6 %collective-permute-start.3 = (f32[2,32,200]{2,1,0:T(8,128)S(1)}, f32[2,32,200]{2,1,0:T(8,128)S(1)}, u32[]{:S(2)}, u32[]{:S(2)}) collective-permute-start(f32[2,32,200]{2,1,0:T(8,128)S(1)} %get-tuple-element.38), channel_id=1, source_target_pairs={{0,2},{1,3},{2,4},{3,5},{4,6},{5,7},{6,0},{7,1},{8,10},{9,11},{10,... | collective-permute-start | bytes 153608 | tf_op jit(solution)/shard_map/ppermute | solution.py:397
  63.9 1.7 %collective-permute-start.5 = (f32[2,32,200]{2,1,0:T(8,128)S(1)}, f32[2,32,200]{2,1,0:T(8,128)S(1)}, u32[]{:S(2)}, u32[]{:S(2)}) collective-permute-start(f32[2,32,200]{2,1,0:T(8,128)S(1)} %get-tuple-element.39), channel_id=1, source_target_pairs={{0,6},{1,7},{2,0},{3,1},{4,2},{5,3},{6,4},{7,5},{8,14},{9,15},{10,... | collective-permute-start | bytes 153608 | tf_op jit(solution)/shard_map/ppermute | solution.py:397
  65.6 1.9 %collective-permute-start.4 = (f32[2,32,200]{2,1,0:T(8,128)S(1)}, f32[2,32,200]{2,1,0:T(8,128)S(1)}, u32[]{:S(2)}, u32[]{:S(2)}) collective-permute-start(f32[2,32,200]{2,1,0:T(8,128)S(1)} %get-tuple-element.40), channel_id=1, source_target_pairs={{0,4},{1,5},{2,6},{3,7},{4,0},{5,1},{6,2},{7,3},{8,12},{9,13},{10,... | collective-permute-start | bytes 153608 | tf_op jit(solution)/shard_map/ppermute | solution.py:397
  67.5 5.0 %collective-permute-done.3 = f32[2,32,200]{2,1,0:T(8,128)S(1)} collective-permute-done((f32[2,32,200]{2,1,0:T(8,128)S(1)}, f32[2,32,200]{2,1,0:T(8,128)S(1)}, u32[]{:S(2)}, u32[]{:S(2)}) %collective-permute-start.3) | collective-permute-done | bytes 51232 | tf_op jit(solution)/shard_map/ppermute | solution.py:397
  72.4 2.2 %collective-permute-done.5 = f32[2,32,200]{2,1,0:T(8,128)S(1)} collective-permute-done((f32[2,32,200]{2,1,0:T(8,128)S(1)}, f32[2,32,200]{2,1,0:T(8,128)S(1)}, u32[]{:S(2)}, u32[]{:S(2)}) %collective-permute-start.5) | collective-permute-done | bytes 51232 | tf_op jit(solution)/shard_map/ppermute | solution.py:397
  74.6 2.1 %collective-permute-done.4 = f32[2,32,200]{2,1,0:T(8,128)S(1)} collective-permute-done((f32[2,32,200]{2,1,0:T(8,128)S(1)}, f32[2,32,200]{2,1,0:T(8,128)S(1)}, u32[]{:S(2)}, u32[]{:S(2)}) %collective-permute-start.4) | collective-permute-done | bytes 51232 | tf_op jit(solution)/shard_map/ppermute | solution.py:397
  76.7 0.5 all-to-all-done.1.parts_ref
  77.3 1.8 %collective-permute-start.6 = (f32[32,200]{1,0:T(8,128)S(1)}, f32[32,200]{1,0:T(8,128)S(1)}, u32[]{:S(2)}, u32[]{:S(2)}) collective-permute-start(f32[32,200]{1,0:T(8,128)S(1)} %slice_bitcast_fusion.4), channel_id=1, source_target_pairs={{0,8},{1,9},{2,10},{3,11},{4,12},{5,13},{6,14},{7,15},{8,0},{9,1},... | collective-permute-start | bytes 76808 | tf_op jit(solution)/shard_map/ppermute | solution.py:399
  79.1 1.0 %finish.1 = (f32[12,6,96]{2,1,0:T(8,128)}, f32[200,128]{1,0:T(8,128)}, f32[80,200]{1,0:T(8,128)}) custom-call(f32[64,56,128]{2,1,0:T(8,128)S(1)} %all-to-all-done.1.parts_ref, f32[80,96]{1,0:T(8,128)S(1)} %bitcast.27), custom_call_target="tpu_custom_call" | custom-call | flops 100000000 | bytes 2097152 | tf_op jit(solution)/shard_map/finish/pallas_call | solution.py:349
  80.1 1.1 %collective-permute-done.6 = f32[32,200]{1,0:T(8,128)S(1)} collective-permute-done((f32[32,200]{1,0:T(8,128)S(1)}, f32[32,200]{1,0:T(8,128)S(1)}, u32[]{:S(2)}, u32[]{:S(2)}) %collective-permute-start.6) | collective-permute-done | bytes 25632 | tf_op jit(solution)/shard_map/ppermute | solution.py:399
  81.2 0.6 bitcast_add_fusion
  (13 shorter events, 0.1 us)
Async XLA Ops:
  0.6 27.8 %copy-start.3 = (f32[96,128]{1,0:T(8,128)S(1)}, f32[96,128]{1,0:T(8,128)}, u32[]{:S(2)}) copy-start(f32[96,128]{1,0:T(8,128)} %lat_ref.1) | copy-start | bytes 147460
  17.3 22.1 %all-to-all-start = ((f32[128,1,4,128]{3,2,1,0:T(4,128)}), f32[128,1,4,128]{3,2,1,0:T(4,128)S(1)}, u32[]{:S(2)}, u32[]{:S(2)}) async-start(f32[128,1,4,128]{3,2,1,0:T(4,128)} %get-tuple-element.21), calls=%async_computation | async-start | bytes 524288 | tf_op jit(solution)/shard_map/all_to_all | solution.py:382
  39.4 3.4 %collective-permute-start = (f32[8,8,48,128]{3,2,1,0:T(8,128)S(1)}, f32[8,8,48,128]{3,2,1,0:T(8,128)S(1)}, u32[]{:S(2)}, u32[]{:S(2)}) collective-permute-start(f32[8,8,48,128]{3,2,1,0:T(8,128)S(1)} %get-tuple-element.26), channel_id=1, source_target_pairs={{0,1},{1,0},{2,3},{3,2},{4,5},{5,4},{6,7},{7,6},{8,9},{9,8},{10,11... | collective-permute-start | bytes 4718600 | tf_op jit(solution)/shard_map/ppermute | solution.py:385
  39.4 3.4 %collective-permute-start.1 = (f32[5,8,128]{2,1,0:T(8,128)S(1)}, f32[5,8,128]{2,1,0:T(8,128)S(1)}, u32[]{:S(2)}, u32[]{:S(2)}) collective-permute-start(f32[5,8,128]{2,1,0:T(8,128)S(1)} %get-tuple-element.29), channel_id=1, source_target_pairs={{0,1},{1,0},{2,3},{3,2},{4,5},{5,4},{6,7},{7,6},{8,9},{9,8},{10,11... | collective-permute-start | bytes 61448 | tf_op jit(solution)/shard_map/ppermute | solution.py:387
  44.2 5.0 %copy-start.1 = (f32[128,200]{0,1:T(8,128)S(1)}, f32[128,200]{0,1:T(8,128)}, u32[]{:S(2)}) copy-start(f32[128,200]{0,1:T(8,128)} %param.9) | copy-start | bytes 307204
  44.2 5.0 %copy-start.2 = (f32[80,200]{1,0:T(8,128)S(1)}, f32[80,200]{1,0:T(8,128)}, u32[]{:S(2)}) copy-start(f32[80,200]{1,0:T(8,128)} %time_ref.1) | copy-start | bytes 192004
  44.2 33.0 %all-to-all-start.1 = ((f32[64,56,128]{2,1,0:T(8,128)}), f32[64,56,128]{2,1,0:T(8,128)S(1)}, u32[]{:S(2)}, u32[]{:S(2)}) async-start(f32[64,56,128]{2,1,0:T(8,128)} %join_shares.1), calls=%async_computation.1 | async-start | bytes 3670016 | tf_op jit(solution)/shard_map/all_to_all | solution.py:390
  49.2 29.9 %copy-start = (f32[96,80]{0,1:T(8,128)S(1)}, f32[96,80]{0,1:T(8,128)}, u32[]{:S(2)}) copy-start(f32[96,80]{0,1:T(8,128)} %param.13) | copy-start | bytes 92164
  60.6 1.6 %collective-permute-start.2 = (f32[4,2,32,200]{3,2,1,0:T(8,128)S(1)}, f32[4,2,32,200]{3,2,1,0:T(8,128)S(1)}, u32[]{:S(2)}, u32[]{:S(2)}) collective-permute-start(f32[4,2,32,200]{3,2,1,0:T(8,128)S(1)} %get-tuple-element.32), channel_id=1, source_target_pairs={{0,1},{1,0},{2,3},{3,2},{4,5},{5,4},{6,7},{7,6},{8,9},{9,8},{10,11... | collective-permute-start | bytes 614408 | tf_op jit(solution)/shard_map/ppermute | solution.py:394
  62.3 10.1 %collective-permute-start.3 = (f32[2,32,200]{2,1,0:T(8,128)S(1)}, f32[2,32,200]{2,1,0:T(8,128)S(1)}, u32[]{:S(2)}, u32[]{:S(2)}) collective-permute-start(f32[2,32,200]{2,1,0:T(8,128)S(1)} %get-tuple-element.38), channel_id=1, source_target_pairs={{0,2},{1,3},{2,4},{3,5},{4,6},{5,7},{6,0},{7,1},{8,10},{9,11},{10,... | collective-permute-start | bytes 153608 | tf_op jit(solution)/shard_map/ppermute | solution.py:397
  63.9 10.7 %collective-permute-start.5 = (f32[2,32,200]{2,1,0:T(8,128)S(1)}, f32[2,32,200]{2,1,0:T(8,128)S(1)}, u32[]{:S(2)}, u32[]{:S(2)}) collective-permute-start(f32[2,32,200]{2,1,0:T(8,128)S(1)} %get-tuple-element.39), channel_id=1, source_target_pairs={{0,6},{1,7},{2,0},{3,1},{4,2},{5,3},{6,4},{7,5},{8,14},{9,15},{10,... | collective-permute-start | bytes 153608 | tf_op jit(solution)/shard_map/ppermute | solution.py:397
  65.6 11.1 %collective-permute-start.4 = (f32[2,32,200]{2,1,0:T(8,128)S(1)}, f32[2,32,200]{2,1,0:T(8,128)S(1)}, u32[]{:S(2)}, u32[]{:S(2)}) collective-permute-start(f32[2,32,200]{2,1,0:T(8,128)S(1)} %get-tuple-element.40), channel_id=1, source_target_pairs={{0,4},{1,5},{2,6},{3,7},{4,0},{5,1},{6,2},{7,3},{8,12},{9,13},{10,... | collective-permute-start | bytes 153608 | tf_op jit(solution)/shard_map/ppermute | solution.py:397
  77.3 3.9 %collective-permute-start.6 = (f32[32,200]{1,0:T(8,128)S(1)}, f32[32,200]{1,0:T(8,128)S(1)}, u32[]{:S(2)}, u32[]{:S(2)}) collective-permute-start(f32[32,200]{1,0:T(8,128)S(1)} %slice_bitcast_fusion.4), channel_id=1, source_target_pairs={{0,8},{1,9},{2,10},{3,11},{4,12},{5,13},{6,14},{7,15},{8,0},{9,1},... | collective-permute-start | bytes 76808 | tf_op jit(solution)/shard_map/ppermute | solution.py:399
